TPU v7x, 32 devices: a whole 2x2x4 slice. The times are simulated.
32 devices in a mesh: groups: 2 (over y), row: 4 (over z), col: 4 (over x, core).
Axes of the slice: x: 2, y: 2, z: 4, core: 2. Of those that a mesh axis runs over, the one named last changes fastest.
Arguments:
- node_embed: bfloat16 [384, 256], P(('groups', 'row')), parts along dimension 0, may hold values from -6 to 6
- rotation: float32 [3, 3, 384], P(None, None, 'groups'), parts along dimension 2, may hold values from -1 to 1, as said below
- translation: float32 [3, 384], P(None, 'groups'), parts along dimension 1, may hold values from -8 to 8
- pair_embed: bfloat16 [384, 192, 128], P(('groups', 'row'), 'col'), parts along dimension 0, may hold values from -1300 to 1300
- chain_index: int32 [384], P('groups'), parts along dimension 0, may hold values from 0 to 7, never falling along the last dimension, each value on 1 to 48 neighbouring positions
- residue_mask: int32 [384], P('groups'), parts along dimension 0, may hold values 0 or 1
- step_index: int32 [2], P('groups'), parts along dimension 0, may hold values from 0 to 999
- w_time: bfloat16 [256, 256], replicated, may hold values from -0.375 to 0.375
- w_query: bfloat16 [256, 2048], replicated, may hold values from -0.375 to 0.375
- w_query_points: bfloat16 [256, 192], replicated, may hold values from -0.375 to 0.375
- w_kv: bfloat16 [256, 4096], replicated, may hold values from -0.375 to 0.375
- w_kvp: bfloat16 [256, 480], replicated, may hold values from -0.375 to 0.375
- w_bias: bfloat16 [128, 8], replicated, may hold values from -0.5 to 0.5
- head_weights: float32 [8], replicated, may hold values from -1 to 1.5
- chain_bias: float32 [8], replicated, may hold values from -2 to 2
- w_out: bfloat16 [3456, 256], replicated, may hold values from -0.109375 to 0.109375
- w_mlp_in: bfloat16 [256, 256], replicated, may hold values from -0.375 to 0.375
- w_mlp_out: bfloat16 [256, 256], replicated, may hold values from -0.375 to 0.375
- w_edge_in: bfloat16 [256, 128], replicated, may hold values from -0.375 to 0.375
- w_trunk_in: bfloat16 [384, 384], replicated, may hold values from -0.3125 to 0.3125
- w_trunk_mid: bfloat16 [384, 384], replicated, may hold values from -0.3125 to 0.3125
- w_final: bfloat16 [384, 128], replicated, may hold values from -0.3125 to 0.3125
Outputs:
- node_out: bfloat16 [384, 256], P(('groups', 'row')), parts along dimension 0
- pair_out: bfloat16 [384, 192, 128], P(('groups', 'row'), 'col'), parts along dimension 0
There are 2 independent parts, one for each index of `groups`. A program takes and returns all parts, laid end to end along the dimension named above; an argument that names none is the same for every part. Nothing has to cross between parts.
Inputs may be any that keep to these rules, and one draw needn't show every extreme that they name: Each rotation[:, :, n] is a proper rotation matrix. `chain_index`: chain ids never fall along the residues; each chain has 1 to 48 residues, one exactly that many.
All inputs are finite; a program needn't handle non-finite values.
Results may differ from a plain program's by a relative error of at most 0.012.
Values may be sent and summed in bfloat16 or wider, within the bound.
No kernel may reach another device: no remote copies, remote signals or barrier semaphores. Data moves between devices by JAX's collectives and lax.ppermute only.
A program may use at most 64 MiB of HBM per device.

v0:
```python
import math

import jax
import jax.numpy as jnp
from jax import lax
from jax.sharding import PartitionSpec as P

CS = 256
CZ = 128
HEADS = 8
CH = 256
QP = 8
VP = 12
NH = 128
HID = 384


norm_epsilon = 1e-05
masked_score = 100000.0
highest = lax.Precision.HIGHEST


def layer_norm(values):
    average = jnp.mean(values, -1, keepdims=True)
    centred = values - average
    spread = jnp.mean(centred * centred, -1, keepdims=True)
    return centred * lax.rsqrt(spread + norm_epsilon)


def time_embedding(step_index, embed_width):
    half_width = embed_width // 2
    frequency = jnp.exp(-math.log(10000.0) * jnp.arange(half_width, dtype=jnp.float32) / half_width)
    angles = step_index.astype(jnp.float32)[0] * frequency
    return jnp.concatenate([jnp.sin(angles), jnp.cos(angles)])[None, :].astype(jnp.bfloat16)


def to_global(rotation, shift_vec, points):
    turned = jnp.einsum("abn,nbm->nam", rotation, points, precision=highest)
    return turned + jnp.transpose(shift_vec)[:, :, None]


def project_keys(embedded, rotation, shift_vec, w_kv, w_kvp):
    item_count = embedded.shape[0]
    key_values = jnp.dot(embedded, w_kv, preferred_element_type=jnp.float32).astype(jnp.bfloat16)
    points = jnp.dot(embedded, w_kvp, preferred_element_type=jnp.float32).reshape(item_count, 3, -1)
    return (key_values, to_global(rotation, shift_vec, points))


def node_finish(
    denominator,
    values_out,
    points_out,
    pair_sums,
    embedded,
    rotation,
    shift_vec,
    mask_rows,
    w_out,
    w_mlp_in,
    w_mlp_out,
    w_edge_in,
):
    item_count = embedded.shape[0]
    scale_back = denominator[:, :, None]
    attended = values_out.reshape(item_count, HEADS, CH) / scale_back
    points = points_out.reshape(item_count, 3, HEADS, VP) / denominator[:, None, :, None]
    relative = points - jnp.transpose(shift_vec)[:, :, None, None]
    framed = jnp.einsum("abi,iahv->ibhv", rotation, relative, precision=highest)
    length = jnp.sqrt(jnp.maximum(jnp.sum(framed * framed, 1), 1.0))
    paired = pair_sums.reshape(item_count, HEADS, CZ) / scale_back
    features = jnp.concatenate(
        [
            attended.reshape(item_count, -1),
            framed.reshape(item_count, -1),
            length.reshape(item_count, -1),
            paired.reshape(item_count, -1),
        ],
        -1,
    ).astype(jnp.bfloat16)
    update = jnp.dot(features, w_out, preferred_element_type=jnp.float32)
    normed = layer_norm(embedded.astype(jnp.float32) + update).astype(jnp.bfloat16)
    normed = lax.optimization_barrier(normed)
    middle = jax.nn.relu(jnp.dot(normed, w_mlp_in, preferred_element_type=jnp.float32)).astype(
        jnp.bfloat16
    )
    node_new = layer_norm(
        normed.astype(jnp.float32) + jnp.dot(middle, w_mlp_out, preferred_element_type=jnp.float32)
    )
    node_new = (node_new * mask_rows.astype(jnp.float32)[:, None]).astype(jnp.bfloat16)
    edge_side = jnp.dot(node_new, w_edge_in, preferred_element_type=jnp.float32).astype(
        jnp.bfloat16
    )
    return (node_new, edge_side)


def body(
    node_embed,
    rotation,
    translation,
    pair_embed,
    chain_index,
    residue_mask,
    step_index,
    w_time,
    w_query,
    w_query_points,
    w_kv,
    w_kvp,
    w_bias,
    head_weights,
    chain_bias,
    w_out,
    w_mlp_in,
    w_mlp_out,
    w_edge_in,
    w_trunk_in,
    w_trunk_mid,
    w_final,
):
    row_count = node_embed.shape[0]
    key_count = pair_embed.shape[1]
    row_start = lax.axis_index("row") * row_count
    key_start = lax.axis_index("col") * key_count
    embedded = (
        node_embed.astype(jnp.float32)
        + jnp.dot(time_embedding(step_index, CS), w_time, preferred_element_type=jnp.float32)
    ).astype(jnp.bfloat16)
    embedded = lax.optimization_barrier(embedded)
    rot_rows = lax.dynamic_slice_in_dim(rotation, row_start, row_count, 2)
    shift_rows = lax.dynamic_slice_in_dim(translation, row_start, row_count, 1)
    mask_rows = lax.dynamic_slice_in_dim(residue_mask, row_start, row_count, 0)
    mask_keys = lax.dynamic_slice_in_dim(residue_mask, key_start, key_count, 0)
    chain_rows = lax.dynamic_slice_in_dim(chain_index, row_start, row_count, 0)
    chain_keys = lax.dynamic_slice_in_dim(chain_index, key_start, key_count, 0)
    query_feat = (
        jnp.dot(embedded, w_query, preferred_element_type=jnp.float32)
        .astype(jnp.bfloat16)
        .reshape(row_count, HEADS, CH)
    )
    query_pts = to_global(
        rot_rows,
        shift_rows,
        jnp.dot(embedded, w_query_points, preferred_element_type=jnp.float32).reshape(
            row_count, 3, HEADS * QP
        ),
    ).reshape(row_count, 3, HEADS, QP)
    all_nodes = lax.all_gather(embedded, "row", axis=0, tiled=True)
    key_nodes = lax.dynamic_slice_in_dim(all_nodes, key_start, key_count, 0)
    rot_keys = lax.dynamic_slice_in_dim(rotation, key_start, key_count, 2)
    shift_keys = lax.dynamic_slice_in_dim(translation, key_start, key_count, 1)
    key_values, key_points = project_keys(key_nodes, rot_keys, shift_keys, w_kv, w_kvp)
    key_feat = key_values[:, : HEADS * CH].reshape(key_count, HEADS, CH)
    value_feat = key_values[:, HEADS * CH :].reshape(key_count, HEADS, CH)
    key_points = key_points.reshape(key_count, 3, HEADS, QP + VP)
    key_pts = key_points[..., :QP]
    value_pts = key_points[..., QP:]
    scaled = math.sqrt(1.0 / 3.0)
    point_weight = math.sqrt(2.0 / (9.0 * QP))
    point_gain = jax.nn.softplus(head_weights)
    feature_dots = jnp.einsum(
        "ihc,jhc->hij", query_feat, key_feat, preferred_element_type=jnp.float32
    ) / math.sqrt(CH)
    pair_bias = jnp.einsum("ijc,ch->hij", pair_embed, w_bias, preferred_element_type=jnp.float32)
    same_chain = (chain_rows[:, None] == chain_keys[None, :]).astype(jnp.float32)
    query_square = jnp.einsum("iahp,iahp->hi", query_pts, query_pts, precision=highest)
    key_square = jnp.einsum("jahp,jahp->hj", key_pts, key_pts, precision=highest)
    cross_term = jnp.einsum("iahp,jahp->hij", query_pts, key_pts, precision=highest)
    distance = query_square[:, :, None] + key_square[:, None, :] - 2.0 * cross_term
    mask_term = (mask_keys.astype(jnp.float32) - 1.0) * masked_score
    scores = (
        scaled * (feature_dots + pair_bias + chain_bias[:, None, None] * same_chain[None])
        - scaled * point_weight * 0.5 * point_gain[:, None, None] * distance
        + mask_term[None, None, :]
    )
    row_peak = lax.pmax(jnp.max(scores, -1), "col")
    weights = jnp.exp(scores - row_peak[:, :, None])
    denominator = jnp.transpose(jnp.sum(weights, -1))
    rounded = weights.astype(jnp.bfloat16)
    values_out = jnp.einsum(
        "hij,jhc->ihc", rounded, value_feat, preferred_element_type=jnp.float32
    ).reshape(row_count, -1)
    points_out = jnp.einsum("hij,jahv->iahv", weights, value_pts, precision=highest).reshape(
        row_count, -1
    )
    pair_sums = jnp.einsum(
        "hij,ijc->ihc", rounded, pair_embed, preferred_element_type=jnp.float32
    ).reshape(row_count, -1)
    summed = lax.psum((denominator, values_out, points_out, pair_sums), "col")
    node_out, edge_side = node_finish(
        summed[0],
        summed[1],
        summed[2],
        summed[3],
        embedded,
        rot_rows,
        shift_rows,
        mask_rows,
        w_out,
        w_mlp_in,
        w_mlp_out,
        w_edge_in,
    )
    side_all = lax.all_gather(edge_side, "row", axis=0, tiled=True)
    side_rows = lax.dynamic_slice_in_dim(side_all, row_start, row_count, 0)
    side_keys = lax.dynamic_slice_in_dim(side_all, key_start, key_count, 0)
    pre_rows = jnp.dot(side_rows, w_trunk_in[CZ : CZ + NH], preferred_element_type=jnp.float32)
    pre_keys = jnp.dot(side_keys, w_trunk_in[CZ + NH :], preferred_element_type=jnp.float32)
    mask_key_f = mask_keys.astype(jnp.float32)
    block_rows = math.gcd(row_count, 8)
    block_count = row_count // block_rows

    def edge_block(inputs):
        pair_block, pre_block, side_block, keep_block = inputs
        lifted = (
            jnp.einsum(
                "ijc,cd->ijd", pair_block, w_trunk_in[:CZ], preferred_element_type=jnp.float32
            )
            + pre_block[:, None, :]
            + pre_keys[None, :, :]
        )
        hidden_one = jax.nn.relu(lifted).astype(jnp.bfloat16)
        hidden_two = jax.nn.relu(
            jnp.einsum("ijd,de->ije", hidden_one, w_trunk_mid, preferred_element_type=jnp.float32)
        )
        stacked = jnp.concatenate(
            [
                pair_block,
                jnp.broadcast_to(side_block[:, None, :], (block_rows, key_count, NH)),
                jnp.broadcast_to(side_keys[None, :, :], (block_rows, key_count, NH)),
            ],
            -1,
        )
        joined = (hidden_two + stacked.astype(jnp.float32)).astype(jnp.bfloat16)
        edge_out = jnp.einsum("ijd,dc->ijc", joined, w_final, preferred_element_type=jnp.float32)
        pair_keep = keep_block.astype(jnp.float32)[:, None] * mask_key_f[None, :]
        return (layer_norm(edge_out) * pair_keep[:, :, None]).astype(jnp.bfloat16)

    pair_out = lax.map(
        edge_block,
        (
            pair_embed.reshape(block_count, block_rows, key_count, CZ),
            pre_rows.reshape(block_count, block_rows, HID),
            side_rows.reshape(block_count, block_rows, NH),
            mask_rows.reshape(block_count, block_rows),
        ),
    )
    return (node_out, pair_out.reshape(row_count, key_count, CZ))


def solution(mesh):
    return jax.shard_map(
        body,
        mesh=mesh,
        in_specs=(
            P(("groups", "row"), None),
            P(None, None, "groups"),
            P(None, "groups"),
            P(("groups", "row"), "col", None),
            P("groups"),
            P("groups"),
            P("groups"),
            P(),
            P(),
            P(),
            P(),
            P(),
            P(),
            P(),
            P(),
            P(),
            P(),
            P(),
            P(),
            P(),
            P(),
            P(),
        ),
        out_specs=(P(("groups", "row"), None), P(("groups", "row"), "col", None)),
        check_vma=False,
    )
```

profile of v0, /device:TPU:0, one launch (start us, length us, event | category | flops | bytes accessed | tf_op | source)
XLA Modules:
  0.0 135.2 jit_solution(5228488410972986476)
XLA Ops:
  8.0 1.2 fusion.59
  9.3 1.3 add_multiply_fusion
  10.6 1.4 %fusion.61 = (f32[48]{0:T(128)}, s32[48]{0:T(128)}, s32[48]{0:T(128)}, s32[48]{0:T(128)}) fusion(s32[192]{0:T(256)} %param.29, s32[]{:T(128)S(6)} %select_n.8, s32[192]{0:T(256)} %param.28, s32[]{:T(128)S(6)} %select_n.7), kind=kLoop, calls=%fused_computation.115 | loop fusion | flops 48 | bytes 1352 | tf_op jit(solution)/shard_map/convert_element_type | solution.py:89
  12.1 0.8 dynamic-slice_bitcast_fusion.4
  12.9 0.9 constant_dynamic-slice_fusion.2
  13.8 1.0 fusion.68
  14.9 0.8 add_convert_fusion
  15.7 15.0 %all_gather.6 = bf16[192,256]{1,0:T(8,128)(2,1)S(1)} all-gather(bf16[48,256]{1,0:T(8,128)(2,1)S(1)} %add_convert_fusion), channel_id=1, replica_groups=mesh['groups'=2,'row'=4,'col'=4] {'row'}, dimensions={0}, use_global_device_ids=true | all-gather | bytes 122880 | tf_op jit(solution)/shard_map/all_gather | solution.py:147
  30.7 1.1 fusion.69
  32.8 0.6 fusion.42
  33.4 1.1 fusion.50
  35.4 1.5 %convolution_convert_fusion.1 = bf16[48,2048]{1,0:T(8,128)(2,1)S(1)} fusion(bf16[48,256]{1,0:T(8,128)(2,1)S(1)} %add_convert_fusion, bf16[256,2048]{1,0:T(8,128)(2,1)} %param.32), kind=kOutput, calls=%fused_computation.30 | convolution fusion | flops 50429952 | bytes 1269760 | tf_op jit(solution)/shard_map/dot_general | solution.py:136
  37.0 1.3 fusion.54
  38.3 0.8 copy.83
  39.1 1.3 convolution_convert_fusion
  40.4 0.7 fusion.63
  41.2 1.1 fusion.27
  42.6 5.7 %pmax.7 = f32[8,48]{1,0:T(8,128)S(1)} all-reduce(f32[8,48]{1,0:T(8,128)S(1)} %get-tuple-element.115), channel_id=1, replica_groups=mesh['groups'=2,'row'=4,'col'=4] {'col'}, use_global_device_ids=true, to_apply=%region_1.2 | all-reduce | flops 384 | bytes 3072 | tf_op jit(solution)/shard_map/pmax | solution.py:175
  48.5 1.2 convolution_bitcast_fusion
  49.6 0.8 copy.131
  50.7 0.7 copy.155
  51.8 15.2 %all-reduce = (f32[48,8]{0,1:T(8,128)S(1)}, f32[48,3,8,12]{0,3,1,2:T(8,128)S(1)}) all-reduce(f32[48,8]{0,1:T(8,128)S(1)} %bitcast.172, f32[48,3,8,12]{0,3,1,2:T(8,128)S(1)} %convolution_bitcast_fusion.1), channel_id=1, replica_groups=mesh['groups'=2,'row'=4,'col'=4] {'col'}, use_global_device_ids=true, to_apply=%region_4.5 | all-reduce | flops 14208 | bytes 113664 | tf_op jit(solution)/shard_map/psum | solution.py:188
  67.0 0.7 divide_subtract_fusion
  67.7 1.8 %copy.97 = f32[48,3,8,12]{3,1,2,0:T(4,128)S(1)} copy(f32[48,3,8,12]{0,3,1,2:T(8,128)} %divide_subtract_fusion) | data formatting | bytes 110592 | tf_op jit(solution)/shard_map/sub | solution.py:67
  69.5 4.5 %multiply_reduce_fusion.1 = (f32[48,8,12]{2,1,0:T(8,128)}, bf16[48,3,8,12]{3,1,2,0:T(4,128)(2,1)}) fusion(f32[48,3,8,12]{3,1,2,0:T(4,128)S(1)} %copy.97, f32[3,3,48]{1,0,2:T(4,128)} %copy-done.4), kind=kOutput, calls=%fused_computation.51 | convolution fusion | flops 534528 | bytes 103104 | tf_op jit(solution)/shard_map/abi,iahv->ibhv/dot_general | solution.py:68
  74.4 1.1 copy.99
  75.6 1.5 %copy.98 = bf16[48,3,8,12]{0,3,2,1:T(8,128)(2,1)S(1)} copy(bf16[48,3,8,12]{3,1,2,0:T(4,128)(2,1)} %get-tuple-element.102) | data formatting | bytes 55296 | tf_op jit(solution)/shard_map/convert.5
  77.2 10.0 %all-reduce.4.cloned.1.call-done = (f32[48,2048]{1,0:T(8,128)}, f32[48,1024]{1,0:T(8,128)}) async-done(((f32[48,2048]{1,0:T(8,128)}, f32[48,1024]{1,0:T(8,128)}), (f32[48,2048]{1,0:T(8,128)}, f32[48,1024]{1,0:T(8,128)})) %all-reduce.4.cloned.1.call-update) | async-done | bytes 589840 | tf_op jit(solution)/shard_map/psum | solution.py:188
  87.3 1.0 fusion.29
  88.3 1.1 divide_convert_fusion
  89.5 2.0 %fusion.66 = (f32[48]{0:T(128)S(1)}, f32[48,256]{1,0:T(8,128)S(1)}) fusion(bf16[48,3456]{1,0:T(8,128)(2,1)S(1)} %concatenate.14, bf16[3456,256]{1,0:T(8,128)(2,1)} %param.39, bf16[48,256]{1,0:T(8,128)(2,1)S(1)} %add_convert_fusion), kind=kOutput, calls=%fused_computation.120 | convolution fusion | flops 84971472 | bytes 2175168 | tf_op jit(solution)/shard_map/dot_general | solution.py:80
  92.5 1.0 convolution_convert_fusion.2
  93.5 13.2 %all_gather.7 = bf16[192,128]{1,0:T(8,128)(2,1)S(1)} all-gather(bf16[48,128]{1,0:T(8,128)(2,1)S(1)} %convolution_convert_fusion.2), channel_id=1, replica_groups=mesh['groups'=2,'row'=4,'col'=4] {'row'}, dimensions={0}, use_global_device_ids=true | all-gather | bytes 61440 | tf_op jit(solution)/shard_map/all_gather | solution.py:203
  106.7 1.0 convolution_bitcast_fusion.3
  107.7 1.7 %fusion.44 = f32[48,384]{1,0:T(8,128)} fusion(bf16[48,128]{1,0:T(8,128)(2,1)S(1)} %get-tuple-element.215, bf16[384,384]{1,0:T(8,128)(2,1)} %param.43), kind=kOutput, calls=%fused_computation.74 | convolution fusion | flops 4718592 | bytes 184320 | tf_op jit(solution)/shard_map/dot_general | solution.py:207
  109.4 18.9 %while.10 = (s32[]{:T(128)}, bf16[6,8,48,128]{3,2,1,0:T(8,128)(2,1)}, bf16[6,8,48,128]{3,2,1,0:T(8,128)(2,1)S(1)}, bf16[384,384]{1,0:T(8,128)(2,1)}, f32[6,8,384...) while((s32[]{:T(128)}, ...), condition=%wide.region_15.16_spmd, body=%wide.region_12.15_spmd.sunk | while | flops 191054592 | bytes 2702265 | solution.py:238
  109.5 1.5 %fusion.111 = bf16[8,48,384]{2,1,0:T(8,128)(2,1)S(1)} fusion(bf16[8,48,128]{2,1,0:T(8,128)(2,1)S(1)} %dynamic-slice_bitcast_fusion.9, bf16[8,48,128]{2,1,0:T(8,128)(2,1)S(1)} %broadcast_in_dim.14, bf16[8,48,128]{2,1,0:T(8,128)(2,1)S(1)} %broadcast_in_dim.15, bf16[384,384]{1,0:T(8,128)(2,1)} %get-tuple-element.239, f32[48,384]{1,0:T(8,128)} %get-tuple-element.238, ...), kind=kOutput, calls=%fused_computation.6.clone.1 | convolution fusion | flops 152911872 | bytes 1167360 | tf_op jit(solution)/shard_map/while/body/eval_jaxpr/ijd,de->ije/dot_general | solution.py:223
  111.7 0.9 fusion.114
  112.7 1.5 %fusion.111 = bf16[8,48,384]{2,1,0:T(8,128)(2,1)S(1)} fusion(bf16[8,48,128]{2,1,0:T(8,128)(2,1)S(1)} %dynamic-slice_bitcast_fusion.9, bf16[8,48,128]{2,1,0:T(8,128)(2,1)S(1)} %broadcast_in_dim.14, bf16[8,48,128]{2,1,0:T(8,128)(2,1)S(1)} %broadcast_in_dim.15, bf16[384,384]{1,0:T(8,128)(2,1)} %get-tuple-element.239, f32[48,384]{1,0:T(8,128)} %get-tuple-element.238, ...), kind=kOutput, calls=%fused_computation.6.clone.1 | convolution fusion | flops 152911872 | bytes 1167360 | tf_op jit(solution)/shard_map/while/body/eval_jaxpr/ijd,de->ije/dot_general | solution.py:223
  114.9 0.9 fusion.114
  115.8 1.5 %fusion.111 = bf16[8,48,384]{2,1,0:T(8,128)(2,1)S(1)} fusion(bf16[8,48,128]{2,1,0:T(8,128)(2,1)S(1)} %dynamic-slice_bitcast_fusion.9, bf16[8,48,128]{2,1,0:T(8,128)(2,1)S(1)} %broadcast_in_dim.14, bf16[8,48,128]{2,1,0:T(8,128)(2,1)S(1)} %broadcast_in_dim.15, bf16[384,384]{1,0:T(8,128)(2,1)} %get-tuple-element.239, f32[48,384]{1,0:T(8,128)} %get-tuple-element.238, ...), kind=kOutput, calls=%fused_computation.6.clone.1 | convolution fusion | flops 152911872 | bytes 1167360 | tf_op jit(solution)/shard_map/while/body/eval_jaxpr/ijd,de->ije/dot_general | solution.py:223
  118.0 0.9 fusion.114
  119.0 1.5 %fusion.111 = bf16[8,48,384]{2,1,0:T(8,128)(2,1)S(1)} fusion(bf16[8,48,128]{2,1,0:T(8,128)(2,1)S(1)} %dynamic-slice_bitcast_fusion.9, bf16[8,48,128]{2,1,0:T(8,128)(2,1)S(1)} %broadcast_in_dim.14, bf16[8,48,128]{2,1,0:T(8,128)(2,1)S(1)} %broadcast_in_dim.15, bf16[384,384]{1,0:T(8,128)(2,1)} %get-tuple-element.239, f32[48,384]{1,0:T(8,128)} %get-tuple-element.238, ...), kind=kOutput, calls=%fused_computation.6.clone.1 | convolution fusion | flops 152911872 | bytes 1167360 | tf_op jit(solution)/shard_map/while/body/eval_jaxpr/ijd,de->ije/dot_general | solution.py:223
  121.2 0.9 fusion.114
  122.1 1.5 %fusion.111 = bf16[8,48,384]{2,1,0:T(8,128)(2,1)S(1)} fusion(bf16[8,48,128]{2,1,0:T(8,128)(2,1)S(1)} %dynamic-slice_bitcast_fusion.9, bf16[8,48,128]{2,1,0:T(8,128)(2,1)S(1)} %broadcast_in_dim.14, bf16[8,48,128]{2,1,0:T(8,128)(2,1)S(1)} %broadcast_in_dim.15, bf16[384,384]{1,0:T(8,128)(2,1)} %get-tuple-element.239, f32[48,384]{1,0:T(8,128)} %get-tuple-element.238, ...), kind=kOutput, calls=%fused_computation.6.clone.1 | convolution fusion | flops 152911872 | bytes 1167360 | tf_op jit(solution)/shard_map/while/body/eval_jaxpr/ijd,de->ije/dot_general | solution.py:223
  124.3 0.9 fusion.114
  125.3 1.5 %fusion.111 = bf16[8,48,384]{2,1,0:T(8,128)(2,1)S(1)} fusion(bf16[8,48,128]{2,1,0:T(8,128)(2,1)S(1)} %dynamic-slice_bitcast_fusion.9, bf16[8,48,128]{2,1,0:T(8,128)(2,1)S(1)} %broadcast_in_dim.14, bf16[8,48,128]{2,1,0:T(8,128)(2,1)S(1)} %broadcast_in_dim.15, bf16[384,384]{1,0:T(8,128)(2,1)} %get-tuple-element.239, f32[48,384]{1,0:T(8,128)} %get-tuple-element.238, ...), kind=kOutput, calls=%fused_computation.6.clone.1 | convolution fusion | flops 152911872 | bytes 1167360 | tf_op jit(solution)/shard_map/while/body/eval_jaxpr/ijd,de->ije/dot_general | solution.py:223
  127.5 0.9 fusion.114
  (138 shorter events, 9.1 us)
Async XLA Ops:
  7.2 32.0 %copy-start = (bf16[256,4096]{1,0:T(8,128)(2,1)S(1)}, bf16[256,4096]{1,0:T(8,128)(2,1)}, u32[]{:S(2)}) copy-start(bf16[256,4096]{1,0:T(8,128)(2,1)} %param.34) | copy-start | bytes 6291460
  7.2 80.0 %all-reduce.4.cloned.1.call-start = ((), (), s32[]{:S(2)}) async-start(), calls=%async_computation | async-start | bytes 1179648 | tf_op jit(solution)/shard_map/psum | solution.py:188
  30.7 2.7 %copy-start.5 = (bf16[192,256]{1,0:T(8,128)(2,1)}, bf16[192,256]{1,0:T(8,128)(2,1)S(1)}, u32[]{:S(2)}) copy-start(bf16[192,256]{1,0:T(8,128)(2,1)S(1)} %all_gather.6) | copy-start | bytes 294916
  32.2 2.3 %copy-start.4 = (f32[3,3,48]{1,0,2:T(4,128)}, f32[3,3,48]{1,0,2:T(4,128)S(1)}, u32[]{:S(2)}) copy-start(f32[3,3,48]{1,0,2:T(4,128)S(1)} %copy.125) | copy-start | bytes 5188
  32.2 4.7 %copy-start.1 = (bf16[48,48,128]{2,1,0:T(8,128)(2,1)S(1)}, bf16[48,48,128]{2,1,0:T(8,128)(2,1)}, u32[]{:S(2)}) copy-start(bf16[48,48,128]{2,1,0:T(8,128)(2,1)} %param.27) | copy-start | bytes 1769476
  36.9 4.2 %copy-start.13 = (s32[48]{0:T(128)S(1)}, s32[48]{0:T(128)}, u32[]{:S(2)}) copy-start(s32[48]{0:T(128)} %get-tuple-element.122) | copy-start | bytes 580
  36.9 4.2 %copy-start.14 = (s32[48]{0:T(128)S(1)}, s32[48]{0:T(128)}, u32[]{:S(2)}) copy-start(s32[48]{0:T(128)} %get-tuple-element.123) | copy-start | bytes 580
  36.9 4.2 %copy-start.9 = (f32[8,48]{1,0:T(8,128)S(1)}, f32[8,48]{1,0:T(8,128)}, u32[]{:S(2)}) copy-start(f32[8,48]{1,0:T(8,128)} %fusion.42) | copy-start | bytes 4612
  38.3 4.0 %copy-start.11 = (f32[48]{0:T(128)S(1)}, f32[48]{0:T(128)}, u32[]{:S(2)}) copy-start(f32[48]{0:T(128)} %get-tuple-element.95) | copy-start | bytes 580
  38.3 4.0 %copy-start.15 = (f32[8]{0:T(128)S(1)}, f32[8]{0:T(128)}, u32[]{:S(2)}) copy-start(f32[8]{0:T(128)} %param.38) | copy-start | bytes 100
  39.1 3.2 %copy-start.3 = (f32[8,48,48]{1,2,0:T(8,128)S(1)}, f32[8,48,48]{1,2,0:T(8,128)}, u32[]{:S(2)}) copy-start(f32[8,48,48]{1,2,0:T(8,128)} %copy.83) | copy-start | bytes 221188
  51.4 22.6 %copy-start.12 = (s32[48]{0:T(128)S(1)}, s32[48]{0:T(128)}, u32[]{:S(2)}) copy-start(s32[48]{0:T(128)} %get-tuple-element.94) | copy-start | bytes 580
  88.3 4.2 %copy-start.10 = (f32[48]{0:T(128)S(1)}, f32[48]{0:T(128)}, u32[]{:S(2)}) copy-start(f32[48]{0:T(128)} %get-tuple-element.93) | copy-start | bytes 580
  89.3 20.1 %copy-start.2 = (bf16[384,128]{1,0:T(8,128)(2,1)S(1)}, bf16[384,128]{1,0:T(8,128)(2,1)}, u32[]{:S(2)}) copy-start(bf16[384,128]{1,0:T(8,128)(2,1)} %param.45) | copy-start | bytes 294916
  89.5 2.4 %copy-start.6 = (bf16[256,256]{1,0:T(8,128)(2,1)S(1)}, bf16[256,256]{1,0:T(8,128)(2,1)}, u32[]{:S(2)}) copy-start(bf16[256,256]{1,0:T(8,128)(2,1)} %param.41) | copy-start | bytes 393220
  89.5 2.4 %copy-start.7 = (bf16[256,256]{1,0:T(8,128)(2,1)S(1)}, bf16[256,256]{1,0:T(8,128)(2,1)}, u32[]{:S(2)}) copy-start(bf16[256,256]{1,0:T(8,128)(2,1)} %param.40) | copy-start | bytes 393220
  92.5 16.9 %copy-start.8 = (bf16[48,256]{1,0:T(8,128)(2,1)}, bf16[48,256]{1,0:T(8,128)(2,1)S(1)}, u32[]{:S(2)}) copy-start(bf16[48,256]{1,0:T(8,128)(2,1)S(1)} %multiply_convert_fusion.1) | copy-start | bytes 73732
Sparse Core Ops, SparseCore 0:
  51.6 35.5 all-reduce.3
where the time goes:
time: 136 us; the launch traced here: 135 us
  blocking collectives  49.1 us (36%)
  matrix products  33.2 us (24%)
  other arithmetic  15.9 us (12%)
  between operations  15.3 us (11%)
  local copies, waits for them, and re-layouts  11.4 us (8%)
  waiting for transfers between devices  10 us (7%)
    psum x1, blocking collectives, body(): summed = lax.psum((denominator, values_out, points_out, pair_sums), 'col')  15.2 us
    all_gather x1, blocking collectives, body(): all_nodes = lax.all_gather(embedded, 'row', axis=0, tiled=True)  15 us
    all_gather x1, blocking collectives, body(): side_all = lax.all_gather(edge_side, 'row', axis=0, tiled=True)  13.2 us
    psum x1, waiting for transfers between devices, body(): summed = lax.psum((denominator, values_out, points_out, pair_sums), 'col')  9.98 us
    dot_general x6, matrix products, edge_block(): jnp.einsum('ijd,de->ije', hidden_one, w_trunk_mid, preferred_element_type...  9.25 us
    pmax x1, blocking collectives, body(): row_peak = lax.pmax(jnp.max(scores, -1), 'col')  5.67 us
    dynamic_update_slice x6, other arithmetic, body(): lax.map(edge_block, (pair_embed.reshape(block_count, block_rows, key_coun...  5.22 us
    dot_general x1, matrix products, node_finish(): framed = jnp.einsum('abi,iahv->ibhv', rotation, relative, precision=highest)  4.51 us
  transfers between devices with their start and end apart: 1, of which 1 were waited for; matrix products, arithmetic and copies ran while one was open for 8% of the time, Pallas kernels for 0%

commit v1 on v0

--- a/solution.py
+++ b/solution.py
@@ -1,8 +1,11 @@
+import functools
 import math
 
 import jax
 import jax.numpy as jnp
 from jax import lax
+from jax.experimental import pallas as pl
+from jax.experimental.pallas import tpu as pltpu
 from jax.sharding import PartitionSpec as P
 
 CS = 256
@@ -247,9 +250,353 @@
     return (node_out, pair_out.reshape(row_count, key_count, CZ))
 
 
+PAD = 64
+GAIN = math.sqrt(1.0 / 3.0)
+POINT = math.sqrt(2.0 / (9.0 * QP))
+f32 = jnp.float32
+bf16 = jnp.bfloat16
+
+
+def dot(a, b, dims=((1,), (0,)), precision=None):
+    return lax.dot_general(a, b, (dims, ((), ())), precision=precision, preferred_element_type=f32)
+
+
+NT = ((1,), (1,))
+TN = ((0,), (0,))
+
+
+def params(mib):
+    return pltpu.CompilerParams(vmem_limit_bytes=mib * 1024 * 1024)
+
+
+def vmem(count):
+    return [pl.BlockSpec(memory_space=pltpu.VMEM)] * count
+
+
+def bias_kernel(pair_ref, w_ref, out_ref):
+    w_t = jnp.transpose(w_ref[...].astype(f32)).astype(bf16)
+    half = pair_ref.shape[0] // 2
+    keys = pair_ref.shape[1]
+    gap = jnp.zeros((PAD - keys, CZ), bf16)
+    for i in range(half):
+        both = jnp.concatenate([pair_ref[i], gap, pair_ref[i + half], gap], 0)
+        out_ref[pl.ds(i, HEADS, stride=half), :] = dot(w_t, both, NT) * GAIN
+
+
+def one_hot(shape, source_dim, offset_of):
+    src = lax.broadcasted_iota(jnp.int32, shape, source_dim)
+    dst = lax.broadcasted_iota(jnp.int32, shape, 1 - source_dim)
+    return (src == offset_of(dst)).astype(f32)
+
+
+def prepare_kernel(
+    step_ref, hw_ref, node_ref, feats_ref, w_time_ref, w_query_ref, w_qp_ref, w_kv_ref, w_kvp_ref, w_out_ref,
+    time_ref, own_ref, qk_ref, qpts_ref, w_mix_ref, w_pts_ref, kfeat_ref, rows_ref, keys_ref, w_head_ref, sem,
+):
+    copy = pltpu.make_async_copy(w_out_ref.at[pl.ds(0, HEADS * CH)], w_head_ref, sem)
+    copy.start()
+    rows = node_ref.shape[0]
+    total = feats_ref.shape[1]
+    half = CS // 2
+    row = lax.axis_index("row")
+    col = lax.axis_index("col")
+    lane = lax.broadcasted_iota(jnp.int32, (8, half), 1).astype(f32)
+    frequency = jnp.exp(-math.log(10000.0) * lane / half)
+    angles = step_ref[0].astype(f32) * frequency
+    temb = jnp.concatenate([jnp.sin(angles), jnp.cos(angles)], 1).astype(bf16)
+    time = dot(temb, w_time_ref[...])
+    time_ref[...] = time
+    own = (node_ref[...].astype(f32) + time[0:1]).astype(bf16)
+    own_ref[...] = own
+    feats = feats_ref[...]
+
+    def key_of(dst):
+        part = dst // PAD
+        inside = dst - part * PAD
+        return jnp.where(inside < rows, (part ^ col) * rows + inside, -1)
+
+    kfeat_ref[...] = dot(feats, one_hot((total, 4 * PAD), 0, key_of), precision=highest)
+    own_cols = dot(one_hot((rows, total), 1, lambda d: d + row * rows), feats, NT, precision=highest)
+    rows_ref[...] = own_cols
+    keys_ref[...] = dot(one_hot((rows, total), 1, lambda d: d + col * rows), feats, NT, precision=highest)
+    copy.wait()
+    query = dot(own, w_query_ref[...]).astype(bf16)
+    for h in range(HEADS):
+        taken = dot(query[:, h * CH : (h + 1) * CH], w_kv_ref[:, h * CH : (h + 1) * CH], NT)
+        qk_ref[h * rows : (h + 1) * rows, :] = (taken * (GAIN / math.sqrt(CH))).astype(bf16)
+        w_mix_ref[h * CH : (h + 1) * CH, :] = dot(
+            w_kv_ref[:, (HEADS + h) * CH : (HEADS + h + 1) * CH], w_head_ref[h * CH : (h + 1) * CH, :]
+        ).astype(bf16)
+    wide = HEADS * QP
+    local = dot(own, w_qp_ref[...])
+    parts = [local[:, b * wide : (b + 1) * wide] for b in range(3)]
+    points = []
+    for a in range(3):
+        turned = own_cols[:, 9 + a : 10 + a]
+        for b in range(3):
+            turned = turned + own_cols[:, 3 * a + b : 3 * a + b + 1] * parts[b]
+        points.append(turned)
+    points = jnp.concatenate(points + [jnp.zeros((rows, wide), f32)], 1)
+    lanes = lax.broadcasted_iota(jnp.int32, (1, 4 * wide), 1)
+    head_lane = lax.broadcasted_iota(jnp.int32, (1, 128), 1)
+    hw = jnp.zeros((1, 128), f32)
+    for h in range(HEADS):
+        hw = jnp.where(head_lane == h, hw_ref[h], hw)
+    gains = GAIN * POINT * 0.5 * (jnp.maximum(hw, 0.0) + jnp.log1p(jnp.exp(-jnp.abs(hw))))
+    rows_ref[...] = own_cols
+    for h in range(HEADS):
+        gain = gains[:, h : h + 1]
+        mine = jnp.where((lanes % wide) // QP == h, points, 0.0)
+        square = jnp.sum(mine * mine, 1, keepdims=True)
+        qpts_ref[h * rows : (h + 1) * rows, :] = jnp.where(lanes == 3 * wide, -square, 2.0 * mine) * gain
+    width = w_kvp_ref.shape[1]
+    group = HEADS * (QP + VP)
+    dst = lax.broadcasted_iota(jnp.int32, (width, width), 0)
+    src = lax.broadcasted_iota(jnp.int32, (width, width), 1)
+    comp = dst // group
+    inside = dst - comp * group
+    value = inside - HEADS * QP
+    from_key = (inside // QP) * (QP + VP) + inside % QP
+    from_value = (value // VP) * (QP + VP) + QP + value % VP
+    wanted = comp * group + jnp.where(inside < HEADS * QP, from_key, from_value)
+    order = (src == wanted).astype(f32).astype(bf16)
+    w_pts_ref[...] = dot(order, w_kvp_ref[...], NT).astype(bf16)
+
+
+def attention_kernel(
+    hw_ref, cb_ref, own_ref, n1_ref, n2_ref, n3_ref, time_ref, qk_ref, qpts_ref, w_mix_ref, w_pts_ref, kfeat_ref,
+    rows_ref, b0_ref, b1_ref, b2_ref, b3_ref, pair_ref, w_out_ref,
+    out_ref, x_ref, prob_ref, near_ref, opair_ref, w_tail_ref, sem,
+):
+    rows = own_ref.shape[0]
+    half = rows // 2
+    row = lax.axis_index("row")
+    col = lax.axis_index("col")
+    tail = HEADS * CH
+    copy = pltpu.make_async_copy(w_out_ref.at[pl.ds(tail, w_out_ref.shape[0] - tail)], w_tail_ref, sem)
+    copy.start()
+    time = time_ref[0:1]
+    x_ref[...] = jnp.zeros(x_ref.shape, bf16)
+    x_ref[pl.ds(pl.multiple_of((col ^ row) * PAD, PAD), rows), :] = own_ref[...]
+    for k, ref in ((1, n1_ref), (2, n2_ref), (3, n3_ref)):
+        place = col ^ ((row + 4 - k) % 4)
+        x_ref[pl.ds(pl.multiple_of(place * PAD, PAD), rows), :] = (ref[...].astype(f32) + time).astype(bf16)
+    x = x_ref[...]
+    keys = x.shape[0]
+    kfeat = kfeat_ref[...]
+    group = HEADS * (QP + VP)
+    wide = HEADS * QP
+    local = dot(w_pts_ref[...], x, NT)
+    points = []
+    for a in range(3):
+        turned = kfeat[9 + a : 10 + a]
+        for b in range(3):
+            turned = turned + kfeat[3 * a + b : 3 * a + b + 1] * local[b * group : (b + 1) * group]
+        points.append(turned)
+    key_points = [p[:wide] for p in points]
+    cross = dot(qpts_ref[...], jnp.concatenate(key_points + [jnp.ones((wide, keys), f32)], 0), precision=highest)
+    key_square = key_points[0] * key_points[0] + key_points[1] * key_points[1] + key_points[2] * key_points[2]
+    feature = dot(qk_ref[...], x, NT)
+    lane = lax.broadcasted_iota(jnp.int32, (1, 128), 1)
+    low = lane < PAD
+    bias_low, bias_high = [], []
+    for left, right in ((b0_ref, b1_ref), (b2_ref, b3_ref)):
+        left, right = left[...], right[...]
+        bias_low.append(jnp.where(low, left, pltpu.roll(right, PAD, 1)))
+        bias_high.append(jnp.where(low, pltpu.roll(left, PAD, 1), right))
+    bias_low = jnp.concatenate(bias_low, 1)
+    bias_high = jnp.concatenate(bias_high, 1)
+    key_lane = lax.broadcasted_iota(jnp.int32, (1, keys), 1)
+    blocked = jnp.where(key_lane % PAD < rows, (kfeat[12:13] - 1.0) * masked_score, -1e30)
+    own_cols = rows_ref[...]
+    same = (own_cols[:, 13:14] == kfeat[13:14]).astype(f32)
+    hw = jnp.zeros((1, 128), f32)
+    for h in range(HEADS):
+        hw = jnp.where(lane == h, hw_ref[h], hw)
+    gains = GAIN * POINT * 0.5 * (jnp.maximum(hw, 0.0) + jnp.log1p(jnp.exp(-jnp.abs(hw))))
+    for h in range(HEADS):
+        at = slice(h * rows, (h + 1) * rows)
+        square = jnp.sum(key_square[h * QP : (h + 1) * QP], 0, keepdims=True)
+        bias = jnp.concatenate([bias_low[h * half : (h + 1) * half], bias_high[h * half : (h + 1) * half]], 0)
+        score = (
+            feature[at] + bias + (GAIN * cb_ref[h]) * same + cross[at] + (blocked - gains[:, h : h + 1] * square)
+        )
+        peak = jnp.max(score, 1, keepdims=True)
+        weight = jnp.exp(score - peak)
+        weight = weight / jnp.sum(weight, 1, keepdims=True)
+        prob_ref[at, :] = weight
+        near_ref[at, :] = weight[:, :128]
+    prob = prob_ref[...]
+    prob_low = prob.astype(bf16)
+    mixed = dot(prob_low, x).astype(bf16)
+    mixed = jnp.concatenate([mixed[h * rows : (h + 1) * rows] for h in range(HEADS)], 1)
+    update = dot(mixed, w_mix_ref[...])
+    empty = jnp.zeros((128 - HEADS * VP, keys), f32)
+    value_points = jnp.concatenate([x for p in points for x in (p[wide:], empty)], 0)
+    gathered = dot(prob, value_points, NT, precision=highest)
+    spread = lax.broadcasted_iota(jnp.int32, (1, 3 * 128), 1) % 128 // VP
+    kept = jnp.zeros((rows, 3 * 128), f32)
+    for h in range(HEADS):
+        kept = jnp.where(spread == h, gathered[h * rows : (h + 1) * rows], kept)
+    relative = [kept[:, a * 128 : (a + 1) * 128] - own_cols[:, 9 + a : 10 + a] for a in range(3)]
+    framed = []
+    for b in range(3):
+        framed.append(
+            own_cols[:, b : b + 1] * relative[0]
+            + own_cols[:, 3 + b : 4 + b] * relative[1]
+            + own_cols[:, 6 + b : 7 + b] * relative[2]
+        )
+    length = jnp.sqrt(jnp.maximum(framed[0] * framed[0] + framed[1] * framed[1] + framed[2] * framed[2], 1.0))
+    own_keys = pair_ref.shape[1]
+    for i in range(rows):
+        weight = near_ref[pl.ds(i, HEADS, stride=rows), :][:, :own_keys].astype(bf16)
+        opair_ref[pl.ds(i, HEADS, stride=rows), :] = dot(weight, pair_ref[i])
+    copy.wait()
+    span = HEADS * VP
+    for n, part in enumerate(framed + [length]):
+        update = update + dot(part[:, :span].astype(bf16), w_tail_ref[n * span : (n + 1) * span])
+    paired = jnp.concatenate([opair_ref[h * rows : (h + 1) * rows, :] for h in range(HEADS)], 1).astype(bf16)
+    out_ref[...] = (0.25 * update + dot(paired, w_tail_ref[4 * span :])).astype(out_ref.dtype)
+
+
+def node_kernel(u0_ref, u1_ref, u2_ref, u3_ref, own_ref, rows_ref, w_in_ref, w_back_ref, w_edge_ref, node_ref, side_ref):
+    update = (u0_ref[...].astype(f32) + u1_ref[...].astype(f32)) + (u2_ref[...].astype(f32) + u3_ref[...].astype(f32))
+    normed = layer_norm(own_ref[...].astype(f32) + update).astype(bf16)
+    middle = jnp.maximum(dot(normed, w_in_ref[...]), 0.0).astype(bf16)
+    node = layer_norm(normed.astype(f32) + dot(middle, w_back_ref[...]))
+    node = (node * rows_ref[:, 12:13]).astype(bf16)
+    node_ref[...] = node
+    side_ref[...] = dot(node, w_edge_ref[...]).astype(bf16)
+
+
+def edge_kernel(side_ref, other_ref, rows_ref, keys_ref, pair_ref, w_in_ref, w_mid_ref, w_final_ref, out_ref):
+    rows, keys = pair_ref.shape[:2]
+    step = 8
+    w_in = w_in_ref[...]
+    side = side_ref[...]
+    other = other_ref[...]
+    pre_rows = dot(side, w_in[CZ : CZ + NH])
+    pre_keys = dot(other, w_in[CZ + NH :])
+    side = side.astype(f32)
+    other = other.astype(f32)
+    keep_rows = rows_ref[:, 12:13]
+    keep_keys = keys_ref[:, 12:13]
+    for begin in range(0, rows, step):
+        pair = pair_ref[begin : begin + step].reshape(step * keys, CZ)
+        lifted = dot(pair, w_in[:CZ])
+        first = jnp.concatenate(
+            [
+                jnp.maximum(lifted[n * keys : (n + 1) * keys] + (pre_keys + pre_rows[begin + n : begin + n + 1]), 0.0).astype(bf16)
+                for n in range(step)
+            ],
+            0,
+        )
+        second = jnp.maximum(dot(first, w_mid_ref[...]), 0.0)
+        stacked = jnp.concatenate(
+            [
+                pair.astype(f32),
+                jnp.concatenate([jnp.broadcast_to(side[begin + n : begin + n + 1], (keys, NH)) for n in range(step)], 0),
+                jnp.concatenate([other] * step, 0),
+            ],
+            1,
+        )
+        edge = layer_norm(dot((second + stacked).astype(bf16), w_final_ref[...]))
+        for n in range(step):
+            keep = keep_keys * keep_rows[begin + n : begin + n + 1]
+            out_ref[begin + n] = (edge[n * keys : (n + 1) * keys] * keep).astype(bf16)
+
+
+def tile_body(
+    node_embed, rotation, translation, pair_embed, chain_index, residue_mask, step_index, w_time, w_query,
+    w_query_points, w_kv, w_kvp, w_bias, head_weights, chain_bias, w_out, w_mlp_in, w_mlp_out, w_edge_in,
+    w_trunk_in, w_trunk_mid, w_final,
+):
+    rows = node_embed.shape[0]
+    total = residue_mask.shape[0]
+    smem = pl.BlockSpec(memory_space=pltpu.SMEM)
+    others = [lax.ppermute(node_embed, "row", [(i, (i + k) % 4) for i in range(4)]) for k in (1, 2, 3)]
+    bias = pl.pallas_call(
+        bias_kernel,
+        out_shape=jax.ShapeDtypeStruct((HEADS * rows // 2, 2 * PAD), f32),
+        in_specs=vmem(2),
+        out_specs=pl.BlockSpec(memory_space=pltpu.VMEM),
+        compiler_params=params(16),
+    )(pair_embed, w_bias)
+    biases = [lax.ppermute(bias, "col", [(i, i ^ k) for i in range(4)]) for k in (1, 2, 3)]
+    feats = jnp.concatenate(
+        [
+            rotation.reshape(9, total),
+            translation,
+            residue_mask.astype(f32)[None],
+            chain_index.astype(f32)[None],
+            jnp.zeros((2, total), f32),
+        ],
+        0,
+    )
+    prepared = pl.pallas_call(
+        prepare_kernel,
+        out_shape=(
+            jax.ShapeDtypeStruct((8, CS), f32),
+            jax.ShapeDtypeStruct((rows, CS), bf16),
+            jax.ShapeDtypeStruct((HEADS * rows, CS), bf16),
+            jax.ShapeDtypeStruct((HEADS * rows, 4 * HEADS * QP), f32),
+            jax.ShapeDtypeStruct((HEADS * CH, CS), bf16),
+            jax.ShapeDtypeStruct((w_kvp.shape[1], CS), bf16),
+            jax.ShapeDtypeStruct((16, 4 * PAD), f32),
+            jax.ShapeDtypeStruct((rows, 16), f32),
+            jax.ShapeDtypeStruct((rows, 16), f32),
+        ),
+        in_specs=[smem, smem] + vmem(7) + [pl.BlockSpec(memory_space=pl.ANY)],
+        out_specs=tuple(vmem(9)),
+        scratch_shapes=[pltpu.VMEM((HEADS * CH, CS), bf16), pltpu.SemaphoreType.DMA],
+        compiler_params=params(24),
+        cost_estimate=pl.CostEstimate(flops=2 * 10**9, bytes_accessed=8 * 10**6, transcendentals=0),
+    )(step_index, head_weights, node_embed, feats, w_time, w_query, w_query_points, w_kv, w_kvp, w_out)
+    time, own, qk, qpts, w_mix, w_pts, kfeat, row_cols, key_cols = prepared
+    partial = pl.pallas_call(
+        attention_kernel,
+        out_shape=jax.ShapeDtypeStruct((rows, CS), f32),
+        in_specs=[smem, smem] + vmem(16) + [pl.BlockSpec(memory_space=pl.ANY)],
+        out_specs=pl.BlockSpec(memory_space=pltpu.VMEM),
+        scratch_shapes=[
+            pltpu.VMEM((4 * PAD, CS), bf16),
+            pltpu.VMEM((HEADS * rows, 4 * PAD), f32),
+            pltpu.VMEM((HEADS * rows, 2 * PAD), f32),
+            pltpu.VMEM((HEADS * rows, CZ), f32),
+            pltpu.VMEM((w_out.shape[0] - HEADS * CH, CS), bf16),
+            pltpu.SemaphoreType.DMA,
+        ],
+        compiler_params=params(24),
+    )(head_weights, chain_bias, own, *others, time, qk, qpts, w_mix, w_pts, kfeat, row_cols, bias, *biases, pair_embed, w_out)
+    partials = [lax.ppermute(partial, "col", [(i, i ^ k) for i in range(4)]) for k in (1, 2, 3)]
+    node_out, side = pl.pallas_call(
+        node_kernel,
+        out_shape=(jax.ShapeDtypeStruct((rows, CS), bf16), jax.ShapeDtypeStruct((rows, NH), bf16)),
+        in_specs=vmem(9),
+        out_specs=tuple(vmem(2)),
+        compiler_params=params(16),
+    )(partial, *partials, own, row_cols, w_mlp_in, w_mlp_out, w_edge_in)
+    turned = [(c * 4 + r, r * 4 + c) for r in range(4) for c in range(4)]
+    other = lax.ppermute(side, ("row", "col"), turned)
+    pair_out = pl.pallas_call(
+        edge_kernel,
+        out_shape=jax.ShapeDtypeStruct(pair_embed.shape, bf16),
+        in_specs=vmem(8),
+        out_specs=pl.BlockSpec(memory_space=pltpu.VMEM),
+        compiler_params=params(24),
+    )(side, other, row_cols, key_cols, pair_embed, w_trunk_in, w_trunk_mid, w_final)
+    return node_out, pair_out
+
+
+def dispatch(sizes, *arrays):
+    rows, keys = arrays[3].shape[:2]
+    square = sizes["row"] == 4 and sizes["col"] == 4 and rows == keys and rows == 48
+    return tile_body(*arrays) if square else body(*arrays)
+
+
 def solution(mesh):
     return jax.shard_map(
-        body,
+        functools.partial(dispatch, dict(mesh.shape)),
         mesh=mesh,
         in_specs=(
             P(("groups", "row"), None),

time: 136 us -> 47.8 us (0.35)
  the two profiles are of different devices: /device:TPU:0 before, /device:TPU:3 now
where the time goes in v1:
time: 47.8 us; the launch traced here: 47.2 us
  starting transfers between devices  12.6 us (26%)
  local copies, waits for them, and re-layouts  12 us (25%)
  Pallas kernels  11.9 us (25%)
  waiting for transfers between devices  7.88 us (16%)
  between operations  1.49 us (3%)
  other arithmetic  1.36 us (3%)
    unnamed x35, local copies, waits for them, and re-layouts  10.6 us
    ppermute x1, waiting for transfers between devices, tile_body(): other = lax.ppermute(side, ('row', 'col'), turned)  5.04 us
    ppermute x3, starting transfers between devices, tile_body(): lax.ppermute(node_embed, 'row', [(i, (i + k) % 4) for i in range(4)])  4.78 us
    pallas_call x1, Pallas kernels, tile_body(): pl.pallas_call(edge_kernel, out_shape=jax.ShapeDtypeStruct(pair_embed.sha...  3.97 us
    pallas_call x1, Pallas kernels, tile_body(): pl.pallas_call(attention_kernel, out_shape=jax.ShapeDtypeStruct((rows, CS...  3.69 us
    ppermute x3, waiting for transfers between devices, tile_body(): lax.ppermute(partial, 'col', [(i, i ^ k) for i in range(4)])  2.82 us
    ppermute x3, starting transfers between devices, tile_body(): lax.ppermute(bias, 'col', [(i, i ^ k) for i in range(4)])  2.7 us
    ppermute x1, starting transfers between devices, tile_body(): other = lax.ppermute(side, ('row', 'col'), turned)  2.65 us
  transfers between devices with their start and end apart: 10, of which 3 were waited for; matrix products, arithmetic and copies ran while one was open for 12% of the time, Pallas kernels for 6%

profile of v1, /device:TPU:3, one launch (start us, length us, event | category | flops | bytes accessed | tf_op | source)
XLA Modules:
  0.0 47.2 jit_solution(16575308269140090404)
XLA Ops:
  0.6 1.3 %collective-permute-start = (bf16[48,256]{1,0:T(8,128)(2,1)}, bf16[48,256]{1,0:T(8,128)(2,1)S(1)}, u32[]{:S(2)}, u32[]{:S(2)}) collective-permute-start(bf16[48,256]{1,0:T(8,128)(2,1)} %node_ref.1), channel_id=1, source_target_pairs={{0,4},{4,8},{8,12},{12,0},{1,5},{5,9},{9,13},{13,1},{2,6},{6,10},{... | collective-permute-start | bytes 73736 | tf_op jit(solution)/shard_map/ppermute | solution.py:517
  2.0 0.8 %copy.26.w_ref = bf16[128,8]{1,0:T(8,128)(2,1)S(1)} copy(bf16[128,8]{0,1:T(8,128)(2,1)} %param.34) | data formatting | bytes 4096 | tf_op args[12]
  2.8 1.1 %copy-done = bf16[48,48,128]{2,1,0:T(8,128)(2,1)S(1)} copy-done((bf16[48,48,128]{2,1,0:T(8,128)(2,1)S(1)}, bf16[48,48,128]{2,1,0:T(8,128)(2,1)}, u32[]{:S(2)}) %copy-start) | copy-done | bytes 589848
  3.8 0.5 %shard_map.222.b0_ref = f32[192,128]{1,0:T(8,128)S(1)} custom-call(bf16[48,48,128]{2,1,0:T(8,128)(2,1)S(1)} %copy-done, bf16[128,8]{1,0:T(8,128)(2,1)S(1)} %copy.26.w_ref), custom_call_target="tpu_custom_call" | custom-call | tf_op jit(solution)/shard_map/pallas_call | solution.py:518
  4.3 1.0 %collective-permute-start.3 = (f32[192,128]{1,0:T(8,128)S(1)}, f32[192,128]{1,0:T(8,128)S(1)}, u32[]{:S(2)}, u32[]{:S(2)}) collective-permute-start(f32[192,128]{1,0:T(8,128)S(1)} %shard_map.222.b0_ref), channel_id=1, source_target_pairs={{0,1},{1,0},{2,3},{3,2},{4,5},{5,4},{6,7},{7,6},{8,9},{9,8},{10,11... | collective-permute-start | bytes 294920 | tf_op jit(solution)/shard_map/ppermute | solution.py:525
  5.3 0.3 collective-permute-start.4
  5.6 1.4 %collective-permute-start.5 = (f32[192,128]{1,0:T(8,128)S(1)}, f32[192,128]{1,0:T(8,128)S(1)}, u32[]{:S(2)}, u32[]{:S(2)}) collective-permute-start(f32[192,128]{1,0:T(8,128)S(1)} %shard_map.222.b0_ref), channel_id=1, source_target_pairs={{0,3},{1,2},{2,1},{3,0},{4,7},{5,6},{6,5},{7,4},{8,11},{9,10},{10,... | collective-permute-start | bytes 294920 | tf_op jit(solution)/shard_map/ppermute | solution.py:525
  7.0 2.3 %collective-permute-start.1 = (bf16[48,256]{1,0:T(8,128)(2,1)}, bf16[48,256]{1,0:T(8,128)(2,1)S(1)}, u32[]{:S(2)}, u32[]{:S(2)}) collective-permute-start(bf16[48,256]{1,0:T(8,128)(2,1)} %node_ref.1), channel_id=1, source_target_pairs={{0,8},{4,12},{8,0},{12,4},{1,9},{5,13},{9,1},{13,5},{2,10},{6,14},... | collective-permute-start | bytes 73736 | tf_op jit(solution)/shard_map/ppermute | solution.py:517
  9.3 1.1 %copy.25.w_kvp_ref = bf16[256,480]{1,0:T(8,128)(2,1)S(1)} copy(bf16[256,480]{0,1:T(8,128)(2,1)} %param.33) | data formatting | bytes 491520 | tf_op args[11]
  10.4 1.0 %copy.24.w_qp_ref = bf16[256,192]{1,0:T(8,128)(2,1)S(1)} copy(bf16[256,192]{0,1:T(8,128)(2,1)} %param.31) | data formatting | bytes 196608 | tf_op args[9]
  11.4 0.7 %reshape.7 = f32[9,192]{1,0:T(8,128)S(1)} reshape(f32[3,3,192]{2,1,0:T(4,128)} %param.23) | data formatting | bytes 13824 | tf_op jit(solution)/shard_map/reshape | solution.py:528
  12.1 0.7 %convert_element_type.6 = f32[192]{0:T(256)S(1)} convert(s32[192]{0:T(256)} %param.27) | non-fusion elementwise | flops 192 | bytes 1536 | tf_op jit(solution)/shard_map/convert_element_type | solution.py:530
  12.8 0.7 %convert_element_type.7 = f32[192]{0:T(256)S(1)} convert(s32[192]{0:T(256)} %param.26) | non-fusion elementwise | flops 192 | bytes 1536 | tf_op jit(solution)/shard_map/convert_element_type | solution.py:531
  14.2 0.0 copy-start.11
  14.2 0.7 %concatenate.3.feats_ref = f32[16,192]{1,0:T(8,128)S(1)} concatenate(f32[9,192]{1,0:T(8,128)S(1)} %reshape.7, f32[3,192]{1,0:T(4,128)} %param.24, f32[1,192]{1,0:T(1,128)S(1)} %bitcast.2, f32[1,192]{1,0:T(1,128)S(1)} %bitcast.3, f32[2,192]{1,0:T(2,128)S(1)} %broadcast_in_dim.11), dimensions={0} | concatenate | bytes 24576 | tf_op jit(solution)/shard_map/concatenate | solution.py:526
  14.9 0.0 collective-permute-done.n1_ref
  14.9 1.1 %collective-permute-start.2 = (bf16[48,256]{1,0:T(8,128)(2,1)}, bf16[48,256]{1,0:T(8,128)(2,1)S(1)}, u32[]{:S(2)}, u32[]{:S(2)}) collective-permute-start(bf16[48,256]{1,0:T(8,128)(2,1)} %node_ref.1), channel_id=1, source_target_pairs={{0,12},{4,0},{8,4},{12,8},{1,13},{5,1},{9,5},{13,9},{2,14},{6,2},{... | collective-permute-start | bytes 73736 | tf_op jit(solution)/shard_map/ppermute | solution.py:517
  16.0 1.5 %copy-done.2 = bf16[3456,256]{1,0:T(8,128)(2,1)S(1)} copy-done((bf16[3456,256]{1,0:T(8,128)(2,1)S(1)}, bf16[3456,256]{1,0:T(8,128)(2,1)}, u32[]{:S(2)}) %copy-start.2) | copy-done | bytes 1769496
  17.5 0.7 %copy-done.10 = f32[8]{0:T(128)S(1)} copy-done((f32[8]{0:T(128)S(1)}, f32[8]{0:T(128)}, u32[]{:S(2)}) %copy-start.10) | copy-done | bytes 56
  18.2 1.6 %copy-done.12 = bf16[256,4096]{1,0:T(8,128)(2,1)S(1)} copy-done((bf16[256,4096]{1,0:T(8,128)(2,1)S(1)}, bf16[256,4096]{1,0:T(8,128)(2,1)}, u32[]{:S(2)}) %copy-start.12) | copy-done | bytes 2097176
  19.8 1.2 %copy-done.13 = bf16[256,2048]{1,0:T(8,128)(2,1)S(1)} copy-done((bf16[256,2048]{1,0:T(8,128)(2,1)S(1)}, bf16[256,2048]{1,0:T(8,128)(2,1)}, u32[]{:S(2)}) %copy-start.13) | copy-done | bytes 1048600
  21.0 0.9 %copy-done.14 = bf16[256,256]{1,0:T(8,128)(2,1)S(1)} copy-done((bf16[256,256]{1,0:T(8,128)(2,1)S(1)}, bf16[256,256]{1,0:T(8,128)(2,1)}, u32[]{:S(2)}) %copy-start.14) | copy-done | bytes 131096
  21.9 0.7 %copy-done.15 = bf16[48,256]{1,0:T(8,128)(2,1)S(1)} copy-done((bf16[48,256]{1,0:T(8,128)(2,1)S(1)}, bf16[48,256]{1,0:T(8,128)(2,1)}, u32[]{:S(2)}) %copy-start.15) | copy-done | bytes 24600
  22.6 2.5 %shard_map.221 = (f32[8,256]{1,0:T(8,128)S(1)}, bf16[48,256]{1,0:T(8,128)(2,1)S(1)}, bf16[384,256]{1,0:T(8,128)(2,1)S(1)}, f32[384,256]{1,0:T(8,128)S(1)}, bf16[...) custom-call(s32[1]{0:T(128)S(6)} %copy.27.step_ref, ...), custom_call_target="tpu_custom_call" | custom-call | flops 2000000000 | bytes 8000000 | tf_op jit(solution)/shard_map/pallas_call | solution.py:536
  25.1 0.0 collective-permute-done.1.n2_ref
  25.1 0.0 collective-permute-done.2.n3_ref
  25.1 0.0 collective-permute-done.3.b1_ref
  25.1 0.0 collective-permute-done.4.b2_ref
  25.2 0.0 collective-permute-done.5.b3_ref
  25.2 0.0 copy-start.6
  25.2 0.0 copy-start.7
  25.2 0.0 copy-start.9
  25.2 0.0 copy-start.4
  25.2 0.0 copy-start.5
  25.3 0.0 copy-start.8
  25.3 3.7 %shard_map.223.u0_ref = f32[48,256]{1,0:T(8,128)S(1)} custom-call(f32[8]{0:T(128)S(1)} %copy-done.10, f32[8]{0:T(128)S(1)} %copy-done.11, bf16[48,256]{1,0:T(8,128)(2,1)S(1)} %get-tuple-element.13.own_ref, bf16[48,256]{1,0:T(8,128)(2,1)S(1)} %collective-permute-done.n1_ref, bf16[48,256]{1,0:T(8,128)(2,1)S(1)} %collective-permute-done.1.n2_ref, ...), custom_call_target="tpu_custom_call" | custom-call | tf_op jit(solution)/shard_map/pallas_call | solution.py:556
  29.0 0.8 %collective-permute-start.6 = (f32[48,256]{1,0:T(8,128)S(1)}, f32[48,256]{1,0:T(8,128)S(1)}, u32[]{:S(2)}, u32[]{:S(2)}) collective-permute-start(f32[48,256]{1,0:T(8,128)S(1)} %shard_map.223.u0_ref), channel_id=1, source_target_pairs={{0,1},{1,0},{2,3},{3,2},{4,5},{5,4},{6,7},{7,6},{8,9},{9,8},{10,11... | collective-permute-start | bytes 147464 | tf_op jit(solution)/shard_map/ppermute | solution.py:571
  29.7 0.3 collective-permute-start.7
  30.0 1.4 %collective-permute-start.8 = (f32[48,256]{1,0:T(8,128)S(1)}, f32[48,256]{1,0:T(8,128)S(1)}, u32[]{:S(2)}, u32[]{:S(2)}) collective-permute-start(f32[48,256]{1,0:T(8,128)S(1)} %shard_map.223.u0_ref), channel_id=1, source_target_pairs={{0,3},{1,2},{2,1},{3,0},{4,7},{5,6},{6,5},{7,4},{8,11},{9,10},{10,... | collective-permute-start | bytes 147464 | tf_op jit(solution)/shard_map/ppermute | solution.py:571
  31.5 0.0 collective-permute-done.6.u1_ref
  31.5 1.2 %collective-permute-done.7.u2_ref = f32[48,256]{1,0:T(8,128)S(1)} collective-permute-done((f32[48,256]{1,0:T(8,128)S(1)}, f32[48,256]{1,0:T(8,128)S(1)}, u32[]{:S(2)}, u32[]{:S(2)}) %collective-permute-start.7) | collective-permute-done | bytes 49184 | tf_op jit(solution)/shard_map/ppermute | solution.py:571
  32.7 1.6 %collective-permute-done.8.u3_ref = f32[48,256]{1,0:T(8,128)S(1)} collective-permute-done((f32[48,256]{1,0:T(8,128)S(1)}, f32[48,256]{1,0:T(8,128)S(1)}, u32[]{:S(2)}, u32[]{:S(2)}) %collective-permute-start.8) | collective-permute-done | bytes 49184 | tf_op jit(solution)/shard_map/ppermute | solution.py:571
  34.3 0.0 copy-done.7
  34.3 1.2 %shard_map.224 = (bf16[48,256]{1,0:T(8,128)(2,1)}, bf16[48,128]{1,0:T(8,128)(2,1)S(1)}) custom-call(f32[48,256]{1,0:T(8,128)S(1)} %shard_map.223.u0_ref, f32[48,256]{1,0:T(8,128)S(1)} %collective-permute-done.6.u1_ref, f32[48,256]{1,0:T(8,128)S(1)} %collective-permute-done.7.u2_ref, f32[48,256]{1,0:T(8,128)S(1)} %collective-permute-done.8.u3_ref, ...), custom_call_target="tpu_custom_call" | custom-call | tf_op jit(solution)/shard_map/pallas_call | solution.py:572
  35.5 2.7 %collective-permute-start.9 = (bf16[48,128]{1,0:T(8,128)(2,1)S(1)}, bf16[48,128]{1,0:T(8,128)(2,1)S(1)}, u32[]{:S(2)}, u32[]{:S(2)}) collective-permute-start(bf16[48,128]{1,0:T(8,128)(2,1)S(1)} %get-tuple-element.22.side_ref), channel_id=1, source_target_pairs={{0,0},{4,1},{8,2},{12,3},{1,4},{5,5},{9,6},{13,7},{2,8},{6,9},{10,... | collective-permute-start | bytes 36872 | tf_op jit(solution)/shard_map/ppermute | solution.py:580
  38.2 5.0 %collective-permute-done.9.other_ref = bf16[48,128]{1,0:T(8,128)(2,1)S(1)} collective-permute-done((bf16[48,128]{1,0:T(8,128)(2,1)S(1)}, bf16[48,128]{1,0:T(8,128)(2,1)S(1)}, u32[]{:S(2)}, u32[]{:S(2)}) %collective-permute-start.9) | collective-permute-done | bytes 12320 | tf_op jit(solution)/shard_map/ppermute | solution.py:580
  43.2 0.0 copy-done.5
  43.2 4.0 %shard_map.225 = bf16[48,48,128]{2,1,0:T(8,128)(2,1)} custom-call(bf16[48,128]{1,0:T(8,128)(2,1)S(1)} %get-tuple-element.22.side_ref, bf16[48,128]{1,0:T(8,128)(2,1)S(1)} %collective-permute-done.9.other_ref, f32[48,16]{1,0:T(8,128)S(1)} %get-tuple-element.20.rows_ref, f32[48,16]{1,0:T(8,128)S(1)} %get-tuple-element.23.keys_ref, ...), custom_call_target="tpu_custom_call" | custom-call | tf_op jit(solution)/shard_map/pallas_call | solution.py:581
  (17 shorter events, 0.0 us)
Async XLA Ops:
  0.6 14.3 %collective-permute-start = (bf16[48,256]{1,0:T(8,128)(2,1)}, bf16[48,256]{1,0:T(8,128)(2,1)S(1)}, u32[]{:S(2)}, u32[]{:S(2)}) collective-permute-start(bf16[48,256]{1,0:T(8,128)(2,1)} %node_ref.1), channel_id=1, source_target_pairs={{0,4},{4,8},{8,12},{12,0},{1,5},{5,9},{9,13},{13,1},{2,6},{6,10},{... | collective-permute-start | bytes 73736 | tf_op jit(solution)/shard_map/ppermute | solution.py:517
  2.8 1.1 %copy-start = (bf16[48,48,128]{2,1,0:T(8,128)(2,1)S(1)}, bf16[48,48,128]{2,1,0:T(8,128)(2,1)}, u32[]{:S(2)}) copy-start(bf16[48,48,128]{2,1,0:T(8,128)(2,1)} %pair_ref.5) | copy-start | bytes 1769476
  4.3 20.8 %collective-permute-start.3 = (f32[192,128]{1,0:T(8,128)S(1)}, f32[192,128]{1,0:T(8,128)S(1)}, u32[]{:S(2)}, u32[]{:S(2)}) collective-permute-start(f32[192,128]{1,0:T(8,128)S(1)} %shard_map.222.b0_ref), channel_id=1, source_target_pairs={{0,1},{1,0},{2,3},{3,2},{4,5},{5,4},{6,7},{7,6},{8,9},{9,8},{10,11... | collective-permute-start | bytes 294920 | tf_op jit(solution)/shard_map/ppermute | solution.py:525
  5.3 19.8 %collective-permute-start.4 = (f32[192,128]{1,0:T(8,128)S(1)}, f32[192,128]{1,0:T(8,128)S(1)}, u32[]{:S(2)}, u32[]{:S(2)}) collective-permute-start(f32[192,128]{1,0:T(8,128)S(1)} %shard_map.222.b0_ref), channel_id=1, source_target_pairs={{0,2},{1,3},{2,0},{3,1},{4,6},{5,7},{6,4},{7,5},{8,10},{9,11},{10,... | collective-permute-start | bytes 294920 | tf_op jit(solution)/shard_map/ppermute | solution.py:525
  5.6 19.6 %collective-permute-start.5 = (f32[192,128]{1,0:T(8,128)S(1)}, f32[192,128]{1,0:T(8,128)S(1)}, u32[]{:S(2)}, u32[]{:S(2)}) collective-permute-start(f32[192,128]{1,0:T(8,128)S(1)} %shard_map.222.b0_ref), channel_id=1, source_target_pairs={{0,3},{1,2},{2,1},{3,0},{4,7},{5,6},{6,5},{7,4},{8,11},{9,10},{10,... | collective-permute-start | bytes 294920 | tf_op jit(solution)/shard_map/ppermute | solution.py:525
  7.0 18.1 %collective-permute-start.1 = (bf16[48,256]{1,0:T(8,128)(2,1)}, bf16[48,256]{1,0:T(8,128)(2,1)S(1)}, u32[]{:S(2)}, u32[]{:S(2)}) collective-permute-start(bf16[48,256]{1,0:T(8,128)(2,1)} %node_ref.1), channel_id=1, source_target_pairs={{0,8},{4,12},{8,0},{12,4},{1,9},{5,13},{9,1},{13,5},{2,10},{6,14},... | collective-permute-start | bytes 73736 | tf_op jit(solution)/shard_map/ppermute | solution.py:517
  14.2 11.0 %copy-start.11 = (f32[8]{0:T(128)S(1)}, f32[8]{0:T(128)}, u32[]{:S(2)}) copy-start(f32[8]{0:T(128)} %cb_ref.1) | copy-start | bytes 100
  14.9 10.3 %copy-start.1 = (bf16[48,48,128]{2,1,0:T(8,128)(2,1)S(1)}, bf16[48,48,128]{2,1,0:T(8,128)(2,1)}, u32[]{:S(2)}) copy-start(bf16[48,48,128]{2,1,0:T(8,128)(2,1)} %pair_ref.5) | copy-start | bytes 1769476
  14.9 10.2 %collective-permute-start.2 = (bf16[48,256]{1,0:T(8,128)(2,1)}, bf16[48,256]{1,0:T(8,128)(2,1)S(1)}, u32[]{:S(2)}, u32[]{:S(2)}) collective-permute-start(bf16[48,256]{1,0:T(8,128)(2,1)} %node_ref.1), channel_id=1, source_target_pairs={{0,12},{4,0},{8,4},{12,8},{1,13},{5,1},{9,5},{13,9},{2,14},{6,2},{... | collective-permute-start | bytes 73736 | tf_op jit(solution)/shard_map/ppermute | solution.py:517
  16.0 1.5 %copy-start.2 = (bf16[3456,256]{1,0:T(8,128)(2,1)S(1)}, bf16[3456,256]{1,0:T(8,128)(2,1)}, u32[]{:S(2)}) copy-start(bf16[3456,256]{1,0:T(8,128)(2,1)} %w_out_ref.3) | copy-start | bytes 5308420
  17.5 0.7 %copy-start.10 = (f32[8]{0:T(128)S(1)}, f32[8]{0:T(128)}, u32[]{:S(2)}) copy-start(f32[8]{0:T(128)} %hw_ref.3) | copy-start | bytes 100
  18.2 1.6 %copy-start.12 = (bf16[256,4096]{1,0:T(8,128)(2,1)S(1)}, bf16[256,4096]{1,0:T(8,128)(2,1)}, u32[]{:S(2)}) copy-start(bf16[256,4096]{1,0:T(8,128)(2,1)} %w_kv_ref.1) | copy-start | bytes 6291460
  19.8 1.2 %copy-start.13 = (bf16[256,2048]{1,0:T(8,128)(2,1)S(1)}, bf16[256,2048]{1,0:T(8,128)(2,1)}, u32[]{:S(2)}) copy-start(bf16[256,2048]{1,0:T(8,128)(2,1)} %w_query_ref.1) | copy-start | bytes 3145732
  21.0 0.9 %copy-start.14 = (bf16[256,256]{1,0:T(8,128)(2,1)S(1)}, bf16[256,256]{1,0:T(8,128)(2,1)}, u32[]{:S(2)}) copy-start(bf16[256,256]{1,0:T(8,128)(2,1)} %w_time_ref.1) | copy-start | bytes 393220
  21.9 0.7 %copy-start.15 = (bf16[48,256]{1,0:T(8,128)(2,1)S(1)}, bf16[48,256]{1,0:T(8,128)(2,1)}, u32[]{:S(2)}) copy-start(bf16[48,256]{1,0:T(8,128)(2,1)} %node_ref.1) | copy-start | bytes 73732
  22.6 2.6 %copy-start.3 = (bf16[3456,256]{1,0:T(8,128)(2,1)S(1)}, bf16[3456,256]{1,0:T(8,128)(2,1)}, u32[]{:S(2)}) copy-start(bf16[3456,256]{1,0:T(8,128)(2,1)} %w_out_ref.3) | copy-start | bytes 5308420
  25.2 9.1 %copy-start.6 = (bf16[256,256]{1,0:T(8,128)(2,1)S(1)}, bf16[256,256]{1,0:T(8,128)(2,1)}, u32[]{:S(2)}) copy-start(bf16[256,256]{1,0:T(8,128)(2,1)} %w_in_ref.2) | copy-start | bytes 393220
  25.2 9.1 %copy-start.7 = (bf16[256,256]{1,0:T(8,128)(2,1)S(1)}, bf16[256,256]{1,0:T(8,128)(2,1)}, u32[]{:S(2)}) copy-start(bf16[256,256]{1,0:T(8,128)(2,1)} %w_back_ref.1) | copy-start | bytes 393220
  25.2 9.1 %copy-start.9 = (bf16[256,128]{1,0:T(8,128)(2,1)S(1)}, bf16[256,128]{1,0:T(8,128)(2,1)}, u32[]{:S(2)}) copy-start(bf16[256,128]{1,0:T(8,128)(2,1)} %w_edge_ref.1) | copy-start | bytes 196612
  25.2 18.0 %copy-start.4 = (bf16[384,384]{1,0:T(8,128)(2,1)S(1)}, bf16[384,384]{1,0:T(8,128)(2,1)}, u32[]{:S(2)}) copy-start(bf16[384,384]{1,0:T(8,128)(2,1)} %w_in_ref.3) | copy-start | bytes 884740
  25.2 18.0 %copy-start.5 = (bf16[384,384]{1,0:T(8,128)(2,1)S(1)}, bf16[384,384]{1,0:T(8,128)(2,1)}, u32[]{:S(2)}) copy-start(bf16[384,384]{1,0:T(8,128)(2,1)} %w_mid_ref.1) | copy-start | bytes 884740
  25.3 18.0 %copy-start.8 = (bf16[384,128]{1,0:T(8,128)(2,1)S(1)}, bf16[384,128]{1,0:T(8,128)(2,1)}, u32[]{:S(2)}) copy-start(bf16[384,128]{1,0:T(8,128)(2,1)} %w_final_ref.1) | copy-start | bytes 294916
  29.0 2.5 %collective-permute-start.6 = (f32[48,256]{1,0:T(8,128)S(1)}, f32[48,256]{1,0:T(8,128)S(1)}, u32[]{:S(2)}, u32[]{:S(2)}) collective-permute-start(f32[48,256]{1,0:T(8,128)S(1)} %shard_map.223.u0_ref), channel_id=1, source_target_pairs={{0,1},{1,0},{2,3},{3,2},{4,5},{5,4},{6,7},{7,6},{8,9},{9,8},{10,11... | collective-permute-start | bytes 147464 | tf_op jit(solution)/shard_map/ppermute | solution.py:571
  29.7 3.0 %collective-permute-start.7 = (f32[48,256]{1,0:T(8,128)S(1)}, f32[48,256]{1,0:T(8,128)S(1)}, u32[]{:S(2)}, u32[]{:S(2)}) collective-permute-start(f32[48,256]{1,0:T(8,128)S(1)} %shard_map.223.u0_ref), channel_id=1, source_target_pairs={{0,2},{1,3},{2,0},{3,1},{4,6},{5,7},{6,4},{7,5},{8,10},{9,11},{10,... | collective-permute-start | bytes 147464 | tf_op jit(solution)/shard_map/ppermute | solution.py:571
  30.0 4.3 %collective-permute-start.8 = (f32[48,256]{1,0:T(8,128)S(1)}, f32[48,256]{1,0:T(8,128)S(1)}, u32[]{:S(2)}, u32[]{:S(2)}) collective-permute-start(f32[48,256]{1,0:T(8,128)S(1)} %shard_map.223.u0_ref), channel_id=1, source_target_pairs={{0,3},{1,2},{2,1},{3,0},{4,7},{5,6},{6,5},{7,4},{8,11},{9,10},{10,... | collective-permute-start | bytes 147464 | tf_op jit(solution)/shard_map/ppermute | solution.py:571
  35.5 7.7 %collective-permute-start.9 = (bf16[48,128]{1,0:T(8,128)(2,1)S(1)}, bf16[48,128]{1,0:T(8,128)(2,1)S(1)}, u32[]{:S(2)}, u32[]{:S(2)}) collective-permute-start(bf16[48,128]{1,0:T(8,128)(2,1)S(1)} %get-tuple-element.22.side_ref), channel_id=1, source_target_pairs={{0,0},{4,1},{8,2},{12,3},{1,4},{5,5},{9,6},{13,7},{2,8},{6,9},{10,... | collective-permute-start | bytes 36872 | tf_op jit(solution)/shard_map/ppermute | solution.py:580

commit v2 on v1

--- a/solution.py
+++ b/solution.py
@@ -273,14 +273,23 @@
     return [pl.BlockSpec(memory_space=pltpu.VMEM)] * count
 
 
-def bias_kernel(pair_ref, w_ref, out_ref):
-    w_t = jnp.transpose(w_ref[...].astype(f32)).astype(bf16)
+def stay(*arrays):
+    return [pltpu.with_memory_space_constraint(array, pltpu.HBM) for array in arrays]
+
+
+def bias_kernel(pair_hbm, w_hbm, out_ref, pair_ref, w_ref, sems):
+    copies = [pltpu.make_async_copy(pair_hbm, pair_ref, sems.at[0]), pltpu.make_async_copy(w_hbm, w_ref, sems.at[1])]
+    for copy in copies:
+        copy.start()
+    for copy in copies:
+        copy.wait()
     half = pair_ref.shape[0] // 2
     keys = pair_ref.shape[1]
+    weight = w_ref[...]
     gap = jnp.zeros((PAD - keys, CZ), bf16)
     for i in range(half):
         both = jnp.concatenate([pair_ref[i], gap, pair_ref[i + half], gap], 0)
-        out_ref[pl.ds(i, HEADS, stride=half), :] = dot(w_t, both, NT) * GAIN
+        out_ref[pl.ds(i, HEADS, stride=half), :] = dot(weight, both, NT) * GAIN
 
 
 def one_hot(shape, source_dim, offset_of):
@@ -290,16 +299,34 @@
 
 
 def prepare_kernel(
-    step_ref, hw_ref, node_ref, feats_ref, w_time_ref, w_query_ref, w_qp_ref, w_kv_ref, w_kvp_ref, w_out_ref,
-    time_ref, own_ref, qk_ref, qpts_ref, w_mix_ref, w_pts_ref, kfeat_ref, rows_ref, keys_ref, w_head_ref, sem,
+    step_ref, hw_hbm, rotation_hbm, shift_hbm, mask_hbm, chain_hbm, node_hbm, w_time_hbm, w_query_hbm, w_qp_hbm, w_kv_hbm,
+    w_kvp_hbm, w_out_hbm,
+    time_ref, own_ref, qk_ref, qpts_ref, w_mix_ref, w_pts_ref, kfeat_ref, rows_ref, keys_ref,
+    hw_ref, rotation_ref, shift_ref, mask_ref, chain_ref, node_ref, w_time_ref, w_query_ref, w_qp_ref, w_kv_ref,
+    w_kvp_ref, w_head_ref, feats_ref, sems,
 ):
-    copy = pltpu.make_async_copy(w_out_ref.at[pl.ds(0, HEADS * CH)], w_head_ref, sem)
-    copy.start()
+    pairs = (
+        (rotation_hbm, rotation_ref), (shift_hbm, shift_ref), (mask_hbm, mask_ref),
+        (chain_hbm, chain_ref), (node_hbm, node_ref), (w_time_hbm, w_time_ref), (hw_hbm, hw_ref), (w_qp_hbm, w_qp_ref),
+        (w_kvp_hbm, w_kvp_ref), (w_query_hbm, w_query_ref), (w_kv_hbm, w_kv_ref),
+        (w_out_hbm.at[pl.ds(0, HEADS * CH)], w_head_ref),
+    )
+    copies = [pltpu.make_async_copy(src, dst, sems.at[n]) for n, (src, dst) in enumerate(pairs)]
+    for copy in copies:
+        copy.start()
+    for copy in copies[:9]:
+        copy.wait()
     rows = node_ref.shape[0]
-    total = feats_ref.shape[1]
     half = CS // 2
     row = lax.axis_index("row")
     col = lax.axis_index("col")
+    feats_ref[...] = jnp.zeros(feats_ref.shape, f32)
+    for a in range(3):
+        feats_ref[3 * a : 3 * a + 3, :] = rotation_ref[a]
+    feats_ref[9:12, :] = shift_ref[...]
+    feats_ref[12:13, :] = mask_ref[...].astype(f32)
+    feats_ref[13:14, :] = chain_ref[...].astype(f32)
+    total = feats_ref.shape[1]
     lane = lax.broadcasted_iota(jnp.int32, (8, half), 1).astype(f32)
     frequency = jnp.exp(-math.log(10000.0) * lane / half)
     angles = step_ref[0].astype(f32) * frequency
@@ -319,7 +346,8 @@
     own_cols = dot(one_hot((rows, total), 1, lambda d: d + row * rows), feats, NT, precision=highest)
     rows_ref[...] = own_cols
     keys_ref[...] = dot(one_hot((rows, total), 1, lambda d: d + col * rows), feats, NT, precision=highest)
-    copy.wait()
+    for copy in copies[9:]:
+        copy.wait()
     query = dot(own, w_query_ref[...]).astype(bf16)
     for h in range(HEADS):
         taken = dot(query[:, h * CH : (h + 1) * CH], w_kv_ref[:, h * CH : (h + 1) * CH], NT)
@@ -328,7 +356,7 @@
             w_kv_ref[:, (HEADS + h) * CH : (HEADS + h + 1) * CH], w_head_ref[h * CH : (h + 1) * CH, :]
         ).astype(bf16)
     wide = HEADS * QP
-    local = dot(own, w_qp_ref[...])
+    local = dot(own, w_qp_ref[...], NT)
     parts = [local[:, b * wide : (b + 1) * wide] for b in range(3)]
     points = []
     for a in range(3):
@@ -349,7 +377,7 @@
         mine = jnp.where((lanes % wide) // QP == h, points, 0.0)
         square = jnp.sum(mine * mine, 1, keepdims=True)
         qpts_ref[h * rows : (h + 1) * rows, :] = jnp.where(lanes == 3 * wide, -square, 2.0 * mine) * gain
-    width = w_kvp_ref.shape[1]
+    width = w_kvp_ref.shape[0]
     group = HEADS * (QP + VP)
     dst = lax.broadcasted_iota(jnp.int32, (width, width), 0)
     src = lax.broadcasted_iota(jnp.int32, (width, width), 1)
@@ -360,21 +388,19 @@
     from_value = (value // VP) * (QP + VP) + QP + value % VP
     wanted = comp * group + jnp.where(inside < HEADS * QP, from_key, from_value)
     order = (src == wanted).astype(f32).astype(bf16)
-    w_pts_ref[...] = dot(order, w_kvp_ref[...], NT).astype(bf16)
+    w_pts_ref[...] = dot(order, w_kvp_ref[...]).astype(bf16)
 
 
 def attention_kernel(
     hw_ref, cb_ref, own_ref, n1_ref, n2_ref, n3_ref, time_ref, qk_ref, qpts_ref, w_mix_ref, w_pts_ref, kfeat_ref,
     rows_ref, b0_ref, b1_ref, b2_ref, b3_ref, pair_ref, w_out_ref,
-    out_ref, x_ref, prob_ref, near_ref, opair_ref, w_tail_ref, sem,
+    out_ref, x_ref, prob_ref, near_ref, opair_ref,
 ):
     rows = own_ref.shape[0]
     half = rows // 2
     row = lax.axis_index("row")
     col = lax.axis_index("col")
     tail = HEADS * CH
-    copy = pltpu.make_async_copy(w_out_ref.at[pl.ds(tail, w_out_ref.shape[0] - tail)], w_tail_ref, sem)
-    copy.start()
     time = time_ref[0:1]
     x_ref[...] = jnp.zeros(x_ref.shape, bf16)
     x_ref[pl.ds(pl.multiple_of((col ^ row) * PAD, PAD), rows), :] = own_ref[...]
@@ -451,12 +477,11 @@
     for i in range(rows):
         weight = near_ref[pl.ds(i, HEADS, stride=rows), :][:, :own_keys].astype(bf16)
         opair_ref[pl.ds(i, HEADS, stride=rows), :] = dot(weight, pair_ref[i])
-    copy.wait()
     span = HEADS * VP
     for n, part in enumerate(framed + [length]):
-        update = update + dot(part[:, :span].astype(bf16), w_tail_ref[n * span : (n + 1) * span])
+        update = update + dot(part[:, :span].astype(bf16), w_out_ref[tail + n * span : tail + (n + 1) * span])
     paired = jnp.concatenate([opair_ref[h * rows : (h + 1) * rows, :] for h in range(HEADS)], 1).astype(bf16)
-    out_ref[...] = (0.25 * update + dot(paired, w_tail_ref[4 * span :])).astype(out_ref.dtype)
+    out_ref[...] = (0.25 * update + dot(paired, w_out_ref[tail + 4 * span :])).astype(out_ref.dtype)
 
 
 def node_kernel(u0_ref, u1_ref, u2_ref, u3_ref, own_ref, rows_ref, w_in_ref, w_back_ref, w_edge_ref, node_ref, side_ref):
@@ -514,25 +539,21 @@
     rows = node_embed.shape[0]
     total = residue_mask.shape[0]
     smem = pl.BlockSpec(memory_space=pltpu.SMEM)
+    hbm = pl.BlockSpec(memory_space=pltpu.HBM)
     others = [lax.ppermute(node_embed, "row", [(i, (i + k) % 4) for i in range(4)]) for k in (1, 2, 3)]
     bias = pl.pallas_call(
         bias_kernel,
         out_shape=jax.ShapeDtypeStruct((HEADS * rows // 2, 2 * PAD), f32),
-        in_specs=vmem(2),
+        in_specs=[hbm, hbm],
         out_specs=pl.BlockSpec(memory_space=pltpu.VMEM),
+        scratch_shapes=[
+            pltpu.VMEM(pair_embed.shape, bf16),
+            pltpu.VMEM((HEADS, CZ), bf16),
+            pltpu.SemaphoreType.DMA((2,)),
+        ],
         compiler_params=params(16),
-    )(pair_embed, w_bias)
+    )(*stay(pair_embed, w_bias.T))
     biases = [lax.ppermute(bias, "col", [(i, i ^ k) for i in range(4)]) for k in (1, 2, 3)]
-    feats = jnp.concatenate(
-        [
-            rotation.reshape(9, total),
-            translation,
-            residue_mask.astype(f32)[None],
-            chain_index.astype(f32)[None],
-            jnp.zeros((2, total), f32),
-        ],
-        0,
-    )
     prepared = pl.pallas_call(
         prepare_kernel,
         out_shape=(
@@ -546,25 +567,44 @@
             jax.ShapeDtypeStruct((rows, 16), f32),
             jax.ShapeDtypeStruct((rows, 16), f32),
         ),
-        in_specs=[smem, smem] + vmem(7) + [pl.BlockSpec(memory_space=pl.ANY)],
+        in_specs=[smem] + [hbm] * 12,
         out_specs=tuple(vmem(9)),
-        scratch_shapes=[pltpu.VMEM((HEADS * CH, CS), bf16), pltpu.SemaphoreType.DMA],
+        scratch_shapes=[
+            pltpu.SMEM((HEADS,), f32),
+            pltpu.VMEM(rotation.shape, f32),
+            pltpu.VMEM(translation.shape, f32),
+            pltpu.VMEM((1, total), jnp.int32),
+            pltpu.VMEM((1, total), jnp.int32),
+            pltpu.VMEM(node_embed.shape, bf16),
+            pltpu.VMEM(w_time.shape, bf16),
+            pltpu.VMEM(w_query.shape, bf16),
+            pltpu.VMEM(w_query_points.shape[::-1], bf16),
+            pltpu.VMEM(w_kv.shape, bf16),
+            pltpu.VMEM(w_kvp.shape[::-1], bf16),
+            pltpu.VMEM((HEADS * CH, CS), bf16),
+            pltpu.VMEM((16, total), f32),
+            pltpu.SemaphoreType.DMA((12,)),
+        ],
         compiler_params=params(24),
         cost_estimate=pl.CostEstimate(flops=2 * 10**9, bytes_accessed=8 * 10**6, transcendentals=0),
-    )(step_index, head_weights, node_embed, feats, w_time, w_query, w_query_points, w_kv, w_kvp, w_out)
+    )(
+        step_index,
+        *stay(
+            head_weights, rotation, translation, residue_mask[None], chain_index[None], node_embed, w_time,
+            w_query, w_query_points.T, w_kv, w_kvp.T, w_out,
+        )
+    )
     time, own, qk, qpts, w_mix, w_pts, kfeat, row_cols, key_cols = prepared
     partial = pl.pallas_call(
         attention_kernel,
         out_shape=jax.ShapeDtypeStruct((rows, CS), f32),
-        in_specs=[smem, smem] + vmem(16) + [pl.BlockSpec(memory_space=pl.ANY)],
+        in_specs=[smem, smem] + vmem(17),
         out_specs=pl.BlockSpec(memory_space=pltpu.VMEM),
         scratch_shapes=[
             pltpu.VMEM((4 * PAD, CS), bf16),
             pltpu.VMEM((HEADS * rows, 4 * PAD), f32),
             pltpu.VMEM((HEADS * rows, 2 * PAD), f32),
             pltpu.VMEM((HEADS * rows, CZ), f32),
-            pltpu.VMEM((w_out.shape[0] - HEADS * CH, CS), bf16),
-            pltpu.SemaphoreType.DMA,
         ],
         compiler_params=params(24),
     )(head_weights, chain_bias, own, *others, time, qk, qpts, w_mix, w_pts, kfeat, row_cols, bias, *biases, pair_embed, w_out)

time: 47.8 us -> 35.5 us (0.74)
  local copies, waits for them, and re-layouts: 12 us -> 0.06 us
  Pallas kernels: 11.9 us -> 14.2 us
  other arithmetic: 1.36 us -> 0 us
  waiting for transfers between devices: 7.88 us -> 6.69 us
    unnamed x35 -> x20, local copies, waits for them, and re-layouts: 10.6 us -> 0.06 us
    pallas_call x1, Pallas kernels: 2.48 us -> 4.19 us  [tile_body(): pl.pallas_call(prepare_kernel, out_shape=(jax.ShapeDtypeStruct((8, CS), f...]
    convert_element_type x2 -> x0, other arithmetic: 1.36 us -> none  [the longest x1 0.68 us: tile_body(): residue_mask.astype(f32)[None]]
    ppermute x1, starting transfers between devices: 2.65 us -> 3.8 us  [tile_body(): other = lax.ppermute(side, ('row', 'col'), turned)]
    ppermute x1, waiting for transfers between devices: 5.04 us -> 3.89 us  [tile_body(): other = lax.ppermute(side, ('row', 'col'), turned)]
    pallas_call x1, Pallas kernels: 0.49 us -> 1.55 us  [tile_body(): pl.pallas_call(bias_kernel, out_shape=jax.ShapeDtypeStruct((HEADS * rows...]
    ppermute x3, starting transfers between devices: 4.78 us -> 3.83 us  [tile_body(): lax.ppermute(node_embed, 'row', [(i, (i + k) % 4) for i in range(4)])]
    reshape x1 -> x0, local copies, waits for them, and re-layouts: 0.72 us -> none  [tile_body(): rotation.reshape(9, total)]
  transfers between devices with their start and end apart: 10 -> 10, of which waited for: 3 -> 3; matrix products, arithmetic and copies ran while one was open for 12% -> 0% of each run, Pallas kernels for 6% -> 16%
where the time goes in v2:
time: 35.5 us; the launch traced here: 35.3 us
  Pallas kernels  14.2 us (40%)
  starting transfers between devices  12.8 us (36%)
  waiting for transfers between devices  6.69 us (19%)
  between operations  1.5 us (4%)
    pallas_call x1, Pallas kernels, tile_body(): pl.pallas_call(prepare_kernel, out_shape=(jax.ShapeDtypeStruct((8, CS), f...  4.19 us
    pallas_call x1, Pallas kernels, tile_body(): pl.pallas_call(edge_kernel, out_shape=jax.ShapeDtypeStruct(pair_embed.sha...  3.98 us
    ppermute x1, waiting for transfers between devices, tile_body(): other = lax.ppermute(side, ('row', 'col'), turned)  3.89 us
    ppermute x3, starting transfers between devices, tile_body(): lax.ppermute(node_embed, 'row', [(i, (i + k) % 4) for i in range(4)])  3.83 us
    ppermute x1, starting transfers between devices, tile_body(): other = lax.ppermute(side, ('row', 'col'), turned)  3.8 us
    pallas_call x1, Pallas kernels, tile_body(): pl.pallas_call(attention_kernel, out_shape=jax.ShapeDtypeStruct((rows, CS...  3.29 us
    ppermute x3, starting transfers between devices, tile_body(): lax.ppermute(bias, 'col', [(i, i ^ k) for i in range(4)])  3 us
    ppermute x3, waiting for transfers between devices, tile_body(): lax.ppermute(partial, 'col', [(i, i ^ k) for i in range(4)])  2.78 us
  transfers between devices with their start and end apart: 10, of which 3 were waited for; matrix products, arithmetic and copies ran while one was open for 0% of the time, Pallas kernels for 16%

profile of v2, /device:TPU:3, one launch (start us, length us, event | category | flops | bytes accessed | tf_op | source)
XLA Modules:
  0.0 35.3 jit_solution(5856251000749691530)
XLA Ops:
  0.6 1.3 %collective-permute-start = (bf16[48,256]{1,0:T(8,128)(2,1)}, bf16[48,256]{1,0:T(8,128)(2,1)S(1)}, u32[]{:S(2)}, u32[]{:S(2)}) collective-permute-start(bf16[48,256]{1,0:T(8,128)(2,1)} %node_hbm.1), channel_id=1, source_target_pairs={{0,4},{4,8},{8,12},{12,0},{1,5},{5,9},{9,13},{13,1},{2,6},{6,10},{... | collective-permute-start | bytes 73736 | tf_op jit(solution)/shard_map/ppermute | solution.py:543
  2.0 2.1 %collective-permute-start.2 = (bf16[48,256]{1,0:T(8,128)(2,1)}, bf16[48,256]{1,0:T(8,128)(2,1)S(1)}, u32[]{:S(2)}, u32[]{:S(2)}) collective-permute-start(bf16[48,256]{1,0:T(8,128)(2,1)} %node_hbm.1), channel_id=1, source_target_pairs={{0,12},{4,0},{8,4},{12,8},{1,13},{5,1},{9,5},{13,9},{2,14},{6,2},{... | collective-permute-start | bytes 73736 | tf_op jit(solution)/shard_map/ppermute | solution.py:543
  4.1 0.4 %collective-permute-start.1 = (bf16[48,256]{1,0:T(8,128)(2,1)}, bf16[48,256]{1,0:T(8,128)(2,1)S(1)}, u32[]{:S(2)}, u32[]{:S(2)}) collective-permute-start(bf16[48,256]{1,0:T(8,128)(2,1)} %node_hbm.1), channel_id=1, source_target_pairs={{0,8},{4,12},{8,0},{12,4},{1,9},{5,13},{9,1},{13,5},{2,10},{6,14},... | collective-permute-start | bytes 73736 | tf_op jit(solution)/shard_map/ppermute | solution.py:543
  4.5 1.6 %shard_map.222.b0_ref = f32[192,128]{1,0:T(8,128)S(1)} custom-call(bf16[48,48,128]{2,1,0:T(8,128)(2,1)} %pair_ref.3, bf16[8,128]{1,0:T(8,128)(2,1)} %bitcast.5), custom_call_target="tpu_custom_call" | custom-call | tf_op jit(solution)/shard_map/pallas_call | solution.py:544
  6.0 1.7 %collective-permute-start.5 = (f32[192,128]{1,0:T(8,128)S(1)}, f32[192,128]{1,0:T(8,128)S(1)}, u32[]{:S(2)}, u32[]{:S(2)}) collective-permute-start(f32[192,128]{1,0:T(8,128)S(1)} %shard_map.222.b0_ref), channel_id=1, source_target_pairs={{0,3},{1,2},{2,1},{3,0},{4,7},{5,6},{6,5},{7,4},{8,11},{9,10},{10,... | collective-permute-start | bytes 294920 | tf_op jit(solution)/shard_map/ppermute | solution.py:556
  7.7 1.2 %collective-permute-start.4 = (f32[192,128]{1,0:T(8,128)S(1)}, f32[192,128]{1,0:T(8,128)S(1)}, u32[]{:S(2)}, u32[]{:S(2)}) collective-permute-start(f32[192,128]{1,0:T(8,128)S(1)} %shard_map.222.b0_ref), channel_id=1, source_target_pairs={{0,2},{1,3},{2,0},{3,1},{4,6},{5,7},{6,4},{7,5},{8,10},{9,11},{10,... | collective-permute-start | bytes 294920 | tf_op jit(solution)/shard_map/ppermute | solution.py:556
  9.6 0.0 collective-permute-done.n1_ref
  9.6 0.1 collective-permute-start.3
  9.7 0.0 copy-start
  9.7 0.0 copy-start.1
  9.7 0.0 copy-start.8
  9.7 0.0 copy-start.9
  9.7 4.2 %shard_map.221 = (f32[8,256]{1,0:T(8,128)S(1)}, bf16[48,256]{1,0:T(8,128)(2,1)S(1)}, bf16[384,256]{1,0:T(8,128)(2,1)S(1)}, f32[384,256]{1,0:T(8,128)S(1)}, bf16[...) custom-call(s32[1]{0:T(128)S(6)} %copy.24.step_ref, ...), custom_call_target="tpu_custom_call" | custom-call | flops 2000000000 | bytes 8000000 | tf_op jit(solution)/shard_map/pallas_call | solution.py:557
  13.9 0.0 collective-permute-done.2.n3_ref
  13.9 0.0 collective-permute-done.1.n2_ref
  14.0 0.0 collective-permute-done.5.b3_ref
  14.0 0.0 collective-permute-done.4.b2_ref
  14.0 0.0 collective-permute-done.3.b1_ref
  14.0 0.0 copy-done
  14.0 0.0 copy-done.1
  14.0 0.0 copy-done.8
  14.0 0.0 copy-done.9
  14.0 0.0 copy-start.4
  14.0 0.0 copy-start.5
  14.1 0.0 copy-start.7
  14.1 0.0 copy-start.2
  14.1 0.0 copy-start.3
  14.1 0.0 copy-start.6
  14.1 3.3 %shard_map.223.u0_ref = f32[48,256]{1,0:T(8,128)S(1)} custom-call(f32[8]{0:T(128)S(1)} %copy-done.8, f32[8]{0:T(128)S(1)} %copy-done.9, bf16[48,256]{1,0:T(8,128)(2,1)S(1)} %get-tuple-element.13.own_ref, bf16[48,256]{1,0:T(8,128)(2,1)S(1)} %collective-permute-done.n1_ref, bf16[48,256]{1,0:T(8,128)(2,1)S(1)} %collective-permute-done.1.n2_ref, ...), custom_call_target="tpu_custom_call" | custom-call | tf_op jit(solution)/shard_map/pallas_call | solution.py:598
  17.4 1.0 %collective-permute-start.8 = (f32[48,256]{1,0:T(8,128)S(1)}, f32[48,256]{1,0:T(8,128)S(1)}, u32[]{:S(2)}, u32[]{:S(2)}) collective-permute-start(f32[48,256]{1,0:T(8,128)S(1)} %shard_map.223.u0_ref), channel_id=1, source_target_pairs={{0,3},{1,2},{2,1},{3,0},{4,7},{5,6},{6,5},{7,4},{8,11},{9,10},{10,... | collective-permute-start | bytes 147464 | tf_op jit(solution)/shard_map/ppermute | solution.py:611
  18.4 0.9 %collective-permute-start.7 = (f32[48,256]{1,0:T(8,128)S(1)}, f32[48,256]{1,0:T(8,128)S(1)}, u32[]{:S(2)}, u32[]{:S(2)}) collective-permute-start(f32[48,256]{1,0:T(8,128)S(1)} %shard_map.223.u0_ref), channel_id=1, source_target_pairs={{0,2},{1,3},{2,0},{3,1},{4,6},{5,7},{6,4},{7,5},{8,10},{9,11},{10,... | collective-permute-start | bytes 147464 | tf_op jit(solution)/shard_map/ppermute | solution.py:611
  19.3 0.3 collective-permute-start.6
  19.6 1.9 %collective-permute-done.8.u3_ref = f32[48,256]{1,0:T(8,128)S(1)} collective-permute-done((f32[48,256]{1,0:T(8,128)S(1)}, f32[48,256]{1,0:T(8,128)S(1)}, u32[]{:S(2)}, u32[]{:S(2)}) %collective-permute-start.8) | collective-permute-done | bytes 49184 | tf_op jit(solution)/shard_map/ppermute | solution.py:611
  21.5 0.9 %collective-permute-done.7.u2_ref = f32[48,256]{1,0:T(8,128)S(1)} collective-permute-done((f32[48,256]{1,0:T(8,128)S(1)}, f32[48,256]{1,0:T(8,128)S(1)}, u32[]{:S(2)}, u32[]{:S(2)}) %collective-permute-start.7) | collective-permute-done | bytes 49184 | tf_op jit(solution)/shard_map/ppermute | solution.py:611
  22.4 0.0 collective-permute-done.6.u1_ref
  22.4 0.0 copy-done.4
  22.4 0.0 copy-done.5
  22.4 0.0 copy-done.7
  22.4 1.2 %shard_map.224 = (bf16[48,256]{1,0:T(8,128)(2,1)}, bf16[48,128]{1,0:T(8,128)(2,1)S(1)}) custom-call(f32[48,256]{1,0:T(8,128)S(1)} %shard_map.223.u0_ref, f32[48,256]{1,0:T(8,128)S(1)} %collective-permute-done.6.u1_ref, f32[48,256]{1,0:T(8,128)S(1)} %collective-permute-done.7.u2_ref, f32[48,256]{1,0:T(8,128)S(1)} %collective-permute-done.8.u3_ref, ...), custom_call_target="tpu_custom_call" | custom-call | tf_op jit(solution)/shard_map/pallas_call | solution.py:612
  23.6 3.8 %collective-permute-start.9 = (bf16[48,128]{1,0:T(8,128)(2,1)S(1)}, bf16[48,128]{1,0:T(8,128)(2,1)S(1)}, u32[]{:S(2)}, u32[]{:S(2)}) collective-permute-start(bf16[48,128]{1,0:T(8,128)(2,1)S(1)} %get-tuple-element.22.side_ref), channel_id=1, source_target_pairs={{0,0},{4,1},{8,2},{12,3},{1,4},{5,5},{9,6},{13,7},{2,8},{6,9},{10,... | collective-permute-start | bytes 36872 | tf_op jit(solution)/shard_map/ppermute | solution.py:620
  27.4 3.9 %collective-permute-done.9.other_ref = bf16[48,128]{1,0:T(8,128)(2,1)S(1)} collective-permute-done((bf16[48,128]{1,0:T(8,128)(2,1)S(1)}, bf16[48,128]{1,0:T(8,128)(2,1)S(1)}, u32[]{:S(2)}, u32[]{:S(2)}) %collective-permute-start.9) | collective-permute-done | bytes 12320 | tf_op jit(solution)/shard_map/ppermute | solution.py:620
  31.3 0.0 copy-done.2
  31.3 0.0 copy-done.3
  31.3 0.0 copy-done.6
  31.3 4.0 %shard_map.225 = bf16[48,48,128]{2,1,0:T(8,128)(2,1)} custom-call(bf16[48,128]{1,0:T(8,128)(2,1)S(1)} %get-tuple-element.22.side_ref, bf16[48,128]{1,0:T(8,128)(2,1)S(1)} %collective-permute-done.9.other_ref, f32[48,16]{1,0:T(8,128)S(1)} %get-tuple-element.20.rows_ref, f32[48,16]{1,0:T(8,128)S(1)} %get-tuple-element.23.keys_ref, ...), custom_call_target="tpu_custom_call" | custom-call | tf_op jit(solution)/shard_map/pallas_call | solution.py:621
Async XLA Ops:
  0.6 9.0 %collective-permute-start = (bf16[48,256]{1,0:T(8,128)(2,1)}, bf16[48,256]{1,0:T(8,128)(2,1)S(1)}, u32[]{:S(2)}, u32[]{:S(2)}) collective-permute-start(bf16[48,256]{1,0:T(8,128)(2,1)} %node_hbm.1), channel_id=1, source_target_pairs={{0,4},{4,8},{8,12},{12,0},{1,5},{5,9},{9,13},{13,1},{2,6},{6,10},{... | collective-permute-start | bytes 73736 | tf_op jit(solution)/shard_map/ppermute | solution.py:543
  2.0 12.0 %collective-permute-start.2 = (bf16[48,256]{1,0:T(8,128)(2,1)}, bf16[48,256]{1,0:T(8,128)(2,1)S(1)}, u32[]{:S(2)}, u32[]{:S(2)}) collective-permute-start(bf16[48,256]{1,0:T(8,128)(2,1)} %node_hbm.1), channel_id=1, source_target_pairs={{0,12},{4,0},{8,4},{12,8},{1,13},{5,1},{9,5},{13,9},{2,14},{6,2},{... | collective-permute-start | bytes 73736 | tf_op jit(solution)/shard_map/ppermute | solution.py:543
  4.1 9.9 %collective-permute-start.1 = (bf16[48,256]{1,0:T(8,128)(2,1)}, bf16[48,256]{1,0:T(8,128)(2,1)S(1)}, u32[]{:S(2)}, u32[]{:S(2)}) collective-permute-start(bf16[48,256]{1,0:T(8,128)(2,1)} %node_hbm.1), channel_id=1, source_target_pairs={{0,8},{4,12},{8,0},{12,4},{1,9},{5,13},{9,1},{13,5},{2,10},{6,14},... | collective-permute-start | bytes 73736 | tf_op jit(solution)/shard_map/ppermute | solution.py:543
  6.0 7.9 %collective-permute-start.5 = (f32[192,128]{1,0:T(8,128)S(1)}, f32[192,128]{1,0:T(8,128)S(1)}, u32[]{:S(2)}, u32[]{:S(2)}) collective-permute-start(f32[192,128]{1,0:T(8,128)S(1)} %shard_map.222.b0_ref), channel_id=1, source_target_pairs={{0,3},{1,2},{2,1},{3,0},{4,7},{5,6},{6,5},{7,4},{8,11},{9,10},{10,... | collective-permute-start | bytes 294920 | tf_op jit(solution)/shard_map/ppermute | solution.py:556
  7.7 6.2 %collective-permute-start.4 = (f32[192,128]{1,0:T(8,128)S(1)}, f32[192,128]{1,0:T(8,128)S(1)}, u32[]{:S(2)}, u32[]{:S(2)}) collective-permute-start(f32[192,128]{1,0:T(8,128)S(1)} %shard_map.222.b0_ref), channel_id=1, source_target_pairs={{0,2},{1,3},{2,0},{3,1},{4,6},{5,7},{6,4},{7,5},{8,10},{9,11},{10,... | collective-permute-start | bytes 294920 | tf_op jit(solution)/shard_map/ppermute | solution.py:556
  9.6 4.4 %collective-permute-start.3 = (f32[192,128]{1,0:T(8,128)S(1)}, f32[192,128]{1,0:T(8,128)S(1)}, u32[]{:S(2)}, u32[]{:S(2)}) collective-permute-start(f32[192,128]{1,0:T(8,128)S(1)} %shard_map.222.b0_ref), channel_id=1, source_target_pairs={{0,1},{1,0},{2,3},{3,2},{4,5},{5,4},{6,7},{7,6},{8,9},{9,8},{10,11... | collective-permute-start | bytes 294920 | tf_op jit(solution)/shard_map/ppermute | solution.py:556
  9.7 4.3 %copy-start = (bf16[48,48,128]{2,1,0:T(8,128)(2,1)S(1)}, bf16[48,48,128]{2,1,0:T(8,128)(2,1)}, u32[]{:S(2)}) copy-start(bf16[48,48,128]{2,1,0:T(8,128)(2,1)} %pair_ref.3) | copy-start | bytes 1769476
  9.7 4.3 %copy-start.1 = (bf16[3456,256]{1,0:T(8,128)(2,1)S(1)}, bf16[3456,256]{1,0:T(8,128)(2,1)}, u32[]{:S(2)}) copy-start(bf16[3456,256]{1,0:T(8,128)(2,1)} %w_out_ref.1) | copy-start | bytes 5308420
  9.7 4.3 %copy-start.8 = (f32[8]{0:T(128)S(1)}, f32[8]{0:T(128)}, u32[]{:S(2)}) copy-start(f32[8]{0:T(128)} %hw_ref.1) | copy-start | bytes 100
  9.7 4.3 %copy-start.9 = (f32[8]{0:T(128)S(1)}, f32[8]{0:T(128)}, u32[]{:S(2)}) copy-start(f32[8]{0:T(128)} %cb_ref.1) | copy-start | bytes 100
  14.0 8.4 %copy-start.4 = (bf16[256,256]{1,0:T(8,128)(2,1)S(1)}, bf16[256,256]{1,0:T(8,128)(2,1)}, u32[]{:S(2)}) copy-start(bf16[256,256]{1,0:T(8,128)(2,1)} %w_in_ref.2) | copy-start | bytes 393220
  14.0 8.3 %copy-start.5 = (bf16[256,256]{1,0:T(8,128)(2,1)S(1)}, bf16[256,256]{1,0:T(8,128)(2,1)}, u32[]{:S(2)}) copy-start(bf16[256,256]{1,0:T(8,128)(2,1)} %w_back_ref.1) | copy-start | bytes 393220
  14.1 8.3 %copy-start.7 = (bf16[256,128]{1,0:T(8,128)(2,1)S(1)}, bf16[256,128]{1,0:T(8,128)(2,1)}, u32[]{:S(2)}) copy-start(bf16[256,128]{1,0:T(8,128)(2,1)} %w_edge_ref.1) | copy-start | bytes 196612
  14.1 17.3 %copy-start.2 = (bf16[384,384]{1,0:T(8,128)(2,1)S(1)}, bf16[384,384]{1,0:T(8,128)(2,1)}, u32[]{:S(2)}) copy-start(bf16[384,384]{1,0:T(8,128)(2,1)} %w_in_ref.3) | copy-start | bytes 884740
  14.1 17.3 %copy-start.3 = (bf16[384,384]{1,0:T(8,128)(2,1)S(1)}, bf16[384,384]{1,0:T(8,128)(2,1)}, u32[]{:S(2)}) copy-start(bf16[384,384]{1,0:T(8,128)(2,1)} %w_mid_ref.1) | copy-start | bytes 884740
  14.1 17.2 %copy-start.6 = (bf16[384,128]{1,0:T(8,128)(2,1)S(1)}, bf16[384,128]{1,0:T(8,128)(2,1)}, u32[]{:S(2)}) copy-start(bf16[384,128]{1,0:T(8,128)(2,1)} %w_final_ref.1) | copy-start | bytes 294916
  17.4 4.1 %collective-permute-start.8 = (f32[48,256]{1,0:T(8,128)S(1)}, f32[48,256]{1,0:T(8,128)S(1)}, u32[]{:S(2)}, u32[]{:S(2)}) collective-permute-start(f32[48,256]{1,0:T(8,128)S(1)} %shard_map.223.u0_ref), channel_id=1, source_target_pairs={{0,3},{1,2},{2,1},{3,0},{4,7},{5,6},{6,5},{7,4},{8,11},{9,10},{10,... | collective-permute-start | bytes 147464 | tf_op jit(solution)/shard_map/ppermute | solution.py:611
  18.4 4.0 %collective-permute-start.7 = (f32[48,256]{1,0:T(8,128)S(1)}, f32[48,256]{1,0:T(8,128)S(1)}, u32[]{:S(2)}, u32[]{:S(2)}) collective-permute-start(f32[48,256]{1,0:T(8,128)S(1)} %shard_map.223.u0_ref), channel_id=1, source_target_pairs={{0,2},{1,3},{2,0},{3,1},{4,6},{5,7},{6,4},{7,5},{8,10},{9,11},{10,... | collective-permute-start | bytes 147464 | tf_op jit(solution)/shard_map/ppermute | solution.py:611
  19.3 3.1 %collective-permute-start.6 = (f32[48,256]{1,0:T(8,128)S(1)}, f32[48,256]{1,0:T(8,128)S(1)}, u32[]{:S(2)}, u32[]{:S(2)}) collective-permute-start(f32[48,256]{1,0:T(8,128)S(1)} %shard_map.223.u0_ref), channel_id=1, source_target_pairs={{0,1},{1,0},{2,3},{3,2},{4,5},{5,4},{6,7},{7,6},{8,9},{9,8},{10,11... | collective-permute-start | bytes 147464 | tf_op jit(solution)/shard_map/ppermute | solution.py:611
  23.6 7.7 %collective-permute-start.9 = (bf16[48,128]{1,0:T(8,128)(2,1)S(1)}, bf16[48,128]{1,0:T(8,128)(2,1)S(1)}, u32[]{:S(2)}, u32[]{:S(2)}) collective-permute-start(bf16[48,128]{1,0:T(8,128)(2,1)S(1)} %get-tuple-element.22.side_ref), channel_id=1, source_target_pairs={{0,0},{4,1},{8,2},{12,3},{1,4},{5,5},{9,6},{13,7},{2,8},{6,9},{10,... | collective-permute-start | bytes 36872 | tf_op jit(solution)/shard_map/ppermute | solution.py:620

commit v3 on v2

--- a/solution.py
+++ b/solution.py
@@ -3,6 +3,7 @@
 
 import jax
 import jax.numpy as jnp
+import numpy as np
 from jax import lax
 from jax.experimental import pallas as pl
 from jax.experimental.pallas import tpu as pltpu
@@ -278,16 +279,23 @@
 
 
 def bias_kernel(pair_hbm, w_hbm, out_ref, pair_ref, w_ref, sems):
-    copies = [pltpu.make_async_copy(pair_hbm, pair_ref, sems.at[0]), pltpu.make_async_copy(w_hbm, w_ref, sems.at[1])]
+    half = pair_ref.shape[0] // 2
+    part = half // 3
+    copies = [pltpu.make_async_copy(w_hbm, w_ref, sems.at[6])]
+    for n in range(3):
+        for m in range(2):
+            at = pl.ds(m * half + n * part, part)
+            copies.append(pltpu.make_async_copy(pair_hbm.at[at], pair_ref.at[at], sems.at[2 * n + m]))
     for copy in copies:
         copy.start()
-    for copy in copies:
-        copy.wait()
-    half = pair_ref.shape[0] // 2
+    copies[0].wait()
     keys = pair_ref.shape[1]
     weight = w_ref[...]
     gap = jnp.zeros((PAD - keys, CZ), bf16)
     for i in range(half):
+        if i % part == 0:
+            copies[1 + 2 * (i // part)].wait()
+            copies[2 + 2 * (i // part)].wait()
         both = jnp.concatenate([pair_ref[i], gap, pair_ref[i + half], gap], 0)
         out_ref[pl.ds(i, HEADS, stride=half), :] = dot(weight, both, NT) * GAIN
 
@@ -300,21 +308,20 @@
 
 def prepare_kernel(
     step_ref, hw_hbm, rotation_hbm, shift_hbm, mask_hbm, chain_hbm, node_hbm, w_time_hbm, w_query_hbm, w_qp_hbm, w_kv_hbm,
-    w_kvp_hbm, w_out_hbm,
-    time_ref, own_ref, qk_ref, qpts_ref, w_mix_ref, w_pts_ref, kfeat_ref, rows_ref, keys_ref,
+    w_kvp_hbm, order_hbm,
+    time_ref, own_ref, qk_ref, qpts_ref, w_pts_ref, kfeat_ref, rows_ref, keys_ref,
     hw_ref, rotation_ref, shift_ref, mask_ref, chain_ref, node_ref, w_time_ref, w_query_ref, w_qp_ref, w_kv_ref,
-    w_kvp_ref, w_head_ref, feats_ref, sems,
+    w_kvp_ref, order_ref, feats_ref, sems,
 ):
     pairs = (
         (rotation_hbm, rotation_ref), (shift_hbm, shift_ref), (mask_hbm, mask_ref),
         (chain_hbm, chain_ref), (node_hbm, node_ref), (w_time_hbm, w_time_ref), (hw_hbm, hw_ref), (w_qp_hbm, w_qp_ref),
-        (w_kvp_hbm, w_kvp_ref), (w_query_hbm, w_query_ref), (w_kv_hbm, w_kv_ref),
-        (w_out_hbm.at[pl.ds(0, HEADS * CH)], w_head_ref),
+        (w_kvp_hbm, w_kvp_ref), (order_hbm, order_ref), (w_query_hbm, w_query_ref), (w_kv_hbm.at[:, pl.ds(0, HEADS * CH)], w_kv_ref),
     )
     copies = [pltpu.make_async_copy(src, dst, sems.at[n]) for n, (src, dst) in enumerate(pairs)]
     for copy in copies:
         copy.start()
-    for copy in copies[:9]:
+    for copy in copies[:10]:
         copy.wait()
     rows = node_ref.shape[0]
     half = CS // 2
@@ -340,21 +347,12 @@
     def key_of(dst):
         part = dst // PAD
         inside = dst - part * PAD
-        return jnp.where(inside < rows, (part ^ col) * rows + inside, -1)
+        return jnp.where(inside < rows, part * rows + inside, -1)
 
     kfeat_ref[...] = dot(feats, one_hot((total, 4 * PAD), 0, key_of), precision=highest)
     own_cols = dot(one_hot((rows, total), 1, lambda d: d + row * rows), feats, NT, precision=highest)
     rows_ref[...] = own_cols
     keys_ref[...] = dot(one_hot((rows, total), 1, lambda d: d + col * rows), feats, NT, precision=highest)
-    for copy in copies[9:]:
-        copy.wait()
-    query = dot(own, w_query_ref[...]).astype(bf16)
-    for h in range(HEADS):
-        taken = dot(query[:, h * CH : (h + 1) * CH], w_kv_ref[:, h * CH : (h + 1) * CH], NT)
-        qk_ref[h * rows : (h + 1) * rows, :] = (taken * (GAIN / math.sqrt(CH))).astype(bf16)
-        w_mix_ref[h * CH : (h + 1) * CH, :] = dot(
-            w_kv_ref[:, (HEADS + h) * CH : (HEADS + h + 1) * CH], w_head_ref[h * CH : (h + 1) * CH, :]
-        ).astype(bf16)
     wide = HEADS * QP
     local = dot(own, w_qp_ref[...], NT)
     parts = [local[:, b * wide : (b + 1) * wide] for b in range(3)]
@@ -377,36 +375,35 @@
         mine = jnp.where((lanes % wide) // QP == h, points, 0.0)
         square = jnp.sum(mine * mine, 1, keepdims=True)
         qpts_ref[h * rows : (h + 1) * rows, :] = jnp.where(lanes == 3 * wide, -square, 2.0 * mine) * gain
-    width = w_kvp_ref.shape[0]
     group = HEADS * (QP + VP)
-    dst = lax.broadcasted_iota(jnp.int32, (width, width), 0)
-    src = lax.broadcasted_iota(jnp.int32, (width, width), 1)
-    comp = dst // group
-    inside = dst - comp * group
-    value = inside - HEADS * QP
-    from_key = (inside // QP) * (QP + VP) + inside % QP
-    from_value = (value // VP) * (QP + VP) + QP + value % VP
-    wanted = comp * group + jnp.where(inside < HEADS * QP, from_key, from_value)
-    order = (src == wanted).astype(f32).astype(bf16)
-    w_pts_ref[...] = dot(order, w_kvp_ref[...]).astype(bf16)
-
-
-def attention_kernel(
-    hw_ref, cb_ref, own_ref, n1_ref, n2_ref, n3_ref, time_ref, qk_ref, qpts_ref, w_mix_ref, w_pts_ref, kfeat_ref,
-    rows_ref, b0_ref, b1_ref, b2_ref, b3_ref, pair_ref, w_out_ref,
-    out_ref, x_ref, prob_ref, near_ref, opair_ref,
+    for a in range(3):
+        at = slice(a * group, (a + 1) * group)
+        w_pts_ref[at, :] = dot(order_ref[...], w_kvp_ref[at, :]).astype(bf16)
+    for copy in copies[10:]:
+        copy.wait()
+    query = dot(own, w_query_ref[...]).astype(bf16)
+    for h in range(HEADS):
+        taken = dot(query[:, h * CH : (h + 1) * CH], w_kv_ref[:, h * CH : (h + 1) * CH], NT)
+        qk_ref[h * rows : (h + 1) * rows, :] = (taken * (GAIN / math.sqrt(CH))).astype(bf16)
+
+
+def score_kernel(
+    hw_ref, cb_ref, own_ref, n1_ref, n2_ref, n3_ref, time_ref, qk_ref, qpts_ref, w_pts_ref, kfeat_ref, rows_ref,
+    b0_ref, b1_ref, b2_ref, b3_ref, pair_ref, w_out_ref,
+    out_ref, x_ref, prob_ref, vpts_ref, near_ref, opair_ref, bias_ref,
 ):
     rows = own_ref.shape[0]
     half = rows // 2
     row = lax.axis_index("row")
     col = lax.axis_index("col")
-    tail = HEADS * CH
     time = time_ref[0:1]
     x_ref[...] = jnp.zeros(x_ref.shape, bf16)
-    x_ref[pl.ds(pl.multiple_of((col ^ row) * PAD, PAD), rows), :] = own_ref[...]
+    x_ref[pl.ds(pl.multiple_of(row * PAD, PAD), rows), :] = own_ref[...]
     for k, ref in ((1, n1_ref), (2, n2_ref), (3, n3_ref)):
-        place = col ^ ((row + 4 - k) % 4)
+        place = (row + 4 - k) % 4
         x_ref[pl.ds(pl.multiple_of(place * PAD, PAD), rows), :] = (ref[...].astype(f32) + time).astype(bf16)
+    for k, ref in enumerate((b0_ref, b1_ref, b2_ref, b3_ref)):
+        bias_ref[col ^ k] = ref[...]
     x = x_ref[...]
     keys = x.shape[0]
     kfeat = kfeat_ref[...]
@@ -419,6 +416,8 @@
         for b in range(3):
             turned = turned + kfeat[3 * a + b : 3 * a + b + 1] * local[b * group : (b + 1) * group]
         points.append(turned)
+    empty = jnp.zeros((128 - HEADS * VP, keys), f32)
+    vpts_ref[...] = jnp.concatenate([part for p in points for part in (p[wide:], empty)], 0)
     key_points = [p[:wide] for p in points]
     cross = dot(qpts_ref[...], jnp.concatenate(key_points + [jnp.ones((wide, keys), f32)], 0), precision=highest)
     key_square = key_points[0] * key_points[0] + key_points[1] * key_points[1] + key_points[2] * key_points[2]
@@ -426,16 +425,15 @@
     lane = lax.broadcasted_iota(jnp.int32, (1, 128), 1)
     low = lane < PAD
     bias_low, bias_high = [], []
-    for left, right in ((b0_ref, b1_ref), (b2_ref, b3_ref)):
-        left, right = left[...], right[...]
+    for n in (0, 2):
+        left, right = bias_ref[n], bias_ref[n + 1]
         bias_low.append(jnp.where(low, left, pltpu.roll(right, PAD, 1)))
         bias_high.append(jnp.where(low, pltpu.roll(left, PAD, 1), right))
     bias_low = jnp.concatenate(bias_low, 1)
     bias_high = jnp.concatenate(bias_high, 1)
     key_lane = lax.broadcasted_iota(jnp.int32, (1, keys), 1)
     blocked = jnp.where(key_lane % PAD < rows, (kfeat[12:13] - 1.0) * masked_score, -1e30)
-    own_cols = rows_ref[...]
-    same = (own_cols[:, 13:14] == kfeat[13:14]).astype(f32)
+    same = (rows_ref[:, 13:14] == kfeat[13:14]).astype(f32)
     hw = jnp.zeros((1, 128), f32)
     for h in range(HEADS):
         hw = jnp.where(lane == h, hw_ref[h], hw)
@@ -451,15 +449,32 @@
         weight = jnp.exp(score - peak)
         weight = weight / jnp.sum(weight, 1, keepdims=True)
         prob_ref[at, :] = weight
-        near_ref[at, :] = weight[:, :128]
+        side = jnp.where(col >= 2, weight[:, 128:], weight[:, :128])
+        near_ref[at, :] = pltpu.roll(side, (col % 2) * PAD, 1)
+    own_keys = pair_ref.shape[1]
+    for i in range(rows):
+        weight = near_ref[pl.ds(i, HEADS, stride=rows), :][:, :own_keys].astype(bf16)
+        opair_ref[pl.ds(i, HEADS, stride=rows), :] = dot(weight, pair_ref[i])
+    tail = HEADS * CH + 4 * HEADS * VP
+    paired = jnp.concatenate([opair_ref[h * rows : (h + 1) * rows, :] for h in range(HEADS)], 1).astype(bf16)
+    out_ref[...] = dot(paired, w_out_ref[tail:]).astype(out_ref.dtype)
+
+
+def value_kernel(x_ref, prob_ref, vpts_ref, own_ref, rows_ref, w_kv_ref, w_out_ref, out_ref):
+    rows = own_ref.shape[0]
+    tail = HEADS * CH
+    own_cols = rows_ref[...]
     prob = prob_ref[...]
-    prob_low = prob.astype(bf16)
-    mixed = dot(prob_low, x).astype(bf16)
-    mixed = jnp.concatenate([mixed[h * rows : (h + 1) * rows] for h in range(HEADS)], 1)
-    update = dot(mixed, w_mix_ref[...])
-    empty = jnp.zeros((128 - HEADS * VP, keys), f32)
-    value_points = jnp.concatenate([x for p in points for x in (p[wide:], empty)], 0)
-    gathered = dot(prob, value_points, NT, precision=highest)
+    mixed = dot(prob.astype(bf16), x_ref[...]).astype(bf16)
+    attended = jnp.concatenate(
+        [
+            dot(mixed[h * rows : (h + 1) * rows], w_kv_ref[:, tail + h * CH : tail + (h + 1) * CH]).astype(bf16)
+            for h in range(HEADS)
+        ],
+        1,
+    )
+    update = own_ref[...].astype(f32) + dot(attended, w_out_ref[:tail])
+    gathered = dot(prob, vpts_ref[...], NT, precision=highest)
     spread = lax.broadcasted_iota(jnp.int32, (1, 3 * 128), 1) % 128 // VP
     kept = jnp.zeros((rows, 3 * 128), f32)
     for h in range(HEADS):
@@ -473,20 +488,15 @@
             + own_cols[:, 6 + b : 7 + b] * relative[2]
         )
     length = jnp.sqrt(jnp.maximum(framed[0] * framed[0] + framed[1] * framed[1] + framed[2] * framed[2], 1.0))
-    own_keys = pair_ref.shape[1]
-    for i in range(rows):
-        weight = near_ref[pl.ds(i, HEADS, stride=rows), :][:, :own_keys].astype(bf16)
-        opair_ref[pl.ds(i, HEADS, stride=rows), :] = dot(weight, pair_ref[i])
     span = HEADS * VP
     for n, part in enumerate(framed + [length]):
         update = update + dot(part[:, :span].astype(bf16), w_out_ref[tail + n * span : tail + (n + 1) * span])
-    paired = jnp.concatenate([opair_ref[h * rows : (h + 1) * rows, :] for h in range(HEADS)], 1).astype(bf16)
-    out_ref[...] = (0.25 * update + dot(paired, w_out_ref[tail + 4 * span :])).astype(out_ref.dtype)
-
-
-def node_kernel(u0_ref, u1_ref, u2_ref, u3_ref, own_ref, rows_ref, w_in_ref, w_back_ref, w_edge_ref, node_ref, side_ref):
+    out_ref[...] = update
+
+
+def node_kernel(u0_ref, u1_ref, u2_ref, u3_ref, base_ref, rows_ref, w_in_ref, w_back_ref, w_edge_ref, node_ref, side_ref):
     update = (u0_ref[...].astype(f32) + u1_ref[...].astype(f32)) + (u2_ref[...].astype(f32) + u3_ref[...].astype(f32))
-    normed = layer_norm(own_ref[...].astype(f32) + update).astype(bf16)
+    normed = layer_norm(base_ref[...] + update).astype(bf16)
     middle = jnp.maximum(dot(normed, w_in_ref[...]), 0.0).astype(bf16)
     node = layer_norm(normed.astype(f32) + dot(middle, w_back_ref[...]))
     node = (node * rows_ref[:, 12:13]).astype(bf16)
@@ -540,7 +550,6 @@
     total = residue_mask.shape[0]
     smem = pl.BlockSpec(memory_space=pltpu.SMEM)
     hbm = pl.BlockSpec(memory_space=pltpu.HBM)
-    others = [lax.ppermute(node_embed, "row", [(i, (i + k) % 4) for i in range(4)]) for k in (1, 2, 3)]
     bias = pl.pallas_call(
         bias_kernel,
         out_shape=jax.ShapeDtypeStruct((HEADS * rows // 2, 2 * PAD), f32),
@@ -549,11 +558,16 @@
         scratch_shapes=[
             pltpu.VMEM(pair_embed.shape, bf16),
             pltpu.VMEM((HEADS, CZ), bf16),
-            pltpu.SemaphoreType.DMA((2,)),
+            pltpu.SemaphoreType.DMA((7,)),
         ],
         compiler_params=params(16),
     )(*stay(pair_embed, w_bias.T))
-    biases = [lax.ppermute(bias, "col", [(i, i ^ k) for i in range(4)]) for k in (1, 2, 3)]
+    near, far = [lax.ppermute(bias, "col", [(i, i ^ k) for i in range(4)]) for k in (1, 2)]
+    others = [lax.ppermute(node_embed, "row", [(i, (i + k) % 4) for i in range(4)]) for k in (1, 2, 3)]
+    biases = [near, far, lax.ppermute(far, "col", [(i, i ^ 1) for i in range(4)])]
+    order = [h * (QP + VP) + n for h in range(HEADS) for n in range(QP)]
+    order += [h * (QP + VP) + QP + n for h in range(HEADS) for n in range(VP)]
+    order = jnp.asarray(np.eye(len(order), dtype=np.float32)[order], bf16)
     prepared = pl.pallas_call(
         prepare_kernel,
         out_shape=(
@@ -561,14 +575,13 @@
             jax.ShapeDtypeStruct((rows, CS), bf16),
             jax.ShapeDtypeStruct((HEADS * rows, CS), bf16),
             jax.ShapeDtypeStruct((HEADS * rows, 4 * HEADS * QP), f32),
-            jax.ShapeDtypeStruct((HEADS * CH, CS), bf16),
             jax.ShapeDtypeStruct((w_kvp.shape[1], CS), bf16),
             jax.ShapeDtypeStruct((16, 4 * PAD), f32),
             jax.ShapeDtypeStruct((rows, 16), f32),
             jax.ShapeDtypeStruct((rows, 16), f32),
         ),
         in_specs=[smem] + [hbm] * 12,
-        out_specs=tuple(vmem(9)),
+        out_specs=tuple(vmem(8)),
         scratch_shapes=[
             pltpu.SMEM((HEADS,), f32),
             pltpu.VMEM(rotation.shape, f32),
@@ -579,9 +592,9 @@
             pltpu.VMEM(w_time.shape, bf16),
             pltpu.VMEM(w_query.shape, bf16),
             pltpu.VMEM(w_query_points.shape[::-1], bf16),
-            pltpu.VMEM(w_kv.shape, bf16),
+            pltpu.VMEM((CS, HEADS * CH), bf16),
             pltpu.VMEM(w_kvp.shape[::-1], bf16),
-            pltpu.VMEM((HEADS * CH, CS), bf16),
+            pltpu.VMEM(order.shape, bf16),
             pltpu.VMEM((16, total), f32),
             pltpu.SemaphoreType.DMA((12,)),
         ],
@@ -591,23 +604,35 @@
         step_index,
         *stay(
             head_weights, rotation, translation, residue_mask[None], chain_index[None], node_embed, w_time,
-            w_query, w_query_points.T, w_kv, w_kvp.T, w_out,
-        )
-    )
-    time, own, qk, qpts, w_mix, w_pts, kfeat, row_cols, key_cols = prepared
-    partial = pl.pallas_call(
-        attention_kernel,
-        out_shape=jax.ShapeDtypeStruct((rows, CS), f32),
-        in_specs=[smem, smem] + vmem(17),
-        out_specs=pl.BlockSpec(memory_space=pltpu.VMEM),
+            w_query, w_query_points.T, w_kv, w_kvp.T, order,
+        )
+    )
+    time, own, qk, qpts, w_pts, kfeat, row_cols, key_cols = prepared
+    partial, x, prob, vpts = pl.pallas_call(
+        score_kernel,
+        out_shape=(
+            jax.ShapeDtypeStruct((rows, CS), bf16),
+            jax.ShapeDtypeStruct((4 * PAD, CS), bf16),
+            jax.ShapeDtypeStruct((HEADS * rows, 4 * PAD), f32),
+            jax.ShapeDtypeStruct((3 * 128, 4 * PAD), f32),
+        ),
+        in_specs=[smem, smem] + vmem(16),
+        out_specs=tuple(vmem(4)),
         scratch_shapes=[
-            pltpu.VMEM((4 * PAD, CS), bf16),
-            pltpu.VMEM((HEADS * rows, 4 * PAD), f32),
             pltpu.VMEM((HEADS * rows, 2 * PAD), f32),
             pltpu.VMEM((HEADS * rows, CZ), f32),
+            pltpu.VMEM((4,) + bias.shape, f32),
         ],
         compiler_params=params(24),
-    )(head_weights, chain_bias, own, *others, time, qk, qpts, w_mix, w_pts, kfeat, row_cols, bias, *biases, pair_embed, w_out)
+    )(head_weights, chain_bias, own, *others, time, qk, qpts, w_pts, kfeat, row_cols, bias, *biases, pair_embed, w_out)
+    base = pl.pallas_call(
+        value_kernel,
+        out_shape=jax.ShapeDtypeStruct((rows, CS), f32),
+        in_specs=vmem(7),
+        out_specs=pl.BlockSpec(memory_space=pltpu.VMEM),
+        compiler_params=params(24),
+        cost_estimate=pl.CostEstimate(flops=10**9, bytes_accessed=4 * 10**6, transcendentals=0),
+    )(x, prob, vpts, own, row_cols, w_kv, w_out)
     partials = [lax.ppermute(partial, "col", [(i, i ^ k) for i in range(4)]) for k in (1, 2, 3)]
     node_out, side = pl.pallas_call(
         node_kernel,
@@ -615,8 +640,11 @@
         in_specs=vmem(9),
         out_specs=tuple(vmem(2)),
         compiler_params=params(16),
-    )(partial, *partials, own, row_cols, w_mlp_in, w_mlp_out, w_edge_in)
-    turned = [(c * 4 + r, r * 4 + c) for r in range(4) for c in range(4)]
+    )(partial, *partials, base, row_cols, w_mlp_in, w_mlp_out, w_edge_in)
+    turned = []
+    for c in range(4):
+        far = sorted((r for r in range(4) if r != c), key=lambda r: -abs(r - c))
+        turned += [(4 * c + source, 4 * r + c) for r, source in zip([c] + far, (c, c ^ 1, c ^ 2, c ^ 3))]
     other = lax.ppermute(side, ("row", "col"), turned)
     pair_out = pl.pallas_call(
         edge_kernel,

time: 35.5 us -> 31.9 us (0.90)
  the two profiles are of different devices: /device:TPU:3 before, /device:TPU:16 now
where the time goes in v3:
time: 31.9 us; the launch traced here: 31.7 us
  Pallas kernels  13.9 us (44%)
  starting transfers between devices  11.9 us (37%)
  waiting for transfers between devices  4.39 us (14%)
  between operations  1.48 us (5%)
    ppermute x3, starting transfers between devices, tile_body(): lax.ppermute(node_embed, 'row', [(i, (i + k) % 4) for i in range(4)])  4.16 us
    pallas_call x1, Pallas kernels, tile_body(): pl.pallas_call(edge_kernel, out_shape=jax.ShapeDtypeStruct(pair_embed.sha...  3.95 us
    ppermute x1, starting transfers between devices, tile_body(): other = lax.ppermute(side, ('row', 'col'), turned)  3.7 us
    ppermute x1, waiting for transfers between devices, tile_body(): other = lax.ppermute(side, ('row', 'col'), turned)  3.66 us
    pallas_call x1, Pallas kernels, tile_body(): pl.pallas_call(prepare_kernel, out_shape=(jax.ShapeDtypeStruct((8, CS), f...  2.79 us
    pallas_call x1, Pallas kernels, tile_body(): pl.pallas_call(score_kernel, out_shape=(jax.ShapeDtypeStruct((rows, CS),...  2.78 us
    ppermute x3, starting transfers between devices, tile_body(): lax.ppermute(partial, 'col', [(i, i ^ k) for i in range(4)])  1.92 us
    pallas_call x1, Pallas kernels, tile_body(): pl.pallas_call(bias_kernel, out_shape=jax.ShapeDtypeStruct((HEADS * rows...  1.72 us
  transfers between devices with their start and end apart: 10, of which 2 were waited for; matrix products, arithmetic and copies ran while one was open for 0% of the time, Pallas kernels for 13%

profile of v3, /device:TPU:16, one launch (start us, length us, event | category | flops | bytes accessed | tf_op | source)
XLA Modules:
  0.0 31.7 jit_solution(2535273427267180618)
XLA Ops:
  0.6 1.7 %shard_map.231.b0_ref = f32[192,128]{1,0:T(8,128)S(1)} custom-call(bf16[48,48,128]{2,1,0:T(8,128)(2,1)} %pair_ref.3, bf16[8,128]{1,0:T(8,128)(2,1)} %bitcast.5), custom_call_target="tpu_custom_call" | custom-call | tf_op jit(solution)/shard_map/pallas_call | solution.py:553
  2.4 1.6 %collective-permute-start.4 = (f32[192,128]{1,0:T(8,128)S(1)}, f32[192,128]{1,0:T(8,128)S(1)}, u32[]{:S(2)}, u32[]{:S(2)}) collective-permute-start(f32[192,128]{1,0:T(8,128)S(1)} %shard_map.231.b0_ref), channel_id=1, source_target_pairs={{0,2},{1,3},{2,0},{3,1},{4,6},{5,7},{6,4},{7,5},{8,10},{9,11},{10,... | collective-permute-start | bytes 294920 | tf_op jit(solution)/shard_map/ppermute | solution.py:565
  3.9 1.6 %collective-permute-start = (bf16[48,256]{1,0:T(8,128)(2,1)}, bf16[48,256]{1,0:T(8,128)(2,1)S(1)}, u32[]{:S(2)}, u32[]{:S(2)}) collective-permute-start(bf16[48,256]{1,0:T(8,128)(2,1)} %node_hbm.1), channel_id=1, source_target_pairs={{0,4},{4,8},{8,12},{12,0},{1,5},{5,9},{9,13},{13,1},{2,6},{6,10},{... | collective-permute-start | bytes 73736 | tf_op jit(solution)/shard_map/ppermute | solution.py:566
  5.5 0.4 %collective-permute-start.2 = (bf16[48,256]{1,0:T(8,128)(2,1)}, bf16[48,256]{1,0:T(8,128)(2,1)S(1)}, u32[]{:S(2)}, u32[]{:S(2)}) collective-permute-start(bf16[48,256]{1,0:T(8,128)(2,1)} %node_hbm.1), channel_id=1, source_target_pairs={{0,12},{4,0},{8,4},{12,8},{1,13},{5,1},{9,5},{13,9},{2,14},{6,2},{... | collective-permute-start | bytes 73736 | tf_op jit(solution)/shard_map/ppermute | solution.py:566
  5.9 2.1 %collective-permute-start.1 = (bf16[48,256]{1,0:T(8,128)(2,1)}, bf16[48,256]{1,0:T(8,128)(2,1)S(1)}, u32[]{:S(2)}, u32[]{:S(2)}) collective-permute-start(bf16[48,256]{1,0:T(8,128)(2,1)} %node_hbm.1), channel_id=1, source_target_pairs={{0,8},{4,12},{8,0},{12,4},{1,9},{5,13},{9,1},{13,5},{2,10},{6,14},... | collective-permute-start | bytes 73736 | tf_op jit(solution)/shard_map/ppermute | solution.py:566
  8.1 0.0 collective-permute-start.3
  8.7 0.0 collective-permute-done.4.b2_ref
  8.7 0.6 %collective-permute-start.5 = (f32[192,128]{1,0:T(8,128)S(1)}, f32[192,128]{1,0:T(8,128)S(1)}, u32[]{:S(2)}, u32[]{:S(2)}) collective-permute-start(f32[192,128]{1,0:T(8,128)S(1)} %collective-permute-done.4.b2_ref), channel_id=1, source_target_pairs={{0,1},{1,0},{2,3},{3,2},{4,5},{5,4},{6,7},{7,6},{8,9},{9,8},{10,11... | collective-permute-start | bytes 294920 | tf_op jit(solution)/shard_map/ppermute | solution.py:567
  9.3 0.0 copy-start
  9.3 0.0 copy-start.1
  9.3 0.0 copy-start.9
  9.3 0.0 copy-start.10
  9.3 2.8 %shard_map.230 = (f32[8,256]{1,0:T(8,128)S(1)}, bf16[48,256]{1,0:T(8,128)(2,1)S(1)}, bf16[384,256]{1,0:T(8,128)(2,1)S(1)}, f32[384,256]{1,0:T(8,128)S(1)}, bf16[...) custom-call(s32[1]{0:T(128)S(6)} %copy.25.step_ref, f32[8]{0:T(128)} %hw_ref.1, ...), custom_call_target="tpu_custom_call" | custom-call | flops 2000000000 | bytes 8000000 | tf_op jit(solution)/shard_map/pallas_call | solution.py:571
  12.1 0.0 copy-start.2
  12.1 0.0 collective-permute-done.n1_ref
  12.1 0.0 collective-permute-done.2.n3_ref
  12.2 0.0 collective-permute-done.1.n2_ref
  12.2 0.0 collective-permute-done.3.b1_ref
  12.2 0.0 collective-permute-done.5.b3_ref
  12.2 0.0 copy-done
  12.2 0.0 copy-done.1
  12.2 0.0 copy-done.9
  12.2 0.0 copy-done.10
  12.2 2.8 %shard_map.232 = (bf16[48,256]{1,0:T(8,128)(2,1)S(1)}, bf16[256,256]{1,0:T(8,128)(2,1)S(1)}, f32[384,256]{1,0:T(8,128)S(1)}, f32[384,256]{1,0:T(8,128)S(1)}) custom-call(f32[8]{0:T(128)S(1)} %copy-done.9, f32[8]{0:T(128)S(1)} %copy-done.10, bf16[48,256]{1,0:T(8,128)(2,1)S(1)} %get-tuple-element.16.own_ref, bf16[48,256]{1,0:T(8,128)(2,1)S(1)} %collective-permute-done.n1_ref, ...), custom_call_target="tpu_custom_call" | custom-call | tf_op jit(solution)/shard_map/pallas_call | solution.py:611
  15.0 0.1 collective-permute-start.8
  15.1 1.7 %collective-permute-start.7 = (bf16[48,256]{1,0:T(8,128)(2,1)S(1)}, bf16[48,256]{1,0:T(8,128)(2,1)S(1)}, u32[]{:S(2)}, u32[]{:S(2)}) collective-permute-start(bf16[48,256]{1,0:T(8,128)(2,1)S(1)} %get-tuple-element.23.u0_ref), channel_id=1, source_target_pairs={{0,2},{1,3},{2,0},{3,1},{4,6},{5,7},{6,4},{7,5},{8,10},{9,11},{10,... | collective-permute-start | bytes 73736 | tf_op jit(solution)/shard_map/ppermute | solution.py:636
  16.8 0.2 collective-permute-start.6
  16.9 0.0 copy-done.2
  16.9 0.0 copy-start.5
  16.9 0.0 copy-start.6
  16.9 0.0 copy-start.8
  17.0 0.0 copy-start.3
  17.0 0.0 copy-start.4
  17.0 0.0 copy-start.7
  17.0 1.4 %shard_map.233.base_ref = f32[48,256]{1,0:T(8,128)S(1)} custom-call(bf16[256,256]{1,0:T(8,128)(2,1)S(1)} %get-tuple-element.24.x_ref, f32[384,256]{1,0:T(8,128)S(1)} %get-tuple-element.25.prob_ref, f32[384,256]{1,0:T(8,128)S(1)} %get-tuple-element.26.vpts_ref, bf16[48,256]{1,0:T(8,128)(2,1)S(1)} %get-tuple-element.16.own_ref, ...), custom_call_target="tpu_custom_call" | custom-call | flops 1000000000 | bytes 4000000 | tf_op jit(solution)/shard_map/pallas_call | solution.py:628
  18.4 0.0 collective-permute-done.8.u3_ref
  18.4 0.7 %collective-permute-done.7.u2_ref = bf16[48,256]{1,0:T(8,128)(2,1)S(1)} collective-permute-done((bf16[48,256]{1,0:T(8,128)(2,1)S(1)}, bf16[48,256]{1,0:T(8,128)(2,1)S(1)}, u32[]{:S(2)}, u32[]{:S(2)}) %collective-permute-start.7) | collective-permute-done | bytes 24608 | tf_op jit(solution)/shard_map/ppermute | solution.py:636
  19.1 0.0 collective-permute-done.6.u1_ref
  19.1 0.0 copy-done.5
  19.1 0.0 copy-done.6
  19.1 0.0 copy-done.8
  19.1 1.2 %shard_map.234 = (bf16[48,256]{1,0:T(8,128)(2,1)}, bf16[48,128]{1,0:T(8,128)(2,1)S(1)}) custom-call(bf16[48,256]{1,0:T(8,128)(2,1)S(1)} %get-tuple-element.23.u0_ref, bf16[48,256]{1,0:T(8,128)(2,1)S(1)} %collective-permute-done.6.u1_ref, bf16[48,256]{1,0:T(8,128)(2,1)S(1)} %collective-permute-done.7.u2_ref, ...), custom_call_target="tpu_custom_call" | custom-call | tf_op jit(solution)/shard_map/pallas_call | solution.py:637
  20.4 3.7 %collective-permute-start.9 = (bf16[48,128]{1,0:T(8,128)(2,1)S(1)}, bf16[48,128]{1,0:T(8,128)(2,1)S(1)}, u32[]{:S(2)}, u32[]{:S(2)}) collective-permute-start(bf16[48,128]{1,0:T(8,128)(2,1)S(1)} %get-tuple-element.28.side_ref), channel_id=1, source_target_pairs={{0,0},{1,12},{2,8},{3,4},{5,5},{4,13},{7,1},{6,9},{10,10},{11,2},{... | collective-permute-start | bytes 36872 | tf_op jit(solution)/shard_map/ppermute | solution.py:648
  24.1 3.7 %collective-permute-done.9.other_ref = bf16[48,128]{1,0:T(8,128)(2,1)S(1)} collective-permute-done((bf16[48,128]{1,0:T(8,128)(2,1)S(1)}, bf16[48,128]{1,0:T(8,128)(2,1)S(1)}, u32[]{:S(2)}, u32[]{:S(2)}) %collective-permute-start.9) | collective-permute-done | bytes 12320 | tf_op jit(solution)/shard_map/ppermute | solution.py:648
  27.7 0.0 copy-done.3
  27.7 0.0 copy-done.4
  27.7 0.0 copy-done.7
  27.8 4.0 %shard_map.235 = bf16[48,48,128]{2,1,0:T(8,128)(2,1)} custom-call(bf16[48,128]{1,0:T(8,128)(2,1)S(1)} %get-tuple-element.28.side_ref, bf16[48,128]{1,0:T(8,128)(2,1)S(1)} %collective-permute-done.9.other_ref, f32[48,16]{1,0:T(8,128)S(1)} %get-tuple-element.22.rows_ref, f32[48,16]{1,0:T(8,128)S(1)} %get-tuple-element.29.keys_ref, ...), custom_call_target="tpu_custom_call" | custom-call | tf_op jit(solution)/shard_map/pallas_call | solution.py:649
Async XLA Ops:
  2.4 6.4 %collective-permute-start.4 = (f32[192,128]{1,0:T(8,128)S(1)}, f32[192,128]{1,0:T(8,128)S(1)}, u32[]{:S(2)}, u32[]{:S(2)}) collective-permute-start(f32[192,128]{1,0:T(8,128)S(1)} %shard_map.231.b0_ref), channel_id=1, source_target_pairs={{0,2},{1,3},{2,0},{3,1},{4,6},{5,7},{6,4},{7,5},{8,10},{9,11},{10,... | collective-permute-start | bytes 294920 | tf_op jit(solution)/shard_map/ppermute | solution.py:565
  3.9 8.2 %collective-permute-start = (bf16[48,256]{1,0:T(8,128)(2,1)}, bf16[48,256]{1,0:T(8,128)(2,1)S(1)}, u32[]{:S(2)}, u32[]{:S(2)}) collective-permute-start(bf16[48,256]{1,0:T(8,128)(2,1)} %node_hbm.1), channel_id=1, source_target_pairs={{0,4},{4,8},{8,12},{12,0},{1,5},{5,9},{9,13},{13,1},{2,6},{6,10},{... | collective-permute-start | bytes 73736 | tf_op jit(solution)/shard_map/ppermute | solution.py:566
  5.5 6.7 %collective-permute-start.2 = (bf16[48,256]{1,0:T(8,128)(2,1)}, bf16[48,256]{1,0:T(8,128)(2,1)S(1)}, u32[]{:S(2)}, u32[]{:S(2)}) collective-permute-start(bf16[48,256]{1,0:T(8,128)(2,1)} %node_hbm.1), channel_id=1, source_target_pairs={{0,12},{4,0},{8,4},{12,8},{1,13},{5,1},{9,5},{13,9},{2,14},{6,2},{... | collective-permute-start | bytes 73736 | tf_op jit(solution)/shard_map/ppermute | solution.py:566
  5.9 6.2 %collective-permute-start.1 = (bf16[48,256]{1,0:T(8,128)(2,1)}, bf16[48,256]{1,0:T(8,128)(2,1)S(1)}, u32[]{:S(2)}, u32[]{:S(2)}) collective-permute-start(bf16[48,256]{1,0:T(8,128)(2,1)} %node_hbm.1), channel_id=1, source_target_pairs={{0,8},{4,12},{8,0},{12,4},{1,9},{5,13},{9,1},{13,5},{2,10},{6,14},... | collective-permute-start | bytes 73736 | tf_op jit(solution)/shard_map/ppermute | solution.py:566
  8.1 4.1 %collective-permute-start.3 = (f32[192,128]{1,0:T(8,128)S(1)}, f32[192,128]{1,0:T(8,128)S(1)}, u32[]{:S(2)}, u32[]{:S(2)}) collective-permute-start(f32[192,128]{1,0:T(8,128)S(1)} %shard_map.231.b0_ref), channel_id=1, source_target_pairs={{0,1},{1,0},{2,3},{3,2},{4,5},{5,4},{6,7},{7,6},{8,9},{9,8},{10,11... | collective-permute-start | bytes 294920 | tf_op jit(solution)/shard_map/ppermute | solution.py:565
  8.7 3.4 %collective-permute-start.5 = (f32[192,128]{1,0:T(8,128)S(1)}, f32[192,128]{1,0:T(8,128)S(1)}, u32[]{:S(2)}, u32[]{:S(2)}) collective-permute-start(f32[192,128]{1,0:T(8,128)S(1)} %collective-permute-done.4.b2_ref), channel_id=1, source_target_pairs={{0,1},{1,0},{2,3},{3,2},{4,5},{5,4},{6,7},{7,6},{8,9},{9,8},{10,11... | collective-permute-start | bytes 294920 | tf_op jit(solution)/shard_map/ppermute | solution.py:567
  9.3 2.9 %copy-start = (bf16[3456,256]{1,0:T(8,128)(2,1)S(1)}, bf16[3456,256]{1,0:T(8,128)(2,1)}, u32[]{:S(2)}) copy-start(bf16[3456,256]{1,0:T(8,128)(2,1)} %w_out_ref.3) | copy-start | bytes 5308420
  9.3 2.9 %copy-start.1 = (bf16[48,48,128]{2,1,0:T(8,128)(2,1)S(1)}, bf16[48,48,128]{2,1,0:T(8,128)(2,1)}, u32[]{:S(2)}) copy-start(bf16[48,48,128]{2,1,0:T(8,128)(2,1)} %pair_ref.3) | copy-start | bytes 1769476
  9.3 2.9 %copy-start.9 = (f32[8]{0:T(128)S(1)}, f32[8]{0:T(128)}, u32[]{:S(2)}) copy-start(f32[8]{0:T(128)} %hw_ref.1) | copy-start | bytes 100
  9.3 2.9 %copy-start.10 = (f32[8]{0:T(128)S(1)}, f32[8]{0:T(128)}, u32[]{:S(2)}) copy-start(f32[8]{0:T(128)} %cb_ref.1) | copy-start | bytes 100
  12.1 4.8 %copy-start.2 = (bf16[256,4096]{1,0:T(8,128)(2,1)S(1)}, bf16[256,4096]{1,0:T(8,128)(2,1)}, u32[]{:S(2)}) copy-start(bf16[256,4096]{1,0:T(8,128)(2,1)} %w_kv_ref.1) | copy-start | bytes 6291460
  15.0 3.4 %collective-permute-start.8 = (bf16[48,256]{1,0:T(8,128)(2,1)S(1)}, bf16[48,256]{1,0:T(8,128)(2,1)S(1)}, u32[]{:S(2)}, u32[]{:S(2)}) collective-permute-start(bf16[48,256]{1,0:T(8,128)(2,1)S(1)} %get-tuple-element.23.u0_ref), channel_id=1, source_target_pairs={{0,3},{1,2},{2,1},{3,0},{4,7},{5,6},{6,5},{7,4},{8,11},{9,10},{10,... | collective-permute-start | bytes 73736 | tf_op jit(solution)/shard_map/ppermute | solution.py:636
  15.1 4.0 %collective-permute-start.7 = (bf16[48,256]{1,0:T(8,128)(2,1)S(1)}, bf16[48,256]{1,0:T(8,128)(2,1)S(1)}, u32[]{:S(2)}, u32[]{:S(2)}) collective-permute-start(bf16[48,256]{1,0:T(8,128)(2,1)S(1)} %get-tuple-element.23.u0_ref), channel_id=1, source_target_pairs={{0,2},{1,3},{2,0},{3,1},{4,6},{5,7},{6,4},{7,5},{8,10},{9,11},{10,... | collective-permute-start | bytes 73736 | tf_op jit(solution)/shard_map/ppermute | solution.py:636
  16.8 2.4 %collective-permute-start.6 = (bf16[48,256]{1,0:T(8,128)(2,1)S(1)}, bf16[48,256]{1,0:T(8,128)(2,1)S(1)}, u32[]{:S(2)}, u32[]{:S(2)}) collective-permute-start(bf16[48,256]{1,0:T(8,128)(2,1)S(1)} %get-tuple-element.23.u0_ref), channel_id=1, source_target_pairs={{0,1},{1,0},{2,3},{3,2},{4,5},{5,4},{6,7},{7,6},{8,9},{9,8},{10,11... | collective-permute-start | bytes 73736 | tf_op jit(solution)/shard_map/ppermute | solution.py:636
  16.9 2.2 %copy-start.5 = (bf16[256,256]{1,0:T(8,128)(2,1)S(1)}, bf16[256,256]{1,0:T(8,128)(2,1)}, u32[]{:S(2)}) copy-start(bf16[256,256]{1,0:T(8,128)(2,1)} %w_in_ref.2) | copy-start | bytes 393220
  16.9 2.2 %copy-start.6 = (bf16[256,256]{1,0:T(8,128)(2,1)S(1)}, bf16[256,256]{1,0:T(8,128)(2,1)}, u32[]{:S(2)}) copy-start(bf16[256,256]{1,0:T(8,128)(2,1)} %w_back_ref.1) | copy-start | bytes 393220
  16.9 2.2 %copy-start.8 = (bf16[256,128]{1,0:T(8,128)(2,1)S(1)}, bf16[256,128]{1,0:T(8,128)(2,1)}, u32[]{:S(2)}) copy-start(bf16[256,128]{1,0:T(8,128)(2,1)} %w_edge_ref.1) | copy-start | bytes 196612
  17.0 10.8 %copy-start.3 = (bf16[384,384]{1,0:T(8,128)(2,1)S(1)}, bf16[384,384]{1,0:T(8,128)(2,1)}, u32[]{:S(2)}) copy-start(bf16[384,384]{1,0:T(8,128)(2,1)} %w_in_ref.3) | copy-start | bytes 884740
  17.0 10.8 %copy-start.4 = (bf16[384,384]{1,0:T(8,128)(2,1)S(1)}, bf16[384,384]{1,0:T(8,128)(2,1)}, u32[]{:S(2)}) copy-start(bf16[384,384]{1,0:T(8,128)(2,1)} %w_mid_ref.1) | copy-start | bytes 884740
  17.0 10.8 %copy-start.7 = (bf16[384,128]{1,0:T(8,128)(2,1)S(1)}, bf16[384,128]{1,0:T(8,128)(2,1)}, u32[]{:S(2)}) copy-start(bf16[384,128]{1,0:T(8,128)(2,1)} %w_final_ref.1) | copy-start | bytes 294916
  20.4 7.4 %collective-permute-start.9 = (bf16[48,128]{1,0:T(8,128)(2,1)S(1)}, bf16[48,128]{1,0:T(8,128)(2,1)S(1)}, u32[]{:S(2)}, u32[]{:S(2)}) collective-permute-start(bf16[48,128]{1,0:T(8,128)(2,1)S(1)} %get-tuple-element.28.side_ref), channel_id=1, source_target_pairs={{0,0},{1,12},{2,8},{3,4},{5,5},{4,13},{7,1},{6,9},{10,10},{11,2},{... | collective-permute-start | bytes 36872 | tf_op jit(solution)/shard_map/ppermute | solution.py:648

commit v4 on v3

--- a/solution.py
+++ b/solution.py
@@ -278,26 +278,31 @@
     return [pltpu.with_memory_space_constraint(array, pltpu.HBM) for array in arrays]
 
 
-def bias_kernel(pair_hbm, w_hbm, out_ref, pair_ref, w_ref, sems):
+def bias_kernel(*refs):
+    count = (len(refs) - 6) // 2
+    pair_hbm, w_hbm, *held_hbm = refs[: 2 + count]
+    out_ref, *held_refs, pair_ref, w_ref, sems = refs[2 + count :]
     half = pair_ref.shape[0] // 2
-    part = half // 3
-    copies = [pltpu.make_async_copy(w_hbm, w_ref, sems.at[6])]
-    for n in range(3):
-        for m in range(2):
-            at = pl.ds(m * half + n * part, part)
-            copies.append(pltpu.make_async_copy(pair_hbm.at[at], pair_ref.at[at], sems.at[2 * n + m]))
+    copies = [pltpu.make_async_copy(w_hbm, w_ref, sems.at[2])]
+    for m in range(2):
+        at = pl.ds(m * half, half)
+        copies.append(pltpu.make_async_copy(pair_hbm.at[at], pair_ref.at[at], sems.at[m]))
+    for n, (src, dst) in enumerate(zip(held_hbm, held_refs)):
+        if src.shape != dst.shape:
+            src = src.at[:, pl.ds(0, dst.shape[1])]
+        copies.append(pltpu.make_async_copy(src, dst, sems.at[3 + n]))
     for copy in copies:
         copy.start()
-    copies[0].wait()
+    for copy in copies[:3]:
+        copy.wait()
     keys = pair_ref.shape[1]
     weight = w_ref[...]
     gap = jnp.zeros((PAD - keys, CZ), bf16)
     for i in range(half):
-        if i % part == 0:
-            copies[1 + 2 * (i // part)].wait()
-            copies[2 + 2 * (i // part)].wait()
         both = jnp.concatenate([pair_ref[i], gap, pair_ref[i + half], gap], 0)
         out_ref[pl.ds(i, HEADS, stride=half), :] = dot(weight, both, NT) * GAIN
+    for copy in copies[3:]:
+        copy.wait()
 
 
 def one_hot(shape, source_dim, offset_of):
@@ -307,22 +312,10 @@
 
 
 def prepare_kernel(
-    step_ref, hw_hbm, rotation_hbm, shift_hbm, mask_hbm, chain_hbm, node_hbm, w_time_hbm, w_query_hbm, w_qp_hbm, w_kv_hbm,
-    w_kvp_hbm, order_hbm,
-    time_ref, own_ref, qk_ref, qpts_ref, w_pts_ref, kfeat_ref, rows_ref, keys_ref,
-    hw_ref, rotation_ref, shift_ref, mask_ref, chain_ref, node_ref, w_time_ref, w_query_ref, w_qp_ref, w_kv_ref,
-    w_kvp_ref, order_ref, feats_ref, sems,
+    step_ref, hw_ref, rotation_ref, shift_ref, mask_ref, chain_ref, node_ref, w_time_ref, w_qp_ref, w_kvp_ref, order_ref,
+    w_query_ref, w_kv_ref,
+    time_ref, own_ref, qk_ref, qpts_ref, w_pts_ref, kfeat_ref, rows_ref, keys_ref, feats_ref,
 ):
-    pairs = (
-        (rotation_hbm, rotation_ref), (shift_hbm, shift_ref), (mask_hbm, mask_ref),
-        (chain_hbm, chain_ref), (node_hbm, node_ref), (w_time_hbm, w_time_ref), (hw_hbm, hw_ref), (w_qp_hbm, w_qp_ref),
-        (w_kvp_hbm, w_kvp_ref), (order_hbm, order_ref), (w_query_hbm, w_query_ref), (w_kv_hbm.at[:, pl.ds(0, HEADS * CH)], w_kv_ref),
-    )
-    copies = [pltpu.make_async_copy(src, dst, sems.at[n]) for n, (src, dst) in enumerate(pairs)]
-    for copy in copies:
-        copy.start()
-    for copy in copies[:10]:
-        copy.wait()
     rows = node_ref.shape[0]
     half = CS // 2
     row = lax.axis_index("row")
@@ -364,10 +357,7 @@
         points.append(turned)
     points = jnp.concatenate(points + [jnp.zeros((rows, wide), f32)], 1)
     lanes = lax.broadcasted_iota(jnp.int32, (1, 4 * wide), 1)
-    head_lane = lax.broadcasted_iota(jnp.int32, (1, 128), 1)
-    hw = jnp.zeros((1, 128), f32)
-    for h in range(HEADS):
-        hw = jnp.where(head_lane == h, hw_ref[h], hw)
+    hw = hw_ref[...]
     gains = GAIN * POINT * 0.5 * (jnp.maximum(hw, 0.0) + jnp.log1p(jnp.exp(-jnp.abs(hw))))
     rows_ref[...] = own_cols
     for h in range(HEADS):
@@ -379,8 +369,6 @@
     for a in range(3):
         at = slice(a * group, (a + 1) * group)
         w_pts_ref[at, :] = dot(order_ref[...], w_kvp_ref[at, :]).astype(bf16)
-    for copy in copies[10:]:
-        copy.wait()
     query = dot(own, w_query_ref[...]).astype(bf16)
     for h in range(HEADS):
         taken = dot(query[:, h * CH : (h + 1) * CH], w_kv_ref[:, h * CH : (h + 1) * CH], NT)
@@ -399,8 +387,8 @@
     time = time_ref[0:1]
     x_ref[...] = jnp.zeros(x_ref.shape, bf16)
     x_ref[pl.ds(pl.multiple_of(row * PAD, PAD), rows), :] = own_ref[...]
-    for k, ref in ((1, n1_ref), (2, n2_ref), (3, n3_ref)):
-        place = (row + 4 - k) % 4
+    for k, ref in ((2 + col % 2, n1_ref), (3 - col % 2, n2_ref), (1, n3_ref)):
+        place = row ^ k
         x_ref[pl.ds(pl.multiple_of(place * PAD, PAD), rows), :] = (ref[...].astype(f32) + time).astype(bf16)
     for k, ref in enumerate((b0_ref, b1_ref, b2_ref, b3_ref)):
         bias_ref[col ^ k] = ref[...]
@@ -504,41 +492,42 @@
     side_ref[...] = dot(node, w_edge_ref[...]).astype(bf16)
 
 
-def edge_kernel(side_ref, other_ref, rows_ref, keys_ref, pair_ref, w_in_ref, w_mid_ref, w_final_ref, out_ref):
+def edge_kernel(
+    side_ref, other_ref, rows_ref, keys_ref, pair_ref, w_in_ref, w_mid_ref, w_final_ref, out_hbm, out_ref, sems
+):
     rows, keys = pair_ref.shape[:2]
-    step = 8
-    w_in = w_in_ref[...]
-    side = side_ref[...]
-    other = other_ref[...]
-    pre_rows = dot(side, w_in[CZ : CZ + NH])
-    pre_keys = dot(other, w_in[CZ + NH :])
-    side = side.astype(f32)
-    other = other.astype(f32)
+    step = math.gcd(rows, 16)
+    pre_rows = dot(side_ref[...], w_in_ref[CZ : CZ + NH])
+    pre_keys = dot(other_ref[...], w_in_ref[CZ + NH :])
+    side = side_ref[...].astype(f32)
+    other = other_ref[...].astype(f32)
     keep_rows = rows_ref[:, 12:13]
     keep_keys = keys_ref[:, 12:13]
+    copies = []
     for begin in range(0, rows, step):
+        parts = [(begin + n, slice(n * keys, (n + 1) * keys)) for n in range(step)]
         pair = pair_ref[begin : begin + step].reshape(step * keys, CZ)
-        lifted = dot(pair, w_in[:CZ])
+        lifted = dot(pair, w_in_ref[:CZ])
         first = jnp.concatenate(
-            [
-                jnp.maximum(lifted[n * keys : (n + 1) * keys] + (pre_keys + pre_rows[begin + n : begin + n + 1]), 0.0).astype(bf16)
-                for n in range(step)
-            ],
-            0,
+            [jnp.maximum(lifted[at] + (pre_keys + pre_rows[i : i + 1]), 0.0).astype(bf16) for i, at in parts], 0
         )
         second = jnp.maximum(dot(first, w_mid_ref[...]), 0.0)
-        stacked = jnp.concatenate(
+        joined = jnp.concatenate(
             [
-                pair.astype(f32),
-                jnp.concatenate([jnp.broadcast_to(side[begin + n : begin + n + 1], (keys, NH)) for n in range(step)], 0),
-                jnp.concatenate([other] * step, 0),
+                (second[:, :CZ] + pair.astype(f32)).astype(bf16),
+                jnp.concatenate([(second[at, CZ : CZ + NH] + side[i : i + 1]).astype(bf16) for i, at in parts], 0),
+                jnp.concatenate([(second[at, CZ + NH :] + other).astype(bf16) for i, at in parts], 0),
             ],
             1,
         )
-        edge = layer_norm(dot((second + stacked).astype(bf16), w_final_ref[...]))
-        for n in range(step):
-            keep = keep_keys * keep_rows[begin + n : begin + n + 1]
-            out_ref[begin + n] = (edge[n * keys : (n + 1) * keys] * keep).astype(bf16)
+        edge = layer_norm(dot(joined, w_final_ref[...]))
+        for i, at in parts:
+            out_ref[i] = (edge[at] * (keep_keys * keep_rows[i : i + 1])).astype(bf16)
+        done = pl.ds(begin, step)
+        copies.append(pltpu.make_async_copy(out_ref.at[done], out_hbm.at[done], sems.at[begin // step]))
+        copies[-1].start()
+    for copy in copies:
+        copy.wait()
 
 
 def tile_body(
@@ -550,24 +539,33 @@
     total = residue_mask.shape[0]
     smem = pl.BlockSpec(memory_space=pltpu.SMEM)
     hbm = pl.BlockSpec(memory_space=pltpu.HBM)
-    bias = pl.pallas_call(
+    order = [h * (QP + VP) + n for h in range(HEADS) for n in range(QP)]
+    order += [h * (QP + VP) + QP + n for h in range(HEADS) for n in range(VP)]
+    order = jnp.asarray(np.eye(len(order), dtype=np.float32)[order], bf16)
+    held = (
+        head_weights[None], rotation, translation, residue_mask[None], chain_index[None], node_embed, w_time,
+        w_query_points.T, w_kvp.T, order, w_query, w_kv,
+    )
+    shapes = [jax.ShapeDtypeStruct(array.shape, array.dtype) for array in held]
+    shapes[-1] = jax.ShapeDtypeStruct((CS, HEADS * CH), bf16)
+    bias, *held = pl.pallas_call(
         bias_kernel,
-        out_shape=jax.ShapeDtypeStruct((HEADS * rows // 2, 2 * PAD), f32),
-        in_specs=[hbm, hbm],
-        out_specs=pl.BlockSpec(memory_space=pltpu.VMEM),
+        out_shape=[jax.ShapeDtypeStruct((HEADS * rows // 2, 2 * PAD), f32)] + shapes,
+        in_specs=[hbm] * (2 + len(held)),
+        out_specs=vmem(1 + len(held)),
         scratch_shapes=[
             pltpu.VMEM(pair_embed.shape, bf16),
             pltpu.VMEM((HEADS, CZ), bf16),
-            pltpu.SemaphoreType.DMA((7,)),
+            pltpu.SemaphoreType.DMA((3 + len(held),)),
         ],
         compiler_params=params(16),
-    )(*stay(pair_embed, w_bias.T))
+    )(*stay(pair_embed, w_bias.T, *held))
     near, far = [lax.ppermute(bias, "col", [(i, i ^ k) for i in range(4)]) for k in (1, 2)]
-    others = [lax.ppermute(node_embed, "row", [(i, (i + k) % 4) for i in range(4)]) for k in (1, 2, 3)]
+    apart = [(4 * r + c, 4 * (r ^ (2 + c % 2)) + c) for r in range(4) for c in range(4)]
+    fetched = lax.ppermute(node_embed, ("row", "col"), apart)
+    beside = lax.ppermute(node_embed, "row", [(i, i ^ 1) for i in range(4)])
+    others = [fetched, lax.ppermute(fetched, "col", [(i, i ^ 1) for i in range(4)]), beside]
     biases = [near, far, lax.ppermute(far, "col", [(i, i ^ 1) for i in range(4)])]
-    order = [h * (QP + VP) + n for h in range(HEADS) for n in range(QP)]
-    order += [h * (QP + VP) + QP + n for h in range(HEADS) for n in range(VP)]
-    order = jnp.asarray(np.eye(len(order), dtype=np.float32)[order], bf16)
     prepared = pl.pallas_call(
         prepare_kernel,
         out_shape=(
@@ -580,33 +578,12 @@
             jax.ShapeDtypeStruct((rows, 16), f32),
             jax.ShapeDtypeStruct((rows, 16), f32),
         ),
-        in_specs=[smem] + [hbm] * 12,
+        in_specs=[smem] + vmem(12),
         out_specs=tuple(vmem(8)),
-        scratch_shapes=[
-            pltpu.SMEM((HEADS,), f32),
-            pltpu.VMEM(rotation.shape, f32),
-            pltpu.VMEM(translation.shape, f32),
-            pltpu.VMEM((1, total), jnp.int32),
-            pltpu.VMEM((1, total), jnp.int32),
-            pltpu.VMEM(node_embed.shape, bf16),
-            pltpu.VMEM(w_time.shape, bf16),
-            pltpu.VMEM(w_query.shape, bf16),
-            pltpu.VMEM(w_query_points.shape[::-1], bf16),
-            pltpu.VMEM((CS, HEADS * CH), bf16),
-            pltpu.VMEM(w_kvp.shape[::-1], bf16),
-            pltpu.VMEM(order.shape, bf16),
-            pltpu.VMEM((16, total), f32),
-            pltpu.SemaphoreType.DMA((12,)),
-        ],
-        compiler_params=params(24),
+        scratch_shapes=[pltpu.VMEM((16, total), f32)],
+        compiler_params=params(16),
         cost_estimate=pl.CostEstimate(flops=2 * 10**9, bytes_accessed=8 * 10**6, transcendentals=0),
-    )(
-        step_index,
-        *stay(
-            head_weights, rotation, translation, residue_mask[None], chain_index[None], node_embed, w_time,
-            w_query, w_query_points.T, w_kv, w_kvp.T, order,
-        )
-    )
+    )(step_index, *held)
     time, own, qk, qpts, w_pts, kfeat, row_cols, key_cols = prepared
     partial, x, prob, vpts = pl.pallas_call(
         score_kernel,
@@ -650,7 +627,8 @@
         edge_kernel,
         out_shape=jax.ShapeDtypeStruct(pair_embed.shape, bf16),
         in_specs=vmem(8),
-        out_specs=pl.BlockSpec(memory_space=pltpu.VMEM),
+        out_specs=hbm,
+        scratch_shapes=[pltpu.VMEM(pair_embed.shape, bf16), pltpu.SemaphoreType.DMA((rows // math.gcd(rows, 16),))],
         compiler_params=params(24),
     )(side, other, row_cols, key_cols, pair_embed, w_trunk_in, w_trunk_mid, w_final)
     return node_out, pair_out

time: 31.9 us -> 30.4 us (0.953)
  the two profiles are of different devices: /device:TPU:16 before, /device:TPU:3 now
where the time goes in v4:
time: 30.4 us; the launch traced here: 29.8 us
  Pallas kernels  11.6 us (38%)
  starting transfers between devices  11.3 us (37%)
  waiting for transfers between devices  4.86 us (16%)
  between operations  1.45 us (5%)
  local copies, waits for them, and re-layouts  0.57 us (2%)
    ppermute x1, starting transfers between devices, tile_body(): fetched = lax.ppermute(node_embed, ('row', 'col'), apart)  3.56 us
    ppermute x1, starting transfers between devices, tile_body(): other = lax.ppermute(side, ('row', 'col'), turned)  3.4 us
    ppermute x1, waiting for transfers between devices, tile_body(): other = lax.ppermute(side, ('row', 'col'), turned)  3.39 us
    pallas_call x1, Pallas kernels, tile_body(): pl.pallas_call(edge_kernel, out_shape=jax.ShapeDtypeStruct(pair_embed.sha...  3.22 us
    pallas_call x1, Pallas kernels, tile_body(): pl.pallas_call(score_kernel, out_shape=(jax.ShapeDtypeStruct((rows, CS),...  2.76 us
    ppermute x3, starting transfers between devices, tile_body(): lax.ppermute(partial, 'col', [(i, i ^ k) for i in range(4)])  2.21 us
    pallas_call x1, Pallas kernels, tile_body(): pl.pallas_call(bias_kernel, out_shape=[jax.ShapeDtypeStruct((HEADS * rows...  2.14 us
    pallas_call x1, Pallas kernels, tile_body(): pl.pallas_call(value_kernel, out_shape=jax.ShapeDtypeStruct((rows, CS), f...  1.4 us
  transfers between devices with their start and end apart: 10, of which 3 were waited for; matrix products, arithmetic and copies ran while one was open for 0% of the time, Pallas kernels for 8%

profile of v4, /device:TPU:3, one launch (start us, length us, event | category | flops | bytes accessed | tf_op | source)
XLA Modules:
  0.0 29.8 jit_solution(11147651181254946464)
XLA Ops:
  0.6 0.0 copy-start.11
  0.6 2.1 %shard_map.230 = (f32[192,128]{1,0:T(8,128)S(1)}, f32[1,8]{1,0:T(1,128)S(1)}, f32[3,3,192]{2,1,0:T(4,128)S(1)}, f32[3,192]{1,0:T(4,128)S(1)}, s32[1,192]{1,0:T(1...) custom-call(bf16[48,48,128]{2,1,0:T(8,128)(2,1)} %pair_ref.3, ...), custom_call_target="tpu_custom_call" | custom-call | tf_op jit(solution)/shard_map/pallas_call | solution.py:551
  2.8 0.1 collective-permute-start.4
  2.9 0.0 copy-done.11
  2.9 3.6 %collective-permute-start = (bf16[48,256]{1,0:T(8,128)(2,1)S(1)}, bf16[48,256]{1,0:T(8,128)(2,1)S(1)}, u32[]{:S(2)}, u32[]{:S(2)}) collective-permute-start(bf16[48,256]{1,0:T(8,128)(2,1)S(1)} %copy-done.11), channel_id=1, source_target_pairs={{0,8},{1,13},{2,10},{3,15},{4,12},{5,9},{6,14},{7,11},{8,0},{9,5},... | collective-permute-start | bytes 73736 | tf_op jit(solution)/shard_map/ppermute | solution.py:565
  6.4 0.2 collective-permute-start.3
  6.7 1.3 %collective-permute-start.2 = (bf16[48,256]{1,0:T(8,128)(2,1)S(1)}, bf16[48,256]{1,0:T(8,128)(2,1)S(1)}, u32[]{:S(2)}, u32[]{:S(2)}) collective-permute-start(bf16[48,256]{1,0:T(8,128)(2,1)S(1)} %copy-done.11), channel_id=1, source_target_pairs={{0,4},{4,0},{8,12},{12,8},{1,5},{5,1},{9,13},{13,9},{2,6},{6,2},{1... | collective-permute-start | bytes 73736 | tf_op jit(solution)/shard_map/ppermute | solution.py:566
  8.6 0.0 collective-permute-done.n1_ref
  8.6 0.3 %collective-permute-start.1 = (bf16[48,256]{1,0:T(8,128)(2,1)S(1)}, bf16[48,256]{1,0:T(8,128)(2,1)S(1)}, u32[]{:S(2)}, u32[]{:S(2)}) collective-permute-start(bf16[48,256]{1,0:T(8,128)(2,1)S(1)} %collective-permute-done.n1_ref), channel_id=1, source_target_pairs={{0,1},{1,0},{2,3},{3,2},{4,5},{5,4},{6,7},{7,6},{8,9},{9,8},{10,11... | collective-permute-start | bytes 73736 | tf_op jit(solution)/shard_map/ppermute | solution.py:567
  9.0 0.0 collective-permute-done.4.b2_ref
  9.0 0.2 collective-permute-start.5
  9.2 0.0 copy-start.1
  9.2 0.0 copy-start.2
  9.2 0.0 copy-start.9
  9.2 0.0 copy-start.10
  9.2 0.9 %shard_map.231 = (f32[8,256]{1,0:T(8,128)S(1)}, bf16[48,256]{1,0:T(8,128)(2,1)S(1)}, bf16[384,256]{1,0:T(8,128)(2,1)S(1)}, f32[384,256]{1,0:T(8,128)S(1)}, bf16[...) custom-call(s32[1]{0:T(128)S(6)} %copy.25.step_ref, ...), custom_call_target="tpu_custom_call" | custom-call | flops 2000000000 | bytes 8000000 | tf_op jit(solution)/shard_map/pallas_call | solution.py:569
  10.1 0.0 copy-start
  10.1 0.0 collective-permute-done.2.n3_ref
  10.1 0.0 collective-permute-done.1.n2_ref
  10.1 0.0 collective-permute-done.3.b1_ref
  10.1 0.1 collective-permute-done.5.b3_ref
  10.3 0.4 %copy-done.1 = bf16[3456,256]{1,0:T(8,128)(2,1)S(1)} copy-done((bf16[3456,256]{1,0:T(8,128)(2,1)S(1)}, bf16[3456,256]{1,0:T(8,128)(2,1)}, u32[]{:S(2)}) %copy-start.1) | copy-done | bytes 1769496
  10.7 0.1 copy-done.2
  10.8 0.0 copy-done.9
  10.8 0.0 copy-done.10
  10.8 2.8 %shard_map.232 = (bf16[48,256]{1,0:T(8,128)(2,1)S(1)}, bf16[256,256]{1,0:T(8,128)(2,1)S(1)}, f32[384,256]{1,0:T(8,128)S(1)}, f32[384,256]{1,0:T(8,128)S(1)}) custom-call(f32[8]{0:T(128)S(1)} %copy-done.9, f32[8]{0:T(128)S(1)} %copy-done.10, bf16[48,256]{1,0:T(8,128)(2,1)S(1)} %get-tuple-element.41.own_ref, bf16[48,256]{1,0:T(8,128)(2,1)S(1)} %collective-permute-done.n1_ref, ...), custom_call_target="tpu_custom_call" | custom-call | tf_op jit(solution)/shard_map/pallas_call | solution.py:588
  13.6 0.3 %collective-permute-start.6 = (bf16[48,256]{1,0:T(8,128)(2,1)S(1)}, bf16[48,256]{1,0:T(8,128)(2,1)S(1)}, u32[]{:S(2)}, u32[]{:S(2)}) collective-permute-start(bf16[48,256]{1,0:T(8,128)(2,1)S(1)} %get-tuple-element.49.u0_ref), channel_id=1, source_target_pairs={{0,1},{1,0},{2,3},{3,2},{4,5},{5,4},{6,7},{7,6},{8,9},{9,8},{10,11... | collective-permute-start | bytes 73736 | tf_op jit(solution)/shard_map/ppermute | solution.py:613
  13.9 1.2 %collective-permute-start.7 = (bf16[48,256]{1,0:T(8,128)(2,1)S(1)}, bf16[48,256]{1,0:T(8,128)(2,1)S(1)}, u32[]{:S(2)}, u32[]{:S(2)}) collective-permute-start(bf16[48,256]{1,0:T(8,128)(2,1)S(1)} %get-tuple-element.49.u0_ref), channel_id=1, source_target_pairs={{0,2},{1,3},{2,0},{3,1},{4,6},{5,7},{6,4},{7,5},{8,10},{9,11},{10,... | collective-permute-start | bytes 73736 | tf_op jit(solution)/shard_map/ppermute | solution.py:613
  15.1 0.6 %collective-permute-start.8 = (bf16[48,256]{1,0:T(8,128)(2,1)S(1)}, bf16[48,256]{1,0:T(8,128)(2,1)S(1)}, u32[]{:S(2)}, u32[]{:S(2)}) collective-permute-start(bf16[48,256]{1,0:T(8,128)(2,1)S(1)} %get-tuple-element.49.u0_ref), channel_id=1, source_target_pairs={{0,3},{1,2},{2,1},{3,0},{4,7},{5,6},{6,5},{7,4},{8,11},{9,10},{10,... | collective-permute-start | bytes 73736 | tf_op jit(solution)/shard_map/ppermute | solution.py:613
  15.8 0.0 copy-done
  15.8 0.0 copy-start.5
  15.8 0.0 copy-start.3
  15.8 0.0 copy-start.4
  15.8 0.0 copy-start.7
  15.8 1.4 %shard_map.233.base_ref = f32[48,256]{1,0:T(8,128)S(1)} custom-call(bf16[256,256]{1,0:T(8,128)(2,1)S(1)} %get-tuple-element.50.x_ref, f32[384,256]{1,0:T(8,128)S(1)} %get-tuple-element.51.prob_ref, f32[384,256]{1,0:T(8,128)S(1)} %get-tuple-element.52.vpts_ref, bf16[48,256]{1,0:T(8,128)(2,1)S(1)} %get-tuple-element.41.own_ref, ...), custom_call_target="tpu_custom_call" | custom-call | flops 1000000000 | bytes 4000000 | tf_op jit(solution)/shard_map/pallas_call | solution.py:605
  17.2 0.0 collective-permute-done.6.u1_ref
  17.2 0.0 collective-permute-done.7.u2_ref
  17.3 1.3 %collective-permute-done.8.u3_ref = bf16[48,256]{1,0:T(8,128)(2,1)S(1)} collective-permute-done((bf16[48,256]{1,0:T(8,128)(2,1)S(1)}, bf16[48,256]{1,0:T(8,128)(2,1)S(1)}, u32[]{:S(2)}, u32[]{:S(2)}) %collective-permute-start.8) | collective-permute-done | bytes 24608 | tf_op jit(solution)/shard_map/ppermute | solution.py:613
  18.6 0.0 copy-done.5
  18.6 0.0 copy-done.6
  18.6 0.0 copy-done.8
  18.6 1.2 %shard_map.234 = (bf16[48,256]{1,0:T(8,128)(2,1)}, bf16[48,128]{1,0:T(8,128)(2,1)S(1)}) custom-call(bf16[48,256]{1,0:T(8,128)(2,1)S(1)} %get-tuple-element.49.u0_ref, bf16[48,256]{1,0:T(8,128)(2,1)S(1)} %collective-permute-done.6.u1_ref, bf16[48,256]{1,0:T(8,128)(2,1)S(1)} %collective-permute-done.7.u2_ref, ...), custom_call_target="tpu_custom_call" | custom-call | tf_op jit(solution)/shard_map/pallas_call | solution.py:614
  19.8 3.4 %collective-permute-start.9 = (bf16[48,128]{1,0:T(8,128)(2,1)S(1)}, bf16[48,128]{1,0:T(8,128)(2,1)S(1)}, u32[]{:S(2)}, u32[]{:S(2)}) collective-permute-start(bf16[48,128]{1,0:T(8,128)(2,1)S(1)} %get-tuple-element.54.side_ref), channel_id=1, source_target_pairs={{0,0},{1,12},{2,8},{3,4},{5,5},{4,13},{7,1},{6,9},{10,10},{11,2},{... | collective-permute-start | bytes 36872 | tf_op jit(solution)/shard_map/ppermute | solution.py:625
  23.2 3.4 %collective-permute-done.9.other_ref = bf16[48,128]{1,0:T(8,128)(2,1)S(1)} collective-permute-done((bf16[48,128]{1,0:T(8,128)(2,1)S(1)}, bf16[48,128]{1,0:T(8,128)(2,1)S(1)}, u32[]{:S(2)}, u32[]{:S(2)}) %collective-permute-start.9) | collective-permute-done | bytes 12320 | tf_op jit(solution)/shard_map/ppermute | solution.py:625
  26.6 0.0 copy-done.3
  26.6 0.0 copy-done.4
  26.6 0.0 copy-done.7
  26.6 3.2 %shard_map.235 = bf16[48,48,128]{2,1,0:T(8,128)(2,1)} custom-call(bf16[48,128]{1,0:T(8,128)(2,1)S(1)} %get-tuple-element.54.side_ref, bf16[48,128]{1,0:T(8,128)(2,1)S(1)} %collective-permute-done.9.other_ref, f32[48,16]{1,0:T(8,128)S(1)} %get-tuple-element.47.rows_ref, f32[48,16]{1,0:T(8,128)S(1)} %get-tuple-element.55.keys_ref, ...), custom_call_target="tpu_custom_call" | custom-call | tf_op jit(solution)/shard_map/pallas_call | solution.py:626
  (2 shorter events, 0.0 us)
Async XLA Ops:
  0.6 2.2 %copy-start.11 = (bf16[48,256]{1,0:T(8,128)(2,1)S(1)}, bf16[48,256]{1,0:T(8,128)(2,1)}, u32[]{:S(2)}) copy-start(bf16[48,256]{1,0:T(8,128)(2,1)} %refs_7_.1) | copy-start | bytes 73732
  2.8 6.2 %collective-permute-start.4 = (f32[192,128]{1,0:T(8,128)S(1)}, f32[192,128]{1,0:T(8,128)S(1)}, u32[]{:S(2)}, u32[]{:S(2)}) collective-permute-start(f32[192,128]{1,0:T(8,128)S(1)} %get-tuple-element.48.b0_ref), channel_id=1, source_target_pairs={{0,2},{1,3},{2,0},{3,1},{4,6},{5,7},{6,4},{7,5},{8,10},{9,11},{10,... | collective-permute-start | bytes 294920 | tf_op jit(solution)/shard_map/ppermute | solution.py:563
  2.9 5.7 %collective-permute-start = (bf16[48,256]{1,0:T(8,128)(2,1)S(1)}, bf16[48,256]{1,0:T(8,128)(2,1)S(1)}, u32[]{:S(2)}, u32[]{:S(2)}) collective-permute-start(bf16[48,256]{1,0:T(8,128)(2,1)S(1)} %copy-done.11), channel_id=1, source_target_pairs={{0,8},{1,13},{2,10},{3,15},{4,12},{5,9},{6,14},{7,11},{8,0},{9,5},... | collective-permute-start | bytes 73736 | tf_op jit(solution)/shard_map/ppermute | solution.py:565
  6.4 3.7 %collective-permute-start.3 = (f32[192,128]{1,0:T(8,128)S(1)}, f32[192,128]{1,0:T(8,128)S(1)}, u32[]{:S(2)}, u32[]{:S(2)}) collective-permute-start(f32[192,128]{1,0:T(8,128)S(1)} %get-tuple-element.48.b0_ref), channel_id=1, source_target_pairs={{0,1},{1,0},{2,3},{3,2},{4,5},{5,4},{6,7},{7,6},{8,9},{9,8},{10,11... | collective-permute-start | bytes 294920 | tf_op jit(solution)/shard_map/ppermute | solution.py:563
  6.7 3.5 %collective-permute-start.2 = (bf16[48,256]{1,0:T(8,128)(2,1)S(1)}, bf16[48,256]{1,0:T(8,128)(2,1)S(1)}, u32[]{:S(2)}, u32[]{:S(2)}) collective-permute-start(bf16[48,256]{1,0:T(8,128)(2,1)S(1)} %copy-done.11), channel_id=1, source_target_pairs={{0,4},{4,0},{8,12},{12,8},{1,5},{5,1},{9,13},{13,9},{2,6},{6,2},{1... | collective-permute-start | bytes 73736 | tf_op jit(solution)/shard_map/ppermute | solution.py:566
  8.6 1.5 %collective-permute-start.1 = (bf16[48,256]{1,0:T(8,128)(2,1)S(1)}, bf16[48,256]{1,0:T(8,128)(2,1)S(1)}, u32[]{:S(2)}, u32[]{:S(2)}) collective-permute-start(bf16[48,256]{1,0:T(8,128)(2,1)S(1)} %collective-permute-done.n1_ref), channel_id=1, source_target_pairs={{0,1},{1,0},{2,3},{3,2},{4,5},{5,4},{6,7},{7,6},{8,9},{9,8},{10,11... | collective-permute-start | bytes 73736 | tf_op jit(solution)/shard_map/ppermute | solution.py:567
  9.0 1.3 %collective-permute-start.5 = (f32[192,128]{1,0:T(8,128)S(1)}, f32[192,128]{1,0:T(8,128)S(1)}, u32[]{:S(2)}, u32[]{:S(2)}) collective-permute-start(f32[192,128]{1,0:T(8,128)S(1)} %collective-permute-done.4.b2_ref), channel_id=1, source_target_pairs={{0,1},{1,0},{2,3},{3,2},{4,5},{5,4},{6,7},{7,6},{8,9},{9,8},{10,11... | collective-permute-start | bytes 294920 | tf_op jit(solution)/shard_map/ppermute | solution.py:568
  9.2 1.5 %copy-start.1 = (bf16[3456,256]{1,0:T(8,128)(2,1)S(1)}, bf16[3456,256]{1,0:T(8,128)(2,1)}, u32[]{:S(2)}) copy-start(bf16[3456,256]{1,0:T(8,128)(2,1)} %w_out_ref.3) | copy-start | bytes 5308420
  9.2 1.6 %copy-start.2 = (bf16[48,48,128]{2,1,0:T(8,128)(2,1)S(1)}, bf16[48,48,128]{2,1,0:T(8,128)(2,1)}, u32[]{:S(2)}) copy-start(bf16[48,48,128]{2,1,0:T(8,128)(2,1)} %pair_ref.3) | copy-start | bytes 1769476
  9.2 1.6 %copy-start.9 = (f32[8]{0:T(128)S(1)}, f32[8]{0:T(128)}, u32[]{:S(2)}) copy-start(f32[8]{0:T(128)} %hw_ref.1) | copy-start | bytes 100
  9.2 1.6 %copy-start.10 = (f32[8]{0:T(128)S(1)}, f32[8]{0:T(128)}, u32[]{:S(2)}) copy-start(f32[8]{0:T(128)} %cb_ref.1) | copy-start | bytes 100
  10.1 5.7 %copy-start = (bf16[256,4096]{1,0:T(8,128)(2,1)S(1)}, bf16[256,4096]{1,0:T(8,128)(2,1)}, u32[]{:S(2)}) copy-start(bf16[256,4096]{1,0:T(8,128)(2,1)} %w_kv_ref.1) | copy-start | bytes 6291460
  13.6 3.7 %collective-permute-start.6 = (bf16[48,256]{1,0:T(8,128)(2,1)S(1)}, bf16[48,256]{1,0:T(8,128)(2,1)S(1)}, u32[]{:S(2)}, u32[]{:S(2)}) collective-permute-start(bf16[48,256]{1,0:T(8,128)(2,1)S(1)} %get-tuple-element.49.u0_ref), channel_id=1, source_target_pairs={{0,1},{1,0},{2,3},{3,2},{4,5},{5,4},{6,7},{7,6},{8,9},{9,8},{10,11... | collective-permute-start | bytes 73736 | tf_op jit(solution)/shard_map/ppermute | solution.py:613
  13.9 3.3 %collective-permute-start.7 = (bf16[48,256]{1,0:T(8,128)(2,1)S(1)}, bf16[48,256]{1,0:T(8,128)(2,1)S(1)}, u32[]{:S(2)}, u32[]{:S(2)}) collective-permute-start(bf16[48,256]{1,0:T(8,128)(2,1)S(1)} %get-tuple-element.49.u0_ref), channel_id=1, source_target_pairs={{0,2},{1,3},{2,0},{3,1},{4,6},{5,7},{6,4},{7,5},{8,10},{9,11},{10,... | collective-permute-start | bytes 73736 | tf_op jit(solution)/shard_map/ppermute | solution.py:613
  15.1 3.4 %collective-permute-start.8 = (bf16[48,256]{1,0:T(8,128)(2,1)S(1)}, bf16[48,256]{1,0:T(8,128)(2,1)S(1)}, u32[]{:S(2)}, u32[]{:S(2)}) collective-permute-start(bf16[48,256]{1,0:T(8,128)(2,1)S(1)} %get-tuple-element.49.u0_ref), channel_id=1, source_target_pairs={{0,3},{1,2},{2,1},{3,0},{4,7},{5,6},{6,5},{7,4},{8,11},{9,10},{10,... | collective-permute-start | bytes 73736 | tf_op jit(solution)/shard_map/ppermute | solution.py:613
  15.8 2.8 %copy-start.5 = (bf16[256,256]{1,0:T(8,128)(2,1)S(1)}, bf16[256,256]{1,0:T(8,128)(2,1)}, u32[]{:S(2)}) copy-start(bf16[256,256]{1,0:T(8,128)(2,1)} %w_in_ref.2) | copy-start | bytes 393220
  15.8 2.8 %copy-start.6 = (bf16[256,256]{1,0:T(8,128)(2,1)S(1)}, bf16[256,256]{1,0:T(8,128)(2,1)}, u32[]{:S(2)}) copy-start(bf16[256,256]{1,0:T(8,128)(2,1)} %w_back_ref.1) | copy-start | bytes 393220
  15.8 2.8 %copy-start.8 = (bf16[256,128]{1,0:T(8,128)(2,1)S(1)}, bf16[256,128]{1,0:T(8,128)(2,1)}, u32[]{:S(2)}) copy-start(bf16[256,128]{1,0:T(8,128)(2,1)} %w_edge_ref.1) | copy-start | bytes 196612
  15.8 10.8 %copy-start.3 = (bf16[384,384]{1,0:T(8,128)(2,1)S(1)}, bf16[384,384]{1,0:T(8,128)(2,1)}, u32[]{:S(2)}) copy-start(bf16[384,384]{1,0:T(8,128)(2,1)} %w_in_ref.3) | copy-start | bytes 884740
  15.8 10.8 %copy-start.4 = (bf16[384,384]{1,0:T(8,128)(2,1)S(1)}, bf16[384,384]{1,0:T(8,128)(2,1)}, u32[]{:S(2)}) copy-start(bf16[384,384]{1,0:T(8,128)(2,1)} %w_mid_ref.1) | copy-start | bytes 884740
  15.8 10.8 %copy-start.7 = (bf16[384,128]{1,0:T(8,128)(2,1)S(1)}, bf16[384,128]{1,0:T(8,128)(2,1)}, u32[]{:S(2)}) copy-start(bf16[384,128]{1,0:T(8,128)(2,1)} %w_final_ref.1) | copy-start | bytes 294916
  19.8 6.8 %collective-permute-start.9 = (bf16[48,128]{1,0:T(8,128)(2,1)S(1)}, bf16[48,128]{1,0:T(8,128)(2,1)S(1)}, u32[]{:S(2)}, u32[]{:S(2)}) collective-permute-start(bf16[48,128]{1,0:T(8,128)(2,1)S(1)} %get-tuple-element.54.side_ref), channel_id=1, source_target_pairs={{0,0},{1,12},{2,8},{3,4},{5,5},{4,13},{7,1},{6,9},{10,10},{11,2},{... | collective-permute-start | bytes 36872 | tf_op jit(solution)/shard_map/ppermute | solution.py:625

commit v5 on v4

--- a/solution.py
+++ b/solution.py
@@ -312,9 +312,9 @@
 
 
 def prepare_kernel(
-    step_ref, hw_ref, rotation_ref, shift_ref, mask_ref, chain_ref, node_ref, w_time_ref, w_qp_ref, w_kvp_ref, order_ref,
+    step_ref, hw_ref, cb_ref, rotation_ref, shift_ref, mask_ref, chain_ref, node_ref, w_time_ref, w_qp_ref, w_kvp_ref, order_ref,
     w_query_ref, w_kv_ref,
-    time_ref, own_ref, qk_ref, qpts_ref, w_pts_ref, kfeat_ref, rows_ref, keys_ref, feats_ref,
+    time_ref, own_ref, qk_ref, qpts_ref, w_pts_ref, kfeat_ref, rows_ref, keys_ref, heads_ref, feats_ref,
 ):
     rows = node_ref.shape[0]
     half = CS // 2
@@ -359,12 +359,16 @@
     lanes = lax.broadcasted_iota(jnp.int32, (1, 4 * wide), 1)
     hw = hw_ref[...]
     gains = GAIN * POINT * 0.5 * (jnp.maximum(hw, 0.0) + jnp.log1p(jnp.exp(-jnp.abs(hw))))
-    rows_ref[...] = own_cols
+    heads_ref[0:1, :] = gains
+    heads_ref[1:2, :] = GAIN * cb_ref[...]
     for h in range(HEADS):
         gain = gains[:, h : h + 1]
         mine = jnp.where((lanes % wide) // QP == h, points, 0.0)
         square = jnp.sum(mine * mine, 1, keepdims=True)
-        qpts_ref[h * rows : (h + 1) * rows, :] = jnp.where(lanes == 3 * wide, -square, 2.0 * mine) * gain
+        mine = jnp.where(lanes == 3 * wide, -square, 2.0 * mine) * gain
+        high = mine.astype(bf16)
+        qpts_ref[0, h * rows : (h + 1) * rows, :] = high
+        qpts_ref[1, h * rows : (h + 1) * rows, :] = (mine - high.astype(f32)).astype(bf16)
     group = HEADS * (QP + VP)
     for a in range(3):
         at = slice(a * group, (a + 1) * group)
@@ -376,10 +380,13 @@
 
 
 def score_kernel(
-    hw_ref, cb_ref, own_ref, n1_ref, n2_ref, n3_ref, time_ref, qk_ref, qpts_ref, w_pts_ref, kfeat_ref, rows_ref,
+    heads_ref, own_ref, n1_ref, n2_ref, n3_ref, time_ref, qk_ref, qpts_ref, w_pts_ref, kfeat_ref, rows_ref,
     b0_ref, b1_ref, b2_ref, b3_ref, pair_ref, w_out_ref,
-    out_ref, x_ref, prob_ref, vpts_ref, near_ref, opair_ref, bias_ref,
+    out_ref, x_ref, prob_ref, vpts_ref, near_ref, opair_ref, bias_ref, w_tail_ref, sem,
 ):
+    tail = HEADS * CH + 4 * HEADS * VP
+    copy = pltpu.make_async_copy(w_out_ref.at[pl.ds(tail, HEADS * CZ)], w_tail_ref, sem)
+    copy.start()
     rows = own_ref.shape[0]
     half = rows // 2
     row = lax.axis_index("row")
@@ -407,7 +414,9 @@
     empty = jnp.zeros((128 - HEADS * VP, keys), f32)
     vpts_ref[...] = jnp.concatenate([part for p in points for part in (p[wide:], empty)], 0)
     key_points = [p[:wide] for p in points]
-    cross = dot(qpts_ref[...], jnp.concatenate(key_points + [jnp.ones((wide, keys), f32)], 0), precision=highest)
+    exact = jnp.concatenate(key_points + [jnp.ones((wide, keys), f32)], 0)
+    high = exact.astype(bf16)
+    cross = dot(qpts_ref[0], high) + (dot(qpts_ref[0], (exact - high.astype(f32)).astype(bf16)) + dot(qpts_ref[1], high))
     key_square = key_points[0] * key_points[0] + key_points[1] * key_points[1] + key_points[2] * key_points[2]
     feature = dot(qk_ref[...], x, NT)
     lane = lax.broadcasted_iota(jnp.int32, (1, 128), 1)
@@ -422,30 +431,39 @@
     key_lane = lax.broadcasted_iota(jnp.int32, (1, keys), 1)
     blocked = jnp.where(key_lane % PAD < rows, (kfeat[12:13] - 1.0) * masked_score, -1e30)
     same = (rows_ref[:, 13:14] == kfeat[13:14]).astype(f32)
-    hw = jnp.zeros((1, 128), f32)
-    for h in range(HEADS):
-        hw = jnp.where(lane == h, hw_ref[h], hw)
-    gains = GAIN * POINT * 0.5 * (jnp.maximum(hw, 0.0) + jnp.log1p(jnp.exp(-jnp.abs(hw))))
+    gains = heads_ref[0:1]
+    together = heads_ref[1:2]
     for h in range(HEADS):
         at = slice(h * rows, (h + 1) * rows)
         square = jnp.sum(key_square[h * QP : (h + 1) * QP], 0, keepdims=True)
         bias = jnp.concatenate([bias_low[h * half : (h + 1) * half], bias_high[h * half : (h + 1) * half]], 0)
         score = (
-            feature[at] + bias + (GAIN * cb_ref[h]) * same + cross[at] + (blocked - gains[:, h : h + 1] * square)
+            feature[at] + bias + together[:, h : h + 1] * same + cross[at] + (blocked - gains[:, h : h + 1] * square)
         )
         peak = jnp.max(score, 1, keepdims=True)
         weight = jnp.exp(score - peak)
         weight = weight / jnp.sum(weight, 1, keepdims=True)
         prob_ref[at, :] = weight
         side = jnp.where(col >= 2, weight[:, 128:], weight[:, :128])
-        near_ref[at, :] = pltpu.roll(side, (col % 2) * PAD, 1)
-    own_keys = pair_ref.shape[1]
-    for i in range(rows):
-        weight = near_ref[pl.ds(i, HEADS, stride=rows), :][:, :own_keys].astype(bf16)
-        opair_ref[pl.ds(i, HEADS, stride=rows), :] = dot(weight, pair_ref[i])
-    tail = HEADS * CH + 4 * HEADS * VP
+        near_ref[0, at, :] = jnp.where(low, pltpu.roll(side, (col % 2) * PAD, 1), 0.0)
+        near_ref[1, at, :] = jnp.where(low, 0.0, pltpu.roll(side, (1 - col % 2) * PAD, 1))
+    gap = jnp.zeros((PAD - pair_ref.shape[1], CZ), bf16)
+    blank = jnp.zeros((2 * HEADS, 2 * PAD), f32)
+    for i in range(0, rows, 4):
+        weight = []
+        for n in (i, i + 2):
+            weight.append(
+                jnp.concatenate([near_ref[m, pl.ds(n + m, HEADS, stride=rows), :] for m in (0, 1)], 0)
+            )
+        weight = jnp.concatenate(
+            [jnp.concatenate([weight[0], blank], 1), jnp.concatenate([blank, weight[1]], 1)], 0
+        ).astype(bf16)
+        summed = dot(weight, jnp.concatenate([part for n in range(4) for part in (pair_ref[i + n], gap)], 0))
+        for n in range(4):
+            opair_ref[pl.ds(i + n, HEADS, stride=rows), :] = summed[n * HEADS : (n + 1) * HEADS]
+    copy.wait()
     paired = jnp.concatenate([opair_ref[h * rows : (h + 1) * rows, :] for h in range(HEADS)], 1).astype(bf16)
-    out_ref[...] = dot(paired, w_out_ref[tail:]).astype(out_ref.dtype)
+    out_ref[...] = dot(paired, w_tail_ref[...]).astype(out_ref.dtype)
 
 
 def value_kernel(x_ref, prob_ref, vpts_ref, own_ref, rows_ref, w_kv_ref, w_out_ref, out_ref):
@@ -543,18 +561,18 @@
     order += [h * (QP + VP) + QP + n for h in range(HEADS) for n in range(VP)]
     order = jnp.asarray(np.eye(len(order), dtype=np.float32)[order], bf16)
     held = (
-        head_weights[None], rotation, translation, residue_mask[None], chain_index[None], node_embed, w_time,
+        head_weights[None], chain_bias[None], rotation, translation, residue_mask[None], chain_index[None], node_embed, w_time,
         w_query_points.T, w_kvp.T, order, w_query, w_kv,
     )
     shapes = [jax.ShapeDtypeStruct(array.shape, array.dtype) for array in held]
     shapes[-1] = jax.ShapeDtypeStruct((CS, HEADS * CH), bf16)
-    bias, *held = pl.pallas_call(
+    bias, *held, pair = pl.pallas_call(
         bias_kernel,
-        out_shape=[jax.ShapeDtypeStruct((HEADS * rows // 2, 2 * PAD), f32)] + shapes,
+        out_shape=[jax.ShapeDtypeStruct((HEADS * rows // 2, 2 * PAD), f32)] + shapes
+        + [jax.ShapeDtypeStruct(pair_embed.shape, bf16)],
         in_specs=[hbm] * (2 + len(held)),
-        out_specs=vmem(1 + len(held)),
+        out_specs=vmem(2 + len(held)),
         scratch_shapes=[
-            pltpu.VMEM(pair_embed.shape, bf16),
             pltpu.VMEM((HEADS, CZ), bf16),
             pltpu.SemaphoreType.DMA((3 + len(held),)),
         ],
@@ -572,19 +590,20 @@
             jax.ShapeDtypeStruct((8, CS), f32),
             jax.ShapeDtypeStruct((rows, CS), bf16),
             jax.ShapeDtypeStruct((HEADS * rows, CS), bf16),
-            jax.ShapeDtypeStruct((HEADS * rows, 4 * HEADS * QP), f32),
+            jax.ShapeDtypeStruct((2, HEADS * rows, 4 * HEADS * QP), bf16),
             jax.ShapeDtypeStruct((w_kvp.shape[1], CS), bf16),
             jax.ShapeDtypeStruct((16, 4 * PAD), f32),
             jax.ShapeDtypeStruct((rows, 16), f32),
             jax.ShapeDtypeStruct((rows, 16), f32),
+            jax.ShapeDtypeStruct((2, HEADS), f32),
         ),
-        in_specs=[smem] + vmem(12),
-        out_specs=tuple(vmem(8)),
+        in_specs=[smem] + vmem(13),
+        out_specs=tuple(vmem(9)),
         scratch_shapes=[pltpu.VMEM((16, total), f32)],
         compiler_params=params(16),
         cost_estimate=pl.CostEstimate(flops=2 * 10**9, bytes_accessed=8 * 10**6, transcendentals=0),
     )(step_index, *held)
-    time, own, qk, qpts, w_pts, kfeat, row_cols, key_cols = prepared
+    time, own, qk, qpts, w_pts, kfeat, row_cols, key_cols, heads = prepared
     partial, x, prob, vpts = pl.pallas_call(
         score_kernel,
         out_shape=(
@@ -593,15 +612,17 @@
             jax.ShapeDtypeStruct((HEADS * rows, 4 * PAD), f32),
             jax.ShapeDtypeStruct((3 * 128, 4 * PAD), f32),
         ),
-        in_specs=[smem, smem] + vmem(16),
+        in_specs=vmem(16) + [hbm],
         out_specs=tuple(vmem(4)),
         scratch_shapes=[
-            pltpu.VMEM((HEADS * rows, 2 * PAD), f32),
+            pltpu.VMEM((2, HEADS * rows, 2 * PAD), f32),
             pltpu.VMEM((HEADS * rows, CZ), f32),
             pltpu.VMEM((4,) + bias.shape, f32),
+            pltpu.VMEM((HEADS * CZ, CS), bf16),
+            pltpu.SemaphoreType.DMA,
         ],
         compiler_params=params(24),
-    )(head_weights, chain_bias, own, *others, time, qk, qpts, w_pts, kfeat, row_cols, bias, *biases, pair_embed, w_out)
+    )(heads, own, *others, time, qk, qpts, w_pts, kfeat, row_cols, bias, *biases, pair, *stay(w_out))
     base = pl.pallas_call(
         value_kernel,
         out_shape=jax.ShapeDtypeStruct((rows, CS), f32),
@@ -630,7 +651,7 @@
         out_specs=hbm,
         scratch_shapes=[pltpu.VMEM(pair_embed.shape, bf16), pltpu.SemaphoreType.DMA((rows // math.gcd(rows, 16),))],
         compiler_params=params(24),
-    )(side, other, row_cols, key_cols, pair_embed, w_trunk_in, w_trunk_mid, w_final)
+    )(side, other, row_cols, key_cols, pair, w_trunk_in, w_trunk_mid, w_final)
     return node_out, pair_out
 
 

time: 30.4 us -> 29.3 us (0.964)
  Pallas kernels: 11.6 us -> 11 us
  local copies, waits for them, and re-layouts: 0.57 us -> 0.05 us
    pallas_call x1, Pallas kernels: 2.76 us -> 2.03 us  [tile_body(): pl.pallas_call(score_kernel, out_shape=(jax.ShapeDtypeStruct((rows, CS),...]
    unnamed x24 -> x18, local copies, waits for them, and re-layouts: 0.57 us -> 0.05 us
where the time goes in v5:
time: 29.3 us; the launch traced here: 28.8 us
  starting transfers between devices  11.5 us (39%)
  Pallas kernels  11 us (38%)
  waiting for transfers between devices  4.79 us (16%)
  between operations  1.45 us (5%)
    ppermute x1, starting transfers between devices, tile_body(): fetched = lax.ppermute(node_embed, ('row', 'col'), apart)  3.56 us
    ppermute x1, starting transfers between devices, tile_body(): other = lax.ppermute(side, ('row', 'col'), turned)  3.49 us
    ppermute x1, waiting for transfers between devices, tile_body(): other = lax.ppermute(side, ('row', 'col'), turned)  3.39 us
    pallas_call x1, Pallas kernels, tile_body(): pl.pallas_call(edge_kernel, out_shape=jax.ShapeDtypeStruct(pair_embed.sha...  3.23 us
    ppermute x3, starting transfers between devices, tile_body(): lax.ppermute(partial, 'col', [(i, i ^ k) for i in range(4)])  2.3 us
    pallas_call x1, Pallas kernels, tile_body(): pl.pallas_call(bias_kernel, out_shape=[jax.ShapeDtypeStruct((HEADS * rows...  2.17 us
    pallas_call x1, Pallas kernels, tile_body(): pl.pallas_call(score_kernel, out_shape=(jax.ShapeDtypeStruct((rows, CS),...  2.03 us
    pallas_call x1, Pallas kernels, tile_body(): pl.pallas_call(value_kernel, out_shape=jax.ShapeDtypeStruct((rows, CS), f...  1.41 us
  transfers between devices with their start and end apart: 10, of which 3 were waited for; matrix products, arithmetic and copies ran while one was open for 0% of the time, Pallas kernels for 8%

profile of v5, /device:TPU:3, one launch (start us, length us, event | category | flops | bytes accessed | tf_op | source)
XLA Modules:
  0.0 28.8 jit_solution(1285784354703163281)
XLA Ops:
  0.6 0.0 copy-start.8
  0.6 2.2 %shard_map.230 = (f32[192,128]{1,0:T(8,128)S(1)}, f32[1,8]{1,0:T(1,128)S(1)}, f32[1,8]{1,0:T(1,128)S(1)}, f32[3,3,192]{2,1,0:T(4,128)S(1)}, f32[3,192]{1,0:T(4,1...) custom-call(bf16[48,48,128]{2,1,0:T(8,128)(2,1)} %refs_0_.1, ...), custom_call_target="tpu_custom_call" | custom-call | tf_op jit(solution)/shard_map/pallas_call | solution.py:569
  2.8 0.1 collective-permute-start.4
  2.9 0.0 copy-done.8
  2.9 3.6 %collective-permute-start = (bf16[48,256]{1,0:T(8,128)(2,1)S(1)}, bf16[48,256]{1,0:T(8,128)(2,1)S(1)}, u32[]{:S(2)}, u32[]{:S(2)}) collective-permute-start(bf16[48,256]{1,0:T(8,128)(2,1)S(1)} %copy-done.8), channel_id=1, source_target_pairs={{0,8},{1,13},{2,10},{3,15},{4,12},{5,9},{6,14},{7,11},{8,0},{9,5},... | collective-permute-start | bytes 73736 | tf_op jit(solution)/shard_map/ppermute | solution.py:583
  6.5 0.2 collective-permute-start.3
  6.7 1.3 %collective-permute-start.2 = (bf16[48,256]{1,0:T(8,128)(2,1)S(1)}, bf16[48,256]{1,0:T(8,128)(2,1)S(1)}, u32[]{:S(2)}, u32[]{:S(2)}) collective-permute-start(bf16[48,256]{1,0:T(8,128)(2,1)S(1)} %copy-done.8), channel_id=1, source_target_pairs={{0,4},{4,0},{8,12},{12,8},{1,5},{5,1},{9,13},{13,9},{2,6},{6,2},{1... | collective-permute-start | bytes 73736 | tf_op jit(solution)/shard_map/ppermute | solution.py:584
  8.6 0.0 collective-permute-done.n1_ref
  8.6 0.3 %collective-permute-start.1 = (bf16[48,256]{1,0:T(8,128)(2,1)S(1)}, bf16[48,256]{1,0:T(8,128)(2,1)S(1)}, u32[]{:S(2)}, u32[]{:S(2)}) collective-permute-start(bf16[48,256]{1,0:T(8,128)(2,1)S(1)} %collective-permute-done.n1_ref), channel_id=1, source_target_pairs={{0,1},{1,0},{2,3},{3,2},{4,5},{5,4},{6,7},{7,6},{8,9},{9,8},{10,11... | collective-permute-start | bytes 73736 | tf_op jit(solution)/shard_map/ppermute | solution.py:585
  9.0 0.0 collective-permute-done.4.b2_ref
  9.0 0.2 collective-permute-start.5
  9.2 0.0 copy-start.1
  9.2 0.9 %shard_map.231 = (f32[8,256]{1,0:T(8,128)S(1)}, bf16[48,256]{1,0:T(8,128)(2,1)S(1)}, bf16[384,256]{1,0:T(8,128)(2,1)S(1)}, bf16[2,384,256]{2,1,0:T(8,128)(2,1)S(...) custom-call(s32[1]{0:T(128)S(6)} %copy.25.step_ref, ...), custom_call_target="tpu_custom_call" | custom-call | flops 2000000000 | bytes 8000000 | tf_op jit(solution)/shard_map/pallas_call | solution.py:587
  10.1 0.0 copy-start
  10.1 0.0 collective-permute-done.2.n3_ref
  10.2 0.0 collective-permute-done.1.n2_ref
  10.2 0.0 collective-permute-done.3.b1_ref
  10.2 0.1 collective-permute-done.5.b3_ref
  10.3 2.0 %shard_map.232 = (bf16[48,256]{1,0:T(8,128)(2,1)S(1)}, bf16[256,256]{1,0:T(8,128)(2,1)S(1)}, f32[384,256]{1,0:T(8,128)S(1)}, f32[384,256]{1,0:T(8,128)S(1)}) custom-call(f32[2,8]{1,0:T(2,128)S(1)} %get-tuple-element.45.heads_ref, bf16[48,256]{1,0:T(8,128)(2,1)S(1)} %get-tuple-element.46.own_ref, bf16[48,256]{1,0:T(8,128)(2,1)S(1)} %collective-permute-done.n1_ref, ...), custom_call_target="tpu_custom_call" | custom-call | tf_op jit(solution)/shard_map/pallas_call | solution.py:607
  12.3 0.6 %collective-permute-start.6 = (bf16[48,256]{1,0:T(8,128)(2,1)S(1)}, bf16[48,256]{1,0:T(8,128)(2,1)S(1)}, u32[]{:S(2)}, u32[]{:S(2)}) collective-permute-start(bf16[48,256]{1,0:T(8,128)(2,1)S(1)} %get-tuple-element.55.u0_ref), channel_id=1, source_target_pairs={{0,1},{1,0},{2,3},{3,2},{4,5},{5,4},{6,7},{7,6},{8,9},{9,8},{10,11... | collective-permute-start | bytes 73736 | tf_op jit(solution)/shard_map/ppermute | solution.py:634
  12.9 1.2 %collective-permute-start.7 = (bf16[48,256]{1,0:T(8,128)(2,1)S(1)}, bf16[48,256]{1,0:T(8,128)(2,1)S(1)}, u32[]{:S(2)}, u32[]{:S(2)}) collective-permute-start(bf16[48,256]{1,0:T(8,128)(2,1)S(1)} %get-tuple-element.55.u0_ref), channel_id=1, source_target_pairs={{0,2},{1,3},{2,0},{3,1},{4,6},{5,7},{6,4},{7,5},{8,10},{9,11},{10,... | collective-permute-start | bytes 73736 | tf_op jit(solution)/shard_map/ppermute | solution.py:634
  14.2 0.5 %collective-permute-start.8 = (bf16[48,256]{1,0:T(8,128)(2,1)S(1)}, bf16[48,256]{1,0:T(8,128)(2,1)S(1)}, u32[]{:S(2)}, u32[]{:S(2)}) collective-permute-start(bf16[48,256]{1,0:T(8,128)(2,1)S(1)} %get-tuple-element.55.u0_ref), channel_id=1, source_target_pairs={{0,3},{1,2},{2,1},{3,0},{4,7},{5,6},{6,5},{7,4},{8,11},{9,10},{10,... | collective-permute-start | bytes 73736 | tf_op jit(solution)/shard_map/ppermute | solution.py:634
  14.6 0.0 copy-done.1
  14.6 0.0 copy-done
  14.6 0.0 copy-start.4
  14.7 0.0 copy-start.5
  14.7 0.0 copy-start.7
  14.7 0.0 copy-start.2
  14.7 0.0 copy-start.3
  14.7 0.0 copy-start.6
  14.7 1.4 %shard_map.233.base_ref = f32[48,256]{1,0:T(8,128)S(1)} custom-call(bf16[256,256]{1,0:T(8,128)(2,1)S(1)} %get-tuple-element.56.x_ref, f32[384,256]{1,0:T(8,128)S(1)} %get-tuple-element.57.prob_ref, f32[384,256]{1,0:T(8,128)S(1)} %get-tuple-element.58.vpts_ref, bf16[48,256]{1,0:T(8,128)(2,1)S(1)} %get-tuple-element.46.own_ref, ...), custom_call_target="tpu_custom_call" | custom-call | flops 1000000000 | bytes 4000000 | tf_op jit(solution)/shard_map/pallas_call | solution.py:626
  16.1 0.0 collective-permute-done.6.u1_ref
  16.1 0.0 collective-permute-done.7.u2_ref
  16.2 1.3 %collective-permute-done.8.u3_ref = bf16[48,256]{1,0:T(8,128)(2,1)S(1)} collective-permute-done((bf16[48,256]{1,0:T(8,128)(2,1)S(1)}, bf16[48,256]{1,0:T(8,128)(2,1)S(1)}, u32[]{:S(2)}, u32[]{:S(2)}) %collective-permute-start.8) | collective-permute-done | bytes 24608 | tf_op jit(solution)/shard_map/ppermute | solution.py:634
  17.4 0.0 copy-done.4
  17.4 0.0 copy-done.5
  17.4 0.0 copy-done.7
  17.4 1.2 %shard_map.234 = (bf16[48,256]{1,0:T(8,128)(2,1)}, bf16[48,128]{1,0:T(8,128)(2,1)S(1)}) custom-call(bf16[48,256]{1,0:T(8,128)(2,1)S(1)} %get-tuple-element.55.u0_ref, bf16[48,256]{1,0:T(8,128)(2,1)S(1)} %collective-permute-done.6.u1_ref, bf16[48,256]{1,0:T(8,128)(2,1)S(1)} %collective-permute-done.7.u2_ref, ...), custom_call_target="tpu_custom_call" | custom-call | tf_op jit(solution)/shard_map/pallas_call | solution.py:635
  18.7 3.5 %collective-permute-start.9 = (bf16[48,128]{1,0:T(8,128)(2,1)S(1)}, bf16[48,128]{1,0:T(8,128)(2,1)S(1)}, u32[]{:S(2)}, u32[]{:S(2)}) collective-permute-start(bf16[48,128]{1,0:T(8,128)(2,1)S(1)} %get-tuple-element.60.side_ref), channel_id=1, source_target_pairs={{0,0},{1,12},{2,8},{3,4},{5,5},{4,13},{7,1},{6,9},{10,10},{11,2},{... | collective-permute-start | bytes 36872 | tf_op jit(solution)/shard_map/ppermute | solution.py:646
  22.2 3.4 %collective-permute-done.9.other_ref = bf16[48,128]{1,0:T(8,128)(2,1)S(1)} collective-permute-done((bf16[48,128]{1,0:T(8,128)(2,1)S(1)}, bf16[48,128]{1,0:T(8,128)(2,1)S(1)}, u32[]{:S(2)}, u32[]{:S(2)}) %collective-permute-start.9) | collective-permute-done | bytes 12320 | tf_op jit(solution)/shard_map/ppermute | solution.py:646
  25.5 0.0 copy-done.2
  25.5 0.0 copy-done.3
  25.5 0.0 copy-done.6
  25.5 3.2 %shard_map.235 = bf16[48,48,128]{2,1,0:T(8,128)(2,1)} custom-call(bf16[48,128]{1,0:T(8,128)(2,1)S(1)} %get-tuple-element.60.side_ref, bf16[48,128]{1,0:T(8,128)(2,1)S(1)} %collective-permute-done.9.other_ref, f32[48,16]{1,0:T(8,128)S(1)} %get-tuple-element.52.rows_ref, f32[48,16]{1,0:T(8,128)S(1)} %get-tuple-element.61.keys_ref, ...), custom_call_target="tpu_custom_call" | custom-call | tf_op jit(solution)/shard_map/pallas_call | solution.py:647
Async XLA Ops:
  0.6 2.3 %copy-start.8 = (bf16[48,256]{1,0:T(8,128)(2,1)S(1)}, bf16[48,256]{1,0:T(8,128)(2,1)}, u32[]{:S(2)}) copy-start(bf16[48,256]{1,0:T(8,128)(2,1)} %refs_8_.1) | copy-start | bytes 73732
  2.8 6.2 %collective-permute-start.4 = (f32[192,128]{1,0:T(8,128)S(1)}, f32[192,128]{1,0:T(8,128)S(1)}, u32[]{:S(2)}, u32[]{:S(2)}) collective-permute-start(f32[192,128]{1,0:T(8,128)S(1)} %get-tuple-element.53.b0_ref), channel_id=1, source_target_pairs={{0,2},{1,3},{2,0},{3,1},{4,6},{5,7},{6,4},{7,5},{8,10},{9,11},{10,... | collective-permute-start | bytes 294920 | tf_op jit(solution)/shard_map/ppermute | solution.py:581
  2.9 5.7 %collective-permute-start = (bf16[48,256]{1,0:T(8,128)(2,1)S(1)}, bf16[48,256]{1,0:T(8,128)(2,1)S(1)}, u32[]{:S(2)}, u32[]{:S(2)}) collective-permute-start(bf16[48,256]{1,0:T(8,128)(2,1)S(1)} %copy-done.8), channel_id=1, source_target_pairs={{0,8},{1,13},{2,10},{3,15},{4,12},{5,9},{6,14},{7,11},{8,0},{9,5},... | collective-permute-start | bytes 73736 | tf_op jit(solution)/shard_map/ppermute | solution.py:583
  6.5 3.7 %collective-permute-start.3 = (f32[192,128]{1,0:T(8,128)S(1)}, f32[192,128]{1,0:T(8,128)S(1)}, u32[]{:S(2)}, u32[]{:S(2)}) collective-permute-start(f32[192,128]{1,0:T(8,128)S(1)} %get-tuple-element.53.b0_ref), channel_id=1, source_target_pairs={{0,1},{1,0},{2,3},{3,2},{4,5},{5,4},{6,7},{7,6},{8,9},{9,8},{10,11... | collective-permute-start | bytes 294920 | tf_op jit(solution)/shard_map/ppermute | solution.py:581
  6.7 3.5 %collective-permute-start.2 = (bf16[48,256]{1,0:T(8,128)(2,1)S(1)}, bf16[48,256]{1,0:T(8,128)(2,1)S(1)}, u32[]{:S(2)}, u32[]{:S(2)}) collective-permute-start(bf16[48,256]{1,0:T(8,128)(2,1)S(1)} %copy-done.8), channel_id=1, source_target_pairs={{0,4},{4,0},{8,12},{12,8},{1,5},{5,1},{9,13},{13,9},{2,6},{6,2},{1... | collective-permute-start | bytes 73736 | tf_op jit(solution)/shard_map/ppermute | solution.py:584
  8.6 1.5 %collective-permute-start.1 = (bf16[48,256]{1,0:T(8,128)(2,1)S(1)}, bf16[48,256]{1,0:T(8,128)(2,1)S(1)}, u32[]{:S(2)}, u32[]{:S(2)}) collective-permute-start(bf16[48,256]{1,0:T(8,128)(2,1)S(1)} %collective-permute-done.n1_ref), channel_id=1, source_target_pairs={{0,1},{1,0},{2,3},{3,2},{4,5},{5,4},{6,7},{7,6},{8,9},{9,8},{10,11... | collective-permute-start | bytes 73736 | tf_op jit(solution)/shard_map/ppermute | solution.py:585
  9.0 1.3 %collective-permute-start.5 = (f32[192,128]{1,0:T(8,128)S(1)}, f32[192,128]{1,0:T(8,128)S(1)}, u32[]{:S(2)}, u32[]{:S(2)}) collective-permute-start(f32[192,128]{1,0:T(8,128)S(1)} %collective-permute-done.4.b2_ref), channel_id=1, source_target_pairs={{0,1},{1,0},{2,3},{3,2},{4,5},{5,4},{6,7},{7,6},{8,9},{9,8},{10,11... | collective-permute-start | bytes 294920 | tf_op jit(solution)/shard_map/ppermute | solution.py:586
  9.2 5.4 %copy-start.1 = (bf16[3456,256]{1,0:T(8,128)(2,1)S(1)}, bf16[3456,256]{1,0:T(8,128)(2,1)}, u32[]{:S(2)}) copy-start(bf16[3456,256]{1,0:T(8,128)(2,1)} %w_out_ref.3) | copy-start | bytes 5308420
  10.1 4.5 %copy-start = (bf16[256,4096]{1,0:T(8,128)(2,1)S(1)}, bf16[256,4096]{1,0:T(8,128)(2,1)}, u32[]{:S(2)}) copy-start(bf16[256,4096]{1,0:T(8,128)(2,1)} %w_kv_ref.1) | copy-start | bytes 6291460
  12.3 3.8 %collective-permute-start.6 = (bf16[48,256]{1,0:T(8,128)(2,1)S(1)}, bf16[48,256]{1,0:T(8,128)(2,1)S(1)}, u32[]{:S(2)}, u32[]{:S(2)}) collective-permute-start(bf16[48,256]{1,0:T(8,128)(2,1)S(1)} %get-tuple-element.55.u0_ref), channel_id=1, source_target_pairs={{0,1},{1,0},{2,3},{3,2},{4,5},{5,4},{6,7},{7,6},{8,9},{9,8},{10,11... | collective-permute-start | bytes 73736 | tf_op jit(solution)/shard_map/ppermute | solution.py:634
  12.9 3.2 %collective-permute-start.7 = (bf16[48,256]{1,0:T(8,128)(2,1)S(1)}, bf16[48,256]{1,0:T(8,128)(2,1)S(1)}, u32[]{:S(2)}, u32[]{:S(2)}) collective-permute-start(bf16[48,256]{1,0:T(8,128)(2,1)S(1)} %get-tuple-element.55.u0_ref), channel_id=1, source_target_pairs={{0,2},{1,3},{2,0},{3,1},{4,6},{5,7},{6,4},{7,5},{8,10},{9,11},{10,... | collective-permute-start | bytes 73736 | tf_op jit(solution)/shard_map/ppermute | solution.py:634
  14.2 3.3 %collective-permute-start.8 = (bf16[48,256]{1,0:T(8,128)(2,1)S(1)}, bf16[48,256]{1,0:T(8,128)(2,1)S(1)}, u32[]{:S(2)}, u32[]{:S(2)}) collective-permute-start(bf16[48,256]{1,0:T(8,128)(2,1)S(1)} %get-tuple-element.55.u0_ref), channel_id=1, source_target_pairs={{0,3},{1,2},{2,1},{3,0},{4,7},{5,6},{6,5},{7,4},{8,11},{9,10},{10,... | collective-permute-start | bytes 73736 | tf_op jit(solution)/shard_map/ppermute | solution.py:634
  14.6 2.8 %copy-start.4 = (bf16[256,256]{1,0:T(8,128)(2,1)S(1)}, bf16[256,256]{1,0:T(8,128)(2,1)}, u32[]{:S(2)}) copy-start(bf16[256,256]{1,0:T(8,128)(2,1)} %w_in_ref.2) | copy-start | bytes 393220
  14.7 2.8 %copy-start.5 = (bf16[256,256]{1,0:T(8,128)(2,1)S(1)}, bf16[256,256]{1,0:T(8,128)(2,1)}, u32[]{:S(2)}) copy-start(bf16[256,256]{1,0:T(8,128)(2,1)} %w_back_ref.1) | copy-start | bytes 393220
  14.7 2.8 %copy-start.7 = (bf16[256,128]{1,0:T(8,128)(2,1)S(1)}, bf16[256,128]{1,0:T(8,128)(2,1)}, u32[]{:S(2)}) copy-start(bf16[256,128]{1,0:T(8,128)(2,1)} %w_edge_ref.1) | copy-start | bytes 196612
  14.7 10.9 %copy-start.2 = (bf16[384,384]{1,0:T(8,128)(2,1)S(1)}, bf16[384,384]{1,0:T(8,128)(2,1)}, u32[]{:S(2)}) copy-start(bf16[384,384]{1,0:T(8,128)(2,1)} %w_in_ref.3) | copy-start | bytes 884740
  14.7 10.9 %copy-start.3 = (bf16[384,384]{1,0:T(8,128)(2,1)S(1)}, bf16[384,384]{1,0:T(8,128)(2,1)}, u32[]{:S(2)}) copy-start(bf16[384,384]{1,0:T(8,128)(2,1)} %w_mid_ref.1) | copy-start | bytes 884740
  14.7 10.9 %copy-start.6 = (bf16[384,128]{1,0:T(8,128)(2,1)S(1)}, bf16[384,128]{1,0:T(8,128)(2,1)}, u32[]{:S(2)}) copy-start(bf16[384,128]{1,0:T(8,128)(2,1)} %w_final_ref.1) | copy-start | bytes 294916
  18.7 6.9 %collective-permute-start.9 = (bf16[48,128]{1,0:T(8,128)(2,1)S(1)}, bf16[48,128]{1,0:T(8,128)(2,1)S(1)}, u32[]{:S(2)}, u32[]{:S(2)}) collective-permute-start(bf16[48,128]{1,0:T(8,128)(2,1)S(1)} %get-tuple-element.60.side_ref), channel_id=1, source_target_pairs={{0,0},{1,12},{2,8},{3,4},{5,5},{4,13},{7,1},{6,9},{10,10},{11,2},{... | collective-permute-start | bytes 36872 | tf_op jit(solution)/shard_map/ppermute | solution.py:646

commit v6 on v5

--- a/solution.py
+++ b/solution.py
@@ -510,12 +510,24 @@
     side_ref[...] = dot(node, w_edge_ref[...]).astype(bf16)
 
 
+def lift_kernel(node_ref, side_ref, pair_ref, w_in_ref, node_hbm, out_ref, sem):
+    copy = pltpu.make_async_copy(node_ref, node_hbm, sem)
+    copy.start()
+    rows, keys = pair_ref.shape[:2]
+    step = math.gcd(rows, 16)
+    pre_rows = dot(side_ref[...], w_in_ref[CZ : CZ + NH])
+    for begin in range(0, rows, step):
+        lifted = dot(pair_ref[begin : begin + step].reshape(step * keys, CZ), w_in_ref[:CZ])
+        for n in range(step):
+            out_ref[begin + n] = lifted[n * keys : (n + 1) * keys] + pre_rows[begin + n : begin + n + 1]
+    copy.wait()
+
+
 def edge_kernel(
-    side_ref, other_ref, rows_ref, keys_ref, pair_ref, w_in_ref, w_mid_ref, w_final_ref, out_hbm, out_ref, sems
+    lifted_ref, side_ref, other_ref, rows_ref, keys_ref, pair_ref, w_in_ref, w_mid_ref, w_final_ref, out_hbm, out_ref, sems
 ):
     rows, keys = pair_ref.shape[:2]
     step = math.gcd(rows, 16)
-    pre_rows = dot(side_ref[...], w_in_ref[CZ : CZ + NH])
     pre_keys = dot(other_ref[...], w_in_ref[CZ + NH :])
     side = side_ref[...].astype(f32)
     other = other_ref[...].astype(f32)
@@ -525,10 +537,7 @@
     for begin in range(0, rows, step):
         parts = [(begin + n, slice(n * keys, (n + 1) * keys)) for n in range(step)]
         pair = pair_ref[begin : begin + step].reshape(step * keys, CZ)
-        lifted = dot(pair, w_in_ref[:CZ])
-        first = jnp.concatenate(
-            [jnp.maximum(lifted[at] + (pre_keys + pre_rows[i : i + 1]), 0.0).astype(bf16) for i, at in parts], 0
-        )
+        first = jnp.concatenate([jnp.maximum(lifted_ref[i] + pre_keys, 0.0).astype(bf16) for i, at in parts], 0)
         second = jnp.maximum(dot(first, w_mid_ref[...]), 0.0)
         joined = jnp.concatenate(
             [
@@ -632,7 +641,7 @@
         cost_estimate=pl.CostEstimate(flops=10**9, bytes_accessed=4 * 10**6, transcendentals=0),
     )(x, prob, vpts, own, row_cols, w_kv, w_out)
     partials = [lax.ppermute(partial, "col", [(i, i ^ k) for i in range(4)]) for k in (1, 2, 3)]
-    node_out, side = pl.pallas_call(
+    node, side = pl.pallas_call(
         node_kernel,
         out_shape=(jax.ShapeDtypeStruct((rows, CS), bf16), jax.ShapeDtypeStruct((rows, NH), bf16)),
         in_specs=vmem(9),
@@ -642,16 +651,28 @@
     turned = []
     for c in range(4):
         far = sorted((r for r in range(4) if r != c), key=lambda r: -abs(r - c))
-        turned += [(4 * c + source, 4 * r + c) for r, source in zip([c] + far, (c, c ^ 1, c ^ 2, c ^ 3))]
+        turned += [(4 * c + source, 4 * r + c) for r, source in zip(far + [c], (c, c ^ 1, c ^ 2, c ^ 3))]
     other = lax.ppermute(side, ("row", "col"), turned)
+    node_out, lifted = pl.pallas_call(
+        lift_kernel,
+        out_shape=(
+            jax.ShapeDtypeStruct(node.shape, bf16),
+            jax.ShapeDtypeStruct(pair_embed.shape[:2] + (HID,), f32),
+        ),
+        in_specs=vmem(4),
+        out_specs=(hbm, pl.BlockSpec(memory_space=pltpu.VMEM)),
+        scratch_shapes=[pltpu.SemaphoreType.DMA],
+        compiler_params=params(16),
+        cost_estimate=pl.CostEstimate(flops=2 * rows * rows * CZ * HID, bytes_accessed=4 * 10**6, transcendentals=0),
+    )(node, side, pair, w_trunk_in)
     pair_out = pl.pallas_call(
         edge_kernel,
         out_shape=jax.ShapeDtypeStruct(pair_embed.shape, bf16),
-        in_specs=vmem(8),
+        in_specs=vmem(9),
         out_specs=hbm,
         scratch_shapes=[pltpu.VMEM(pair_embed.shape, bf16), pltpu.SemaphoreType.DMA((rows // math.gcd(rows, 16),))],
         compiler_params=params(24),
-    )(side, other, row_cols, key_cols, pair, w_trunk_in, w_trunk_mid, w_final)
+    )(lifted, side, other, row_cols, key_cols, pair, w_trunk_in, w_trunk_mid, w_final)
     return node_out, pair_out
 
 

time: 29.3 us -> 27.5 us (0.939)
  the two profiles are of different devices: /device:TPU:3 before, /device:TPU:0 now
where the time goes in v6:
time: 27.5 us; the launch traced here: 27.3 us
  starting transfers between devices  13.2 us (48%)
  Pallas kernels  10.7 us (39%)
  waiting for transfers between devices  1.93 us (7%)
  between operations  1.42 us (5%)
    ppermute x1, starting transfers between devices, tile_body(): other = lax.ppermute(side, ('row', 'col'), turned)  3.48 us
    ppermute x2, starting transfers between devices, tile_body(): lax.ppermute(bias, 'col', [(i, i ^ k) for i in range(4)])  3.01 us
    pallas_call x1, Pallas kernels, tile_body(): pl.pallas_call(edge_kernel, out_shape=jax.ShapeDtypeStruct(pair_embed.sha...  2.79 us
    ppermute x1, starting transfers between devices, tile_body(): fetched = lax.ppermute(node_embed, ('row', 'col'), apart)  2.59 us
    pallas_call x1, Pallas kernels, tile_body(): pl.pallas_call(bias_kernel, out_shape=[jax.ShapeDtypeStruct((HEADS * rows...  2.17 us
    pallas_call x1, Pallas kernels, tile_body(): pl.pallas_call(score_kernel, out_shape=(jax.ShapeDtypeStruct((rows, CS),...  2.04 us
    ppermute x3, starting transfers between devices, tile_body(): lax.ppermute(partial, 'col', [(i, i ^ k) for i in range(4)])  1.93 us
    ppermute x1, starting transfers between devices, tile_body(): beside = lax.ppermute(node_embed, 'row', [(i, i ^ 1) for i in range(4)])  1.58 us
  transfers between devices with their start and end apart: 10, of which 3 were waited for; matrix products, arithmetic and copies ran while one was open for 0% of the time, Pallas kernels for 11%

profile of v6, /device:TPU:0, one launch (start us, length us, event | category | flops | bytes accessed | tf_op | source)
XLA Modules:
  0.0 27.3 jit_solution(15126853732269207328)
XLA Ops:
  0.6 0.0 copy-start.8
  0.6 2.2 %shard_map.230 = (f32[192,128]{1,0:T(8,128)S(1)}, f32[1,8]{1,0:T(1,128)S(1)}, f32[1,8]{1,0:T(1,128)S(1)}, f32[3,3,192]{2,1,0:T(4,128)S(1)}, f32[3,192]{1,0:T(4,1...) custom-call(bf16[48,48,128]{2,1,0:T(8,128)(2,1)} %refs_0_.1, ...), custom_call_target="tpu_custom_call" | custom-call | tf_op jit(solution)/shard_map/pallas_call | solution.py:578
  2.8 3.0 %collective-permute-start.4 = (f32[192,128]{1,0:T(8,128)S(1)}, f32[192,128]{1,0:T(8,128)S(1)}, u32[]{:S(2)}, u32[]{:S(2)}) collective-permute-start(f32[192,128]{1,0:T(8,128)S(1)} %get-tuple-element.55.b0_ref), channel_id=1, source_target_pairs={{0,2},{1,3},{2,0},{3,1},{4,6},{5,7},{6,4},{7,5},{8,10},{9,11},{10,... | collective-permute-start | bytes 294920 | tf_op jit(solution)/shard_map/ppermute | solution.py:590
  5.8 0.0 copy-done.8
  5.8 2.6 %collective-permute-start = (bf16[48,256]{1,0:T(8,128)(2,1)S(1)}, bf16[48,256]{1,0:T(8,128)(2,1)S(1)}, u32[]{:S(2)}, u32[]{:S(2)}) collective-permute-start(bf16[48,256]{1,0:T(8,128)(2,1)S(1)} %copy-done.8), channel_id=1, source_target_pairs={{0,8},{1,13},{2,10},{3,15},{4,12},{5,9},{6,14},{7,11},{8,0},{9,5},... | collective-permute-start | bytes 73736 | tf_op jit(solution)/shard_map/ppermute | solution.py:592
  8.4 1.6 %collective-permute-start.2 = (bf16[48,256]{1,0:T(8,128)(2,1)S(1)}, bf16[48,256]{1,0:T(8,128)(2,1)S(1)}, u32[]{:S(2)}, u32[]{:S(2)}) collective-permute-start(bf16[48,256]{1,0:T(8,128)(2,1)S(1)} %copy-done.8), channel_id=1, source_target_pairs={{0,4},{4,0},{8,12},{12,8},{1,5},{5,1},{9,13},{13,9},{2,6},{6,2},{1... | collective-permute-start | bytes 73736 | tf_op jit(solution)/shard_map/ppermute | solution.py:593
  10.0 0.0 collective-permute-start.3
  10.6 0.0 collective-permute-done.n1_ref
  10.7 0.6 %collective-permute-start.1 = (bf16[48,256]{1,0:T(8,128)(2,1)S(1)}, bf16[48,256]{1,0:T(8,128)(2,1)S(1)}, u32[]{:S(2)}, u32[]{:S(2)}) collective-permute-start(bf16[48,256]{1,0:T(8,128)(2,1)S(1)} %collective-permute-done.n1_ref), channel_id=1, source_target_pairs={{0,1},{1,0},{2,3},{3,2},{4,5},{5,4},{6,7},{7,6},{8,9},{9,8},{10,11... | collective-permute-start | bytes 73736 | tf_op jit(solution)/shard_map/ppermute | solution.py:594
  11.2 0.0 collective-permute-done.4.b2_ref
  11.2 0.1 collective-permute-start.5
  11.3 0.0 copy-start.1
  11.3 0.9 %shard_map.231 = (f32[8,256]{1,0:T(8,128)S(1)}, bf16[48,256]{1,0:T(8,128)(2,1)S(1)}, bf16[384,256]{1,0:T(8,128)(2,1)S(1)}, bf16[2,384,256]{2,1,0:T(8,128)(2,1)S(...) custom-call(s32[1]{0:T(128)S(6)} %copy.25.step_ref, ...), custom_call_target="tpu_custom_call" | custom-call | flops 2000000000 | bytes 8000000 | tf_op jit(solution)/shard_map/pallas_call | solution.py:596
  12.2 0.0 copy-start
  12.2 0.0 collective-permute-done.2.n3_ref
  12.2 0.0 collective-permute-done.1.n2_ref
  12.2 0.0 collective-permute-done.3.b1_ref
  12.3 0.3 %collective-permute-done.5.b3_ref = f32[192,128]{1,0:T(8,128)S(1)} collective-permute-done((f32[192,128]{1,0:T(8,128)S(1)}, f32[192,128]{1,0:T(8,128)S(1)}, u32[]{:S(2)}, u32[]{:S(2)}) %collective-permute-start.5) | collective-permute-done | bytes 98336 | tf_op jit(solution)/shard_map/ppermute | solution.py:595
  12.5 2.0 %shard_map.232 = (bf16[48,256]{1,0:T(8,128)(2,1)S(1)}, bf16[256,256]{1,0:T(8,128)(2,1)S(1)}, f32[384,256]{1,0:T(8,128)S(1)}, f32[384,256]{1,0:T(8,128)S(1)}) custom-call(f32[2,8]{1,0:T(2,128)S(1)} %get-tuple-element.47.heads_ref, bf16[48,256]{1,0:T(8,128)(2,1)S(1)} %get-tuple-element.48.own_ref, bf16[48,256]{1,0:T(8,128)(2,1)S(1)} %collective-permute-done.n1_ref, ...), custom_call_target="tpu_custom_call" | custom-call | tf_op jit(solution)/shard_map/pallas_call | solution.py:616
  14.6 0.2 collective-permute-start.6
  14.8 0.5 %collective-permute-start.7 = (bf16[48,256]{1,0:T(8,128)(2,1)S(1)}, bf16[48,256]{1,0:T(8,128)(2,1)S(1)}, u32[]{:S(2)}, u32[]{:S(2)}) collective-permute-start(bf16[48,256]{1,0:T(8,128)(2,1)S(1)} %get-tuple-element.57.u0_ref), channel_id=1, source_target_pairs={{0,2},{1,3},{2,0},{3,1},{4,6},{5,7},{6,4},{7,5},{8,10},{9,11},{10,... | collective-permute-start | bytes 73736 | tf_op jit(solution)/shard_map/ppermute | solution.py:643
  15.3 1.2 %collective-permute-start.8 = (bf16[48,256]{1,0:T(8,128)(2,1)S(1)}, bf16[48,256]{1,0:T(8,128)(2,1)S(1)}, u32[]{:S(2)}, u32[]{:S(2)}) collective-permute-start(bf16[48,256]{1,0:T(8,128)(2,1)S(1)} %get-tuple-element.57.u0_ref), channel_id=1, source_target_pairs={{0,3},{1,2},{2,1},{3,0},{4,7},{5,6},{6,5},{7,4},{8,11},{9,10},{10,... | collective-permute-start | bytes 73736 | tf_op jit(solution)/shard_map/ppermute | solution.py:643
  16.5 0.0 copy-done.1
  16.5 0.0 copy-done
  16.5 0.0 copy-start.4
  16.5 0.0 copy-start.5
  16.5 0.0 copy-start.7
  16.5 0.0 copy-start.2
  16.5 0.0 copy-start.3
  16.6 0.0 copy-start.6
  16.6 1.4 %shard_map.233.base_ref = f32[48,256]{1,0:T(8,128)S(1)} custom-call(bf16[256,256]{1,0:T(8,128)(2,1)S(1)} %get-tuple-element.58.x_ref, f32[384,256]{1,0:T(8,128)S(1)} %get-tuple-element.59.prob_ref, f32[384,256]{1,0:T(8,128)S(1)} %get-tuple-element.60.vpts_ref, bf16[48,256]{1,0:T(8,128)(2,1)S(1)} %get-tuple-element.48.own_ref, ...), custom_call_target="tpu_custom_call" | custom-call | flops 1000000000 | bytes 4000000 | tf_op jit(solution)/shard_map/pallas_call | solution.py:635
  18.0 0.0 collective-permute-done.6.u1_ref
  18.0 0.9 %collective-permute-done.7.u2_ref = bf16[48,256]{1,0:T(8,128)(2,1)S(1)} collective-permute-done((bf16[48,256]{1,0:T(8,128)(2,1)S(1)}, bf16[48,256]{1,0:T(8,128)(2,1)S(1)}, u32[]{:S(2)}, u32[]{:S(2)}) %collective-permute-start.7) | collective-permute-done | bytes 24608 | tf_op jit(solution)/shard_map/ppermute | solution.py:643
  18.9 0.0 collective-permute-done.8.u3_ref
  18.9 0.0 copy-done.4
  18.9 0.0 copy-done.5
  18.9 0.0 copy-done.7
  18.9 0.7 %shard_map.234 = (bf16[48,256]{1,0:T(8,128)(2,1)S(1)}, bf16[48,128]{1,0:T(8,128)(2,1)S(1)}) custom-call(bf16[48,256]{1,0:T(8,128)(2,1)S(1)} %get-tuple-element.57.u0_ref, bf16[48,256]{1,0:T(8,128)(2,1)S(1)} %collective-permute-done.6.u1_ref, bf16[48,256]{1,0:T(8,128)(2,1)S(1)} %collective-permute-done.7.u2_ref, ...), custom_call_target="tpu_custom_call" | custom-call | tf_op jit(solution)/shard_map/pallas_call | solution.py:644
  19.6 3.5 %collective-permute-start.9 = (bf16[48,128]{1,0:T(8,128)(2,1)S(1)}, bf16[48,128]{1,0:T(8,128)(2,1)S(1)}, u32[]{:S(2)}, u32[]{:S(2)}) collective-permute-start(bf16[48,128]{1,0:T(8,128)(2,1)S(1)} %get-tuple-element.62.side_ref), channel_id=1, source_target_pairs={{0,12},{1,8},{2,4},{3,0},{5,13},{4,1},{7,9},{6,5},{10,2},{11,6},{8... | collective-permute-start | bytes 36872 | tf_op jit(solution)/shard_map/ppermute | solution.py:655
  23.1 0.0 copy-done.2
  23.1 0.6 %shard_map.235 = (bf16[48,256]{1,0:T(8,128)(2,1)}, f32[48,48,384]{2,1,0:T(8,128)S(1)}) custom-call(bf16[48,256]{1,0:T(8,128)(2,1)S(1)} %get-tuple-element.61.node_ref, bf16[48,128]{1,0:T(8,128)(2,1)S(1)} %get-tuple-element.62.side_ref, bf16[48,48,128]{2,1,0:T(8,128)(2,1)S(1)} %get-tuple-element.56.pair_ref, bf16[384,384]{1,0:T(8,128)(2,1)S(1)} %copy-done.2), custom_call_target="tpu_custom_call" | custom-call | flops 226492416 | bytes 4000000 | tf_op jit(solution)/shard_map/pallas_call | solution.py:656
  23.7 0.8 %collective-permute-done.9.other_ref = bf16[48,128]{1,0:T(8,128)(2,1)S(1)} collective-permute-done((bf16[48,128]{1,0:T(8,128)(2,1)S(1)}, bf16[48,128]{1,0:T(8,128)(2,1)S(1)}, u32[]{:S(2)}, u32[]{:S(2)}) %collective-permute-start.9) | collective-permute-done | bytes 12320 | tf_op jit(solution)/shard_map/ppermute | solution.py:655
  24.5 0.0 copy-done.3
  24.5 0.0 copy-done.6
  24.5 2.8 %shard_map.236 = bf16[48,48,128]{2,1,0:T(8,128)(2,1)} custom-call(f32[48,48,384]{2,1,0:T(8,128)S(1)} %get-tuple-element.64.lifted_ref, bf16[48,128]{1,0:T(8,128)(2,1)S(1)} %get-tuple-element.62.side_ref, bf16[48,128]{1,0:T(8,128)(2,1)S(1)} %collective-permute-done.9.other_ref, f32[48,16]{1,0:T(8,128)S(1)} %get-tuple-element.54.rows_ref, ...), custom_call_target="tpu_custom_call" | custom-call | tf_op jit(solution)/shard_map/pallas_call | solution.py:668
Async XLA Ops:
  0.6 5.2 %copy-start.8 = (bf16[48,256]{1,0:T(8,128)(2,1)S(1)}, bf16[48,256]{1,0:T(8,128)(2,1)}, u32[]{:S(2)}) copy-start(bf16[48,256]{1,0:T(8,128)(2,1)} %refs_8_.1) | copy-start | bytes 73732
  2.8 8.4 %collective-permute-start.4 = (f32[192,128]{1,0:T(8,128)S(1)}, f32[192,128]{1,0:T(8,128)S(1)}, u32[]{:S(2)}, u32[]{:S(2)}) collective-permute-start(f32[192,128]{1,0:T(8,128)S(1)} %get-tuple-element.55.b0_ref), channel_id=1, source_target_pairs={{0,2},{1,3},{2,0},{3,1},{4,6},{5,7},{6,4},{7,5},{8,10},{9,11},{10,... | collective-permute-start | bytes 294920 | tf_op jit(solution)/shard_map/ppermute | solution.py:590
  5.8 4.8 %collective-permute-start = (bf16[48,256]{1,0:T(8,128)(2,1)S(1)}, bf16[48,256]{1,0:T(8,128)(2,1)S(1)}, u32[]{:S(2)}, u32[]{:S(2)}) collective-permute-start(bf16[48,256]{1,0:T(8,128)(2,1)S(1)} %copy-done.8), channel_id=1, source_target_pairs={{0,8},{1,13},{2,10},{3,15},{4,12},{5,9},{6,14},{7,11},{8,0},{9,5},... | collective-permute-start | bytes 73736 | tf_op jit(solution)/shard_map/ppermute | solution.py:592
  8.4 3.8 %collective-permute-start.2 = (bf16[48,256]{1,0:T(8,128)(2,1)S(1)}, bf16[48,256]{1,0:T(8,128)(2,1)S(1)}, u32[]{:S(2)}, u32[]{:S(2)}) collective-permute-start(bf16[48,256]{1,0:T(8,128)(2,1)S(1)} %copy-done.8), channel_id=1, source_target_pairs={{0,4},{4,0},{8,12},{12,8},{1,5},{5,1},{9,13},{13,9},{2,6},{6,2},{1... | collective-permute-start | bytes 73736 | tf_op jit(solution)/shard_map/ppermute | solution.py:593
  10.0 2.3 %collective-permute-start.3 = (f32[192,128]{1,0:T(8,128)S(1)}, f32[192,128]{1,0:T(8,128)S(1)}, u32[]{:S(2)}, u32[]{:S(2)}) collective-permute-start(f32[192,128]{1,0:T(8,128)S(1)} %get-tuple-element.55.b0_ref), channel_id=1, source_target_pairs={{0,1},{1,0},{2,3},{3,2},{4,5},{5,4},{6,7},{7,6},{8,9},{9,8},{10,11... | collective-permute-start | bytes 294920 | tf_op jit(solution)/shard_map/ppermute | solution.py:590
  10.7 1.6 %collective-permute-start.1 = (bf16[48,256]{1,0:T(8,128)(2,1)S(1)}, bf16[48,256]{1,0:T(8,128)(2,1)S(1)}, u32[]{:S(2)}, u32[]{:S(2)}) collective-permute-start(bf16[48,256]{1,0:T(8,128)(2,1)S(1)} %collective-permute-done.n1_ref), channel_id=1, source_target_pairs={{0,1},{1,0},{2,3},{3,2},{4,5},{5,4},{6,7},{7,6},{8,9},{9,8},{10,11... | collective-permute-start | bytes 73736 | tf_op jit(solution)/shard_map/ppermute | solution.py:594
  11.2 1.3 %collective-permute-start.5 = (f32[192,128]{1,0:T(8,128)S(1)}, f32[192,128]{1,0:T(8,128)S(1)}, u32[]{:S(2)}, u32[]{:S(2)}) collective-permute-start(f32[192,128]{1,0:T(8,128)S(1)} %collective-permute-done.4.b2_ref), channel_id=1, source_target_pairs={{0,1},{1,0},{2,3},{3,2},{4,5},{5,4},{6,7},{7,6},{8,9},{9,8},{10,11... | collective-permute-start | bytes 294920 | tf_op jit(solution)/shard_map/ppermute | solution.py:595
  11.3 5.2 %copy-start.1 = (bf16[3456,256]{1,0:T(8,128)(2,1)S(1)}, bf16[3456,256]{1,0:T(8,128)(2,1)}, u32[]{:S(2)}) copy-start(bf16[3456,256]{1,0:T(8,128)(2,1)} %w_out_ref.3) | copy-start | bytes 5308420
  12.2 4.3 %copy-start = (bf16[256,4096]{1,0:T(8,128)(2,1)S(1)}, bf16[256,4096]{1,0:T(8,128)(2,1)}, u32[]{:S(2)}) copy-start(bf16[256,4096]{1,0:T(8,128)(2,1)} %w_kv_ref.1) | copy-start | bytes 6291460
  14.6 3.4 %collective-permute-start.6 = (bf16[48,256]{1,0:T(8,128)(2,1)S(1)}, bf16[48,256]{1,0:T(8,128)(2,1)S(1)}, u32[]{:S(2)}, u32[]{:S(2)}) collective-permute-start(bf16[48,256]{1,0:T(8,128)(2,1)S(1)} %get-tuple-element.57.u0_ref), channel_id=1, source_target_pairs={{0,1},{1,0},{2,3},{3,2},{4,5},{5,4},{6,7},{7,6},{8,9},{9,8},{10,11... | collective-permute-start | bytes 73736 | tf_op jit(solution)/shard_map/ppermute | solution.py:643
  14.8 4.1 %collective-permute-start.7 = (bf16[48,256]{1,0:T(8,128)(2,1)S(1)}, bf16[48,256]{1,0:T(8,128)(2,1)S(1)}, u32[]{:S(2)}, u32[]{:S(2)}) collective-permute-start(bf16[48,256]{1,0:T(8,128)(2,1)S(1)} %get-tuple-element.57.u0_ref), channel_id=1, source_target_pairs={{0,2},{1,3},{2,0},{3,1},{4,6},{5,7},{6,4},{7,5},{8,10},{9,11},{10,... | collective-permute-start | bytes 73736 | tf_op jit(solution)/shard_map/ppermute | solution.py:643
  15.3 3.5 %collective-permute-start.8 = (bf16[48,256]{1,0:T(8,128)(2,1)S(1)}, bf16[48,256]{1,0:T(8,128)(2,1)S(1)}, u32[]{:S(2)}, u32[]{:S(2)}) collective-permute-start(bf16[48,256]{1,0:T(8,128)(2,1)S(1)} %get-tuple-element.57.u0_ref), channel_id=1, source_target_pairs={{0,3},{1,2},{2,1},{3,0},{4,7},{5,6},{6,5},{7,4},{8,11},{9,10},{10,... | collective-permute-start | bytes 73736 | tf_op jit(solution)/shard_map/ppermute | solution.py:643
  16.5 2.4 %copy-start.4 = (bf16[256,256]{1,0:T(8,128)(2,1)S(1)}, bf16[256,256]{1,0:T(8,128)(2,1)}, u32[]{:S(2)}) copy-start(bf16[256,256]{1,0:T(8,128)(2,1)} %w_in_ref.3) | copy-start | bytes 393220
  16.5 2.4 %copy-start.5 = (bf16[256,256]{1,0:T(8,128)(2,1)S(1)}, bf16[256,256]{1,0:T(8,128)(2,1)}, u32[]{:S(2)}) copy-start(bf16[256,256]{1,0:T(8,128)(2,1)} %w_back_ref.1) | copy-start | bytes 393220
  16.5 2.4 %copy-start.7 = (bf16[256,128]{1,0:T(8,128)(2,1)S(1)}, bf16[256,128]{1,0:T(8,128)(2,1)}, u32[]{:S(2)}) copy-start(bf16[256,128]{1,0:T(8,128)(2,1)} %w_edge_ref.1) | copy-start | bytes 196612
  16.5 6.6 %copy-start.2 = (bf16[384,384]{1,0:T(8,128)(2,1)S(1)}, bf16[384,384]{1,0:T(8,128)(2,1)}, u32[]{:S(2)}) copy-start(bf16[384,384]{1,0:T(8,128)(2,1)} %w_in_ref.5) | copy-start | bytes 884740
  16.5 8.0 %copy-start.3 = (bf16[384,384]{1,0:T(8,128)(2,1)S(1)}, bf16[384,384]{1,0:T(8,128)(2,1)}, u32[]{:S(2)}) copy-start(bf16[384,384]{1,0:T(8,128)(2,1)} %w_mid_ref.1) | copy-start | bytes 884740
  16.6 7.9 %copy-start.6 = (bf16[384,128]{1,0:T(8,128)(2,1)S(1)}, bf16[384,128]{1,0:T(8,128)(2,1)}, u32[]{:S(2)}) copy-start(bf16[384,128]{1,0:T(8,128)(2,1)} %w_final_ref.1) | copy-start | bytes 294916
  19.6 4.9 %collective-permute-start.9 = (bf16[48,128]{1,0:T(8,128)(2,1)S(1)}, bf16[48,128]{1,0:T(8,128)(2,1)S(1)}, u32[]{:S(2)}, u32[]{:S(2)}) collective-permute-start(bf16[48,128]{1,0:T(8,128)(2,1)S(1)} %get-tuple-element.62.side_ref), channel_id=1, source_target_pairs={{0,12},{1,8},{2,4},{3,0},{5,13},{4,1},{7,9},{6,5},{10,2},{11,6},{8... | collective-permute-start | bytes 36872 | tf_op jit(solution)/shard_map/ppermute | solution.py:655

commit v7 on v6

--- a/solution.py
+++ b/solution.py
@@ -442,7 +442,7 @@
         )
         peak = jnp.max(score, 1, keepdims=True)
         weight = jnp.exp(score - peak)
-        weight = weight / jnp.sum(weight, 1, keepdims=True)
+        weight = weight * (1.0 / jnp.sum(weight, 1, keepdims=True))
         prob_ref[at, :] = weight
         side = jnp.where(col >= 2, weight[:, 128:], weight[:, :128])
         near_ref[0, at, :] = jnp.where(low, pltpu.roll(side, (col % 2) * PAD, 1), 0.0)
@@ -588,7 +588,7 @@
         compiler_params=params(16),
     )(*stay(pair_embed, w_bias.T, *held))
     near, far = [lax.ppermute(bias, "col", [(i, i ^ k) for i in range(4)]) for k in (1, 2)]
-    apart = [(4 * r + c, 4 * (r ^ (2 + c % 2)) + c) for r in range(4) for c in range(4)]
+    apart = [(4 * r + c, 4 * (r ^ (3 - c % 2)) + (c ^ 1)) for r in range(4) for c in range(4)]
     fetched = lax.ppermute(node_embed, ("row", "col"), apart)
     beside = lax.ppermute(node_embed, "row", [(i, i ^ 1) for i in range(4)])
     others = [fetched, lax.ppermute(fetched, "col", [(i, i ^ 1) for i in range(4)]), beside]
@@ -651,7 +651,7 @@
     turned = []
     for c in range(4):
         far = sorted((r for r in range(4) if r != c), key=lambda r: -abs(r - c))
-        turned += [(4 * c + source, 4 * r + c) for r, source in zip(far + [c], (c, c ^ 1, c ^ 2, c ^ 3))]
+        turned += [(4 * c + source, 4 * r + c) for r, source in zip(far + [c], (c ^ 1, c, c ^ 2, c ^ 3))]
     other = lax.ppermute(side, ("row", "col"), turned)
     node_out, lifted = pl.pallas_call(
         lift_kernel,

time: 27.5 us -> 26.2 us (0.953)
  the two profiles are of different devices: /device:TPU:0 before, /device:TPU:3 now
where the time goes in v7:
time: 26.2 us; the launch traced here: 26 us
  Pallas kernels  10.7 us (41%)
  starting transfers between devices  8.31 us (32%)
  waiting for transfers between devices  5.57 us (21%)
  between operations  1.45 us (6%)
    ppermute x1, waiting for transfers between devices, tile_body(): other = lax.ppermute(side, ('row', 'col'), turned)  3.48 us
    ppermute x1, starting transfers between devices, tile_body(): fetched = lax.ppermute(node_embed, ('row', 'col'), apart)  3.38 us
    pallas_call x1, Pallas kernels, tile_body(): pl.pallas_call(edge_kernel, out_shape=jax.ShapeDtypeStruct(pair_embed.sha...  2.79 us
    ppermute x3, starting transfers between devices, tile_body(): lax.ppermute(partial, 'col', [(i, i ^ k) for i in range(4)])  2.21 us
    pallas_call x1, Pallas kernels, tile_body(): pl.pallas_call(bias_kernel, out_shape=[jax.ShapeDtypeStruct((HEADS * rows...  2.17 us
    pallas_call x1, Pallas kernels, tile_body(): pl.pallas_call(score_kernel, out_shape=(jax.ShapeDtypeStruct((rows, CS),...  2.04 us
    pallas_call x1, Pallas kernels, tile_body(): pl.pallas_call(value_kernel, out_shape=jax.ShapeDtypeStruct((rows, CS), f...  1.41 us
    ppermute x1, starting transfers between devices, tile_body(): beside = lax.ppermute(node_embed, 'row', [(i, i ^ 1) for i in range(4)])  1.3 us
  transfers between devices with their start and end apart: 10, of which 3 were waited for; matrix products, arithmetic and copies ran while one was open for 0% of the time, Pallas kernels for 11%

profile of v7, /device:TPU:3, one launch (start us, length us, event | category | flops | bytes accessed | tf_op | source)
XLA Modules:
  0.0 26.0 jit_solution(1560181686839877412)
XLA Ops:
  0.6 0.0 copy-start.8
  0.6 2.2 %shard_map.230 = (f32[192,128]{1,0:T(8,128)S(1)}, f32[1,8]{1,0:T(1,128)S(1)}, f32[1,8]{1,0:T(1,128)S(1)}, f32[3,3,192]{2,1,0:T(4,128)S(1)}, f32[3,192]{1,0:T(4,1...) custom-call(bf16[48,48,128]{2,1,0:T(8,128)(2,1)} %refs_0_.1, ...), custom_call_target="tpu_custom_call" | custom-call | tf_op jit(solution)/shard_map/pallas_call | solution.py:578
  2.8 0.1 collective-permute-start.4
  2.9 0.0 copy-done.8
  2.9 3.4 %collective-permute-start = (bf16[48,256]{1,0:T(8,128)(2,1)S(1)}, bf16[48,256]{1,0:T(8,128)(2,1)S(1)}, u32[]{:S(2)}, u32[]{:S(2)}) collective-permute-start(bf16[48,256]{1,0:T(8,128)(2,1)S(1)} %copy-done.8), channel_id=1, source_target_pairs={{0,13},{1,8},{2,15},{3,10},{4,9},{5,12},{6,11},{7,14},{8,5},{9,0},... | collective-permute-start | bytes 73736 | tf_op jit(solution)/shard_map/ppermute | solution.py:592
  6.3 1.3 %collective-permute-start.2 = (bf16[48,256]{1,0:T(8,128)(2,1)S(1)}, bf16[48,256]{1,0:T(8,128)(2,1)S(1)}, u32[]{:S(2)}, u32[]{:S(2)}) collective-permute-start(bf16[48,256]{1,0:T(8,128)(2,1)S(1)} %copy-done.8), channel_id=1, source_target_pairs={{0,4},{4,0},{8,12},{12,8},{1,5},{5,1},{9,13},{13,9},{2,6},{6,2},{1... | collective-permute-start | bytes 73736 | tf_op jit(solution)/shard_map/ppermute | solution.py:593
  7.6 0.0 collective-permute-start.3
  8.2 0.8 %collective-permute-done.n1_ref = bf16[48,256]{1,0:T(8,128)(2,1)S(1)} collective-permute-done((bf16[48,256]{1,0:T(8,128)(2,1)S(1)}, bf16[48,256]{1,0:T(8,128)(2,1)S(1)}, u32[]{:S(2)}, u32[]{:S(2)}) %collective-permute-start) | collective-permute-done | bytes 24608 | tf_op jit(solution)/shard_map/ppermute | solution.py:592
  9.1 0.0 collective-permute-start.1
  9.1 0.0 collective-permute-done.4.b2_ref
  9.1 0.5 %collective-permute-start.5 = (f32[192,128]{1,0:T(8,128)S(1)}, f32[192,128]{1,0:T(8,128)S(1)}, u32[]{:S(2)}, u32[]{:S(2)}) collective-permute-start(f32[192,128]{1,0:T(8,128)S(1)} %collective-permute-done.4.b2_ref), channel_id=1, source_target_pairs={{0,1},{1,0},{2,3},{3,2},{4,5},{5,4},{6,7},{7,6},{8,9},{9,8},{10,11... | collective-permute-start | bytes 294920 | tf_op jit(solution)/shard_map/ppermute | solution.py:595
  9.6 0.0 copy-start.1
  9.6 0.9 %shard_map.231 = (f32[8,256]{1,0:T(8,128)S(1)}, bf16[48,256]{1,0:T(8,128)(2,1)S(1)}, bf16[384,256]{1,0:T(8,128)(2,1)S(1)}, bf16[2,384,256]{2,1,0:T(8,128)(2,1)S(...) custom-call(s32[1]{0:T(128)S(6)} %copy.25.step_ref, ...), custom_call_target="tpu_custom_call" | custom-call | flops 2000000000 | bytes 8000000 | tf_op jit(solution)/shard_map/pallas_call | solution.py:596
  10.5 0.0 copy-start
  10.5 0.0 collective-permute-done.2.n3_ref
  10.5 0.0 collective-permute-done.1.n2_ref
  10.5 0.0 collective-permute-done.3.b1_ref
  10.5 0.0 collective-permute-done.5.b3_ref
  10.5 2.0 %shard_map.232 = (bf16[48,256]{1,0:T(8,128)(2,1)S(1)}, bf16[256,256]{1,0:T(8,128)(2,1)S(1)}, f32[384,256]{1,0:T(8,128)S(1)}, f32[384,256]{1,0:T(8,128)S(1)}) custom-call(f32[2,8]{1,0:T(2,128)S(1)} %get-tuple-element.47.heads_ref, bf16[48,256]{1,0:T(8,128)(2,1)S(1)} %get-tuple-element.48.own_ref, bf16[48,256]{1,0:T(8,128)(2,1)S(1)} %collective-permute-done.n1_ref, ...), custom_call_target="tpu_custom_call" | custom-call | tf_op jit(solution)/shard_map/pallas_call | solution.py:616
  12.6 0.4 %collective-permute-start.6 = (bf16[48,256]{1,0:T(8,128)(2,1)S(1)}, bf16[48,256]{1,0:T(8,128)(2,1)S(1)}, u32[]{:S(2)}, u32[]{:S(2)}) collective-permute-start(bf16[48,256]{1,0:T(8,128)(2,1)S(1)} %get-tuple-element.57.u0_ref), channel_id=1, source_target_pairs={{0,1},{1,0},{2,3},{3,2},{4,5},{5,4},{6,7},{7,6},{8,9},{9,8},{10,11... | collective-permute-start | bytes 73736 | tf_op jit(solution)/shard_map/ppermute | solution.py:643
  13.0 1.2 %collective-permute-start.7 = (bf16[48,256]{1,0:T(8,128)(2,1)S(1)}, bf16[48,256]{1,0:T(8,128)(2,1)S(1)}, u32[]{:S(2)}, u32[]{:S(2)}) collective-permute-start(bf16[48,256]{1,0:T(8,128)(2,1)S(1)} %get-tuple-element.57.u0_ref), channel_id=1, source_target_pairs={{0,2},{1,3},{2,0},{3,1},{4,6},{5,7},{6,4},{7,5},{8,10},{9,11},{10,... | collective-permute-start | bytes 73736 | tf_op jit(solution)/shard_map/ppermute | solution.py:643
  14.2 0.6 %collective-permute-start.8 = (bf16[48,256]{1,0:T(8,128)(2,1)S(1)}, bf16[48,256]{1,0:T(8,128)(2,1)S(1)}, u32[]{:S(2)}, u32[]{:S(2)}) collective-permute-start(bf16[48,256]{1,0:T(8,128)(2,1)S(1)} %get-tuple-element.57.u0_ref), channel_id=1, source_target_pairs={{0,3},{1,2},{2,1},{3,0},{4,7},{5,6},{6,5},{7,4},{8,11},{9,10},{10,... | collective-permute-start | bytes 73736 | tf_op jit(solution)/shard_map/ppermute | solution.py:643
  14.8 0.0 copy-done.1
  14.8 0.0 copy-done
  14.8 0.0 copy-start.4
  14.8 0.0 copy-start.5
  14.8 0.0 copy-start.7
  14.8 0.0 copy-start.2
  14.8 0.0 copy-start.3
  14.9 0.0 copy-start.6
  14.9 1.4 %shard_map.233.base_ref = f32[48,256]{1,0:T(8,128)S(1)} custom-call(bf16[256,256]{1,0:T(8,128)(2,1)S(1)} %get-tuple-element.58.x_ref, f32[384,256]{1,0:T(8,128)S(1)} %get-tuple-element.59.prob_ref, f32[384,256]{1,0:T(8,128)S(1)} %get-tuple-element.60.vpts_ref, bf16[48,256]{1,0:T(8,128)(2,1)S(1)} %get-tuple-element.48.own_ref, ...), custom_call_target="tpu_custom_call" | custom-call | flops 1000000000 | bytes 4000000 | tf_op jit(solution)/shard_map/pallas_call | solution.py:635
  16.3 0.0 collective-permute-done.6.u1_ref
  16.3 0.0 collective-permute-done.7.u2_ref
  16.3 1.2 %collective-permute-done.8.u3_ref = bf16[48,256]{1,0:T(8,128)(2,1)S(1)} collective-permute-done((bf16[48,256]{1,0:T(8,128)(2,1)S(1)}, bf16[48,256]{1,0:T(8,128)(2,1)S(1)}, u32[]{:S(2)}, u32[]{:S(2)}) %collective-permute-start.8) | collective-permute-done | bytes 24608 | tf_op jit(solution)/shard_map/ppermute | solution.py:643
  17.5 0.0 copy-done.4
  17.5 0.0 copy-done.5
  17.5 0.0 copy-done.7
  17.5 0.7 %shard_map.234 = (bf16[48,256]{1,0:T(8,128)(2,1)S(1)}, bf16[48,128]{1,0:T(8,128)(2,1)S(1)}) custom-call(bf16[48,256]{1,0:T(8,128)(2,1)S(1)} %get-tuple-element.57.u0_ref, bf16[48,256]{1,0:T(8,128)(2,1)S(1)} %collective-permute-done.6.u1_ref, bf16[48,256]{1,0:T(8,128)(2,1)S(1)} %collective-permute-done.7.u2_ref, ...), custom_call_target="tpu_custom_call" | custom-call | tf_op jit(solution)/shard_map/pallas_call | solution.py:644
  18.3 0.8 %collective-permute-start.9 = (bf16[48,128]{1,0:T(8,128)(2,1)S(1)}, bf16[48,128]{1,0:T(8,128)(2,1)S(1)}, u32[]{:S(2)}, u32[]{:S(2)}) collective-permute-start(bf16[48,128]{1,0:T(8,128)(2,1)S(1)} %get-tuple-element.62.side_ref), channel_id=1, source_target_pairs={{1,12},{0,8},{2,4},{3,0},{4,13},{5,1},{7,9},{6,5},{11,2},{10,6},{8... | collective-permute-start | bytes 36872 | tf_op jit(solution)/shard_map/ppermute | solution.py:655
  19.1 0.0 copy-done.2
  19.1 0.6 %shard_map.235 = (bf16[48,256]{1,0:T(8,128)(2,1)}, f32[48,48,384]{2,1,0:T(8,128)S(1)}) custom-call(bf16[48,256]{1,0:T(8,128)(2,1)S(1)} %get-tuple-element.61.node_ref, bf16[48,128]{1,0:T(8,128)(2,1)S(1)} %get-tuple-element.62.side_ref, bf16[48,48,128]{2,1,0:T(8,128)(2,1)S(1)} %get-tuple-element.56.pair_ref, bf16[384,384]{1,0:T(8,128)(2,1)S(1)} %copy-done.2), custom_call_target="tpu_custom_call" | custom-call | flops 226492416 | bytes 4000000 | tf_op jit(solution)/shard_map/pallas_call | solution.py:656
  19.8 3.5 %collective-permute-done.9.other_ref = bf16[48,128]{1,0:T(8,128)(2,1)S(1)} collective-permute-done((bf16[48,128]{1,0:T(8,128)(2,1)S(1)}, bf16[48,128]{1,0:T(8,128)(2,1)S(1)}, u32[]{:S(2)}, u32[]{:S(2)}) %collective-permute-start.9) | collective-permute-done | bytes 12320 | tf_op jit(solution)/shard_map/ppermute | solution.py:655
  23.2 0.0 copy-done.3
  23.2 0.0 copy-done.6
  23.2 2.8 %shard_map.236 = bf16[48,48,128]{2,1,0:T(8,128)(2,1)} custom-call(f32[48,48,384]{2,1,0:T(8,128)S(1)} %get-tuple-element.64.lifted_ref, bf16[48,128]{1,0:T(8,128)(2,1)S(1)} %get-tuple-element.62.side_ref, bf16[48,128]{1,0:T(8,128)(2,1)S(1)} %collective-permute-done.9.other_ref, f32[48,16]{1,0:T(8,128)S(1)} %get-tuple-element.54.rows_ref, ...), custom_call_target="tpu_custom_call" | custom-call | tf_op jit(solution)/shard_map/pallas_call | solution.py:668
Async XLA Ops:
  0.6 2.3 %copy-start.8 = (bf16[48,256]{1,0:T(8,128)(2,1)S(1)}, bf16[48,256]{1,0:T(8,128)(2,1)}, u32[]{:S(2)}) copy-start(bf16[48,256]{1,0:T(8,128)(2,1)} %refs_8_.1) | copy-start | bytes 73732
  2.8 6.3 %collective-permute-start.4 = (f32[192,128]{1,0:T(8,128)S(1)}, f32[192,128]{1,0:T(8,128)S(1)}, u32[]{:S(2)}, u32[]{:S(2)}) collective-permute-start(f32[192,128]{1,0:T(8,128)S(1)} %get-tuple-element.55.b0_ref), channel_id=1, source_target_pairs={{0,2},{1,3},{2,0},{3,1},{4,6},{5,7},{6,4},{7,5},{8,10},{9,11},{10,... | collective-permute-start | bytes 294920 | tf_op jit(solution)/shard_map/ppermute | solution.py:590
  2.9 6.2 %collective-permute-start = (bf16[48,256]{1,0:T(8,128)(2,1)S(1)}, bf16[48,256]{1,0:T(8,128)(2,1)S(1)}, u32[]{:S(2)}, u32[]{:S(2)}) collective-permute-start(bf16[48,256]{1,0:T(8,128)(2,1)S(1)} %copy-done.8), channel_id=1, source_target_pairs={{0,13},{1,8},{2,15},{3,10},{4,9},{5,12},{6,11},{7,14},{8,5},{9,0},... | collective-permute-start | bytes 73736 | tf_op jit(solution)/shard_map/ppermute | solution.py:592
  6.3 4.2 %collective-permute-start.2 = (bf16[48,256]{1,0:T(8,128)(2,1)S(1)}, bf16[48,256]{1,0:T(8,128)(2,1)S(1)}, u32[]{:S(2)}, u32[]{:S(2)}) collective-permute-start(bf16[48,256]{1,0:T(8,128)(2,1)S(1)} %copy-done.8), channel_id=1, source_target_pairs={{0,4},{4,0},{8,12},{12,8},{1,5},{5,1},{9,13},{13,9},{2,6},{6,2},{1... | collective-permute-start | bytes 73736 | tf_op jit(solution)/shard_map/ppermute | solution.py:593
  7.6 2.9 %collective-permute-start.3 = (f32[192,128]{1,0:T(8,128)S(1)}, f32[192,128]{1,0:T(8,128)S(1)}, u32[]{:S(2)}, u32[]{:S(2)}) collective-permute-start(f32[192,128]{1,0:T(8,128)S(1)} %get-tuple-element.55.b0_ref), channel_id=1, source_target_pairs={{0,1},{1,0},{2,3},{3,2},{4,5},{5,4},{6,7},{7,6},{8,9},{9,8},{10,11... | collective-permute-start | bytes 294920 | tf_op jit(solution)/shard_map/ppermute | solution.py:590
  9.1 1.4 %collective-permute-start.1 = (bf16[48,256]{1,0:T(8,128)(2,1)S(1)}, bf16[48,256]{1,0:T(8,128)(2,1)S(1)}, u32[]{:S(2)}, u32[]{:S(2)}) collective-permute-start(bf16[48,256]{1,0:T(8,128)(2,1)S(1)} %collective-permute-done.n1_ref), channel_id=1, source_target_pairs={{0,1},{1,0},{2,3},{3,2},{4,5},{5,4},{6,7},{7,6},{8,9},{9,8},{10,11... | collective-permute-start | bytes 73736 | tf_op jit(solution)/shard_map/ppermute | solution.py:594
  9.1 1.5 %collective-permute-start.5 = (f32[192,128]{1,0:T(8,128)S(1)}, f32[192,128]{1,0:T(8,128)S(1)}, u32[]{:S(2)}, u32[]{:S(2)}) collective-permute-start(f32[192,128]{1,0:T(8,128)S(1)} %collective-permute-done.4.b2_ref), channel_id=1, source_target_pairs={{0,1},{1,0},{2,3},{3,2},{4,5},{5,4},{6,7},{7,6},{8,9},{9,8},{10,11... | collective-permute-start | bytes 294920 | tf_op jit(solution)/shard_map/ppermute | solution.py:595
  9.6 5.2 %copy-start.1 = (bf16[3456,256]{1,0:T(8,128)(2,1)S(1)}, bf16[3456,256]{1,0:T(8,128)(2,1)}, u32[]{:S(2)}) copy-start(bf16[3456,256]{1,0:T(8,128)(2,1)} %w_out_ref.3) | copy-start | bytes 5308420
  10.5 4.3 %copy-start = (bf16[256,4096]{1,0:T(8,128)(2,1)S(1)}, bf16[256,4096]{1,0:T(8,128)(2,1)}, u32[]{:S(2)}) copy-start(bf16[256,4096]{1,0:T(8,128)(2,1)} %w_kv_ref.1) | copy-start | bytes 6291460
  12.6 3.7 %collective-permute-start.6 = (bf16[48,256]{1,0:T(8,128)(2,1)S(1)}, bf16[48,256]{1,0:T(8,128)(2,1)S(1)}, u32[]{:S(2)}, u32[]{:S(2)}) collective-permute-start(bf16[48,256]{1,0:T(8,128)(2,1)S(1)} %get-tuple-element.57.u0_ref), channel_id=1, source_target_pairs={{0,1},{1,0},{2,3},{3,2},{4,5},{5,4},{6,7},{7,6},{8,9},{9,8},{10,11... | collective-permute-start | bytes 73736 | tf_op jit(solution)/shard_map/ppermute | solution.py:643
  13.0 3.3 %collective-permute-start.7 = (bf16[48,256]{1,0:T(8,128)(2,1)S(1)}, bf16[48,256]{1,0:T(8,128)(2,1)S(1)}, u32[]{:S(2)}, u32[]{:S(2)}) collective-permute-start(bf16[48,256]{1,0:T(8,128)(2,1)S(1)} %get-tuple-element.57.u0_ref), channel_id=1, source_target_pairs={{0,2},{1,3},{2,0},{3,1},{4,6},{5,7},{6,4},{7,5},{8,10},{9,11},{10,... | collective-permute-start | bytes 73736 | tf_op jit(solution)/shard_map/ppermute | solution.py:643
  14.2 3.3 %collective-permute-start.8 = (bf16[48,256]{1,0:T(8,128)(2,1)S(1)}, bf16[48,256]{1,0:T(8,128)(2,1)S(1)}, u32[]{:S(2)}, u32[]{:S(2)}) collective-permute-start(bf16[48,256]{1,0:T(8,128)(2,1)S(1)} %get-tuple-element.57.u0_ref), channel_id=1, source_target_pairs={{0,3},{1,2},{2,1},{3,0},{4,7},{5,6},{6,5},{7,4},{8,11},{9,10},{10,... | collective-permute-start | bytes 73736 | tf_op jit(solution)/shard_map/ppermute | solution.py:643
  14.8 2.7 %copy-start.4 = (bf16[256,256]{1,0:T(8,128)(2,1)S(1)}, bf16[256,256]{1,0:T(8,128)(2,1)}, u32[]{:S(2)}) copy-start(bf16[256,256]{1,0:T(8,128)(2,1)} %w_in_ref.3) | copy-start | bytes 393220
  14.8 2.7 %copy-start.5 = (bf16[256,256]{1,0:T(8,128)(2,1)S(1)}, bf16[256,256]{1,0:T(8,128)(2,1)}, u32[]{:S(2)}) copy-start(bf16[256,256]{1,0:T(8,128)(2,1)} %w_back_ref.1) | copy-start | bytes 393220
  14.8 2.7 %copy-start.7 = (bf16[256,128]{1,0:T(8,128)(2,1)S(1)}, bf16[256,128]{1,0:T(8,128)(2,1)}, u32[]{:S(2)}) copy-start(bf16[256,128]{1,0:T(8,128)(2,1)} %w_edge_ref.1) | copy-start | bytes 196612
  14.8 4.3 %copy-start.2 = (bf16[384,384]{1,0:T(8,128)(2,1)S(1)}, bf16[384,384]{1,0:T(8,128)(2,1)}, u32[]{:S(2)}) copy-start(bf16[384,384]{1,0:T(8,128)(2,1)} %w_in_ref.5) | copy-start | bytes 884740
  14.8 8.4 %copy-start.3 = (bf16[384,384]{1,0:T(8,128)(2,1)S(1)}, bf16[384,384]{1,0:T(8,128)(2,1)}, u32[]{:S(2)}) copy-start(bf16[384,384]{1,0:T(8,128)(2,1)} %w_mid_ref.1) | copy-start | bytes 884740
  14.9 8.4 %copy-start.6 = (bf16[384,128]{1,0:T(8,128)(2,1)S(1)}, bf16[384,128]{1,0:T(8,128)(2,1)}, u32[]{:S(2)}) copy-start(bf16[384,128]{1,0:T(8,128)(2,1)} %w_final_ref.1) | copy-start | bytes 294916
  18.3 5.0 %collective-permute-start.9 = (bf16[48,128]{1,0:T(8,128)(2,1)S(1)}, bf16[48,128]{1,0:T(8,128)(2,1)S(1)}, u32[]{:S(2)}, u32[]{:S(2)}) collective-permute-start(bf16[48,128]{1,0:T(8,128)(2,1)S(1)} %get-tuple-element.62.side_ref), channel_id=1, source_target_pairs={{1,12},{0,8},{2,4},{3,0},{4,13},{5,1},{7,9},{6,5},{11,2},{10,6},{8... | collective-permute-start | bytes 36872 | tf_op jit(solution)/shard_map/ppermute | solution.py:655
